TPU v7x, 32 devices: a whole 2x2x4 slice. The times are simulated.
32 devices in a mesh: expert: 8 (over z, core), shard: 4 (over y, x).
Axes of the slice: x: 2, y: 2, z: 4, core: 2. Of those that a mesh axis runs over, the one named last changes fastest.
Arguments:
- tokens: bfloat16 [25216, 768], P(('expert', 'shard')), may hold values from -6 to 6
- routes: int32 [25216, 2], P(('expert', 'shard')), may hold values from 0 to 15, all different within a row; in each aligned block of 788 rows (0 to 787, 788 to 1575, ...) at most 152 rows name the same one
- cotangent: bfloat16 [25216, 768], P(('expert', 'shard')), may hold values from -6 to 6
- gain_attn: bfloat16 [768], P('shard'), may hold values from 0.5 to 1.5
- w_qkv: bfloat16 [768, 2304], P('shard'), may hold values from -0.21875 to 0.21875
- w_proj: bfloat16 [768, 768], P('shard'), may hold values from -0.875 to 0.875
- gain_moe: bfloat16 [768], P('shard'), may hold values from 0.5 to 1.5
- w_router: bfloat16 [768, 16], P('shard'), may hold values from -0.4375 to 0.4375
- w_in: bfloat16 [16, 768, 3072], P('expert', None, 'shard'), may hold values from -0.21875 to 0.21875
- w_out: bfloat16 [16, 3072, 768], P('expert', 'shard'), may hold values from -0.15625 to 0.15625
- v_attn: float32 [768], P('shard'), may hold values from 4300.8 to 17203.2
- v_moe: float32 [768], P('shard'), may hold values from 26476.8 to 105907.2
- row_qkv: float32 [768], P('shard'), may hold values from 1433.6 to 5734.4
- col_qkv: float32 [2304], replicated, may hold values from 1433.6 to 5734.4
- row_proj: float32 [768], P('shard'), may hold values from 358.4 to 1433.6
- col_proj: float32 [768], replicated, may hold values from 358.4 to 1433.6
- row_router: float32 [768], P('shard'), may hold values from 211814.4 to 847257.6
- col_router: float32 [16], replicated, may hold values from 211814.4 to 847257.6
- row_in: float32 [16, 768], P('expert'), may hold values from 96.6 to 386.4
- col_in: float32 [16, 3072], P('expert', 'shard'), may hold values from 96.6 to 386.4
- row_out: float32 [16, 3072], P('expert', 'shard'), may hold values from 198.8 to 795.2
- col_out: float32 [16, 768], P('expert'), may hold values from 198.8 to 795.2
Outputs:
- block_out: bfloat16 [25216, 768], P(('expert', 'shard'))
- grad_tokens: float32 [25216, 768], P(('expert', 'shard'))
- dense_rms: float32 [5], replicated
- expert_rms: float32 [16, 2], P('expert')
- grad_gain_attn: float32 [768], P('shard')
- new_gain_attn: float32 [768], P('shard')
- v_attn_new: float32 [768], P('shard')
- grad_gain_moe: float32 [768], P('shard')
- new_gain_moe: float32 [768], P('shard')
- v_moe_new: float32 [768], P('shard')
- grad_w_qkv: float32 [768, 2304], P('shard')
- new_w_qkv: float32 [768, 2304], P('shard')
- row_qkv_new: float32 [768], P('shard')
- col_qkv_new: float32 [2304], replicated
- grad_w_proj: float32 [768, 768], P('shard')
- new_w_proj: float32 [768, 768], P('shard')
- row_proj_new: float32 [768], P('shard')
- col_proj_new: float32 [768], replicated
- grad_w_router: float32 [768, 16], P('shard')
- new_w_router: float32 [768, 16], P('shard')
- row_router_new: float32 [768], P('shard')
- col_router_new: float32 [16], replicated
- grad_w_in: float32 [16, 768, 3072], P('expert', None, 'shard')
- new_w_in: float32 [16, 768, 3072], P('expert', None, 'shard')
- row_in_new: float32 [16, 768], P('expert')
- col_in_new: float32 [16, 3072], P('expert', 'shard')
- grad_w_out: float32 [16, 3072, 768], P('expert', 'shard')
- new_w_out: float32 [16, 3072, 768], P('expert', 'shard')
- row_out_new: float32 [16, 3072], P('expert', 'shard')
- col_out_new: float32 [16, 768], P('expert')
Inputs may be any that keep to these rules, and one draw needn't show every extreme that they name: `routes`: each row names two different experts; within each aligned block of 788 rows (the rows of one device) no expert is named by more than 152 rows.
All inputs are finite; a program needn't handle non-finite values.
Results may differ from a plain program's by a relative error of at most 0.015.
Values may be sent and summed in bfloat16 or wider, within the bound.
A program may use at most 256 MiB of HBM per device.

v0:
```python
import jax
import jax.numpy as jnp
from jax import lax
from jax.sharding import PartitionSpec as P

D = 768
HEADS = 12
HEAD = 64
FF = 3072
SEQ = 197


PRECISE = lax.Precision.HIGHEST
EPS_NORM = 1e-06
EPS_SQUARE = 1e-30
RATE = 0.3
DECAY = 0.5
CLIP = 0.05


def normalize(values):
    center = values - jnp.mean(values, axis=-1, keepdims=True)
    inv_root = lax.rsqrt(jnp.mean(center * center, axis=-1, keepdims=True) + EPS_NORM)
    return (center * inv_root, inv_root)


def norm_back(grad, normed, inv_root, gain):
    scaled = grad * gain
    grad_in = inv_root * (
        scaled
        - jnp.mean(scaled, axis=-1, keepdims=True)
        - normed * jnp.mean(scaled * normed, axis=-1, keepdims=True)
    )
    return (grad_in, jnp.sum(grad * normed, axis=0))


def gelu_tanh(values):
    return jax.nn.gelu(values, approximate=True)


def local(
    tokens,
    routes,
    cotangent,
    gain_attn,
    w_qkv,
    w_proj,
    gain_moe,
    w_router,
    w_in,
    w_out,
    v_attn,
    v_moe,
    row_qkv,
    col_qkv,
    row_proj,
    col_proj,
    row_router,
    col_router,
    row_in,
    col_in,
    row_out,
    col_out,
):
    gain_first, qkv_full, proj_full, gain_second, router_full = (
        lax.all_gather(gain_attn, "shard", axis=0, tiled=True),
        lax.all_gather(w_qkv, "shard", axis=0, tiled=True),
        lax.all_gather(w_proj, "shard", axis=0, tiled=True),
        lax.all_gather(gain_moe, "shard", axis=0, tiled=True),
        lax.all_gather(w_router, "shard", axis=0, tiled=True),
    )
    first_full, second_full = (
        lax.all_gather(w_in, "shard", axis=2, tiled=True),
        lax.all_gather(w_out, "shard", axis=1, tiled=True),
    )
    row_count = tokens.shape[0]
    image_count = row_count // SEQ
    expert_count = router_full.shape[1]
    per_device = w_in.shape[0]
    axis_count = lax.axis_size("expert")
    capacity = ((3 * row_count + expert_count - 1) // expert_count + 7) // 8 * 8
    score_scale = HEAD ** (-0.5)
    tok_float = tokens.astype(jnp.float32)
    gain_one = gain_first.astype(jnp.float32)
    gain_two = gain_second.astype(jnp.float32)
    attn_hat, attn_inv = normalize(tok_float)
    attn_low = (attn_hat * gain_one).astype(jnp.bfloat16)
    qkv_low = jnp.dot(attn_low, qkv_full, preferred_element_type=jnp.float32).astype(jnp.bfloat16)
    qkv_split = qkv_low.reshape(image_count, SEQ, 3, HEADS, HEAD)
    query_part = qkv_split[:, :, 0]
    key_part = qkv_split[:, :, 1]
    value_part = qkv_split[:, :, 2]
    scores = (
        jnp.einsum("ishd,ithd->ihst", query_part, key_part, preferred_element_type=jnp.float32)
        * score_scale
    )
    log_total = jax.nn.logsumexp(scores, axis=-1, keepdims=True)
    soft_low = jnp.exp(scores - log_total).astype(jnp.bfloat16)
    attended = (
        jnp.einsum("ihst,ithd->ishd", soft_low, value_part, preferred_element_type=jnp.float32)
        .reshape(row_count, D)
        .astype(jnp.bfloat16)
    )
    hidden = tok_float + jnp.dot(attended, proj_full, preferred_element_type=jnp.float32)
    moe_hat, moe_inv = normalize(hidden)
    moe_low = (moe_hat * gain_two).astype(jnp.bfloat16)
    logits = jnp.dot(moe_low, router_full, preferred_element_type=jnp.float32)
    labels = jnp.arange(expert_count, dtype=jnp.int32)
    route_hits = (routes[:, :, None] == labels[None, None, :]).astype(jnp.float32)
    chosen = jnp.sum(route_hits * logits[:, None, :], axis=2)
    gates = jax.nn.softmax(chosen, axis=-1)
    flat_routes = routes.reshape(-1)
    one_hot = (flat_routes[:, None] == labels[None, :]).astype(jnp.int32)
    slot_rank = jnp.sum((jnp.cumsum(one_hot, axis=0) - 1) * one_hot, axis=1)
    slot_dest = flat_routes * capacity + slot_rank
    pair_index = jnp.arange(2 * row_count, dtype=jnp.int32)
    slot_pair = (
        jnp.full((expert_count * capacity,), 2 * row_count, jnp.int32).at[slot_dest].set(pair_index)
    )
    slot_token = slot_pair // 2
    zero_row = jnp.zeros((1, D), jnp.bfloat16)
    send_rows = jnp.concatenate([moe_low, zero_row], axis=0)[slot_token].reshape(
        axis_count, per_device, capacity, D
    )
    received = lax.all_to_all(send_rows, "expert", split_axis=0, concat_axis=0, tiled=True)
    pre_gelu = jnp.einsum(
        "sekd,edf->sekf", received, first_full, preferred_element_type=jnp.float32
    )
    activated = gelu_tanh(pre_gelu).astype(jnp.bfloat16)
    expert_out = jnp.einsum(
        "sekf,efd->sekd", activated, second_full, preferred_element_type=jnp.float32
    ).astype(jnp.bfloat16)
    back_rows = lax.all_to_all(expert_out, "expert", split_axis=0, concat_axis=0, tiled=True)
    back_rows, received, pre_gelu, activated = (back_rows, received, pre_gelu, activated)
    picked = (
        back_rows.reshape(expert_count * capacity, D)[slot_dest]
        .reshape(row_count, 2, D)
        .astype(jnp.float32)
    )
    block_out = (hidden + jnp.sum(gates[:, :, None] * picked, axis=1)).astype(jnp.bfloat16)
    grad_out = cotangent.astype(jnp.float32)
    grad_picked = (gates[:, :, None] * grad_out[:, None, :]).astype(jnp.bfloat16)
    grad_gates = jnp.sum(grad_out[:, None, :] * picked, axis=2)
    grad_chosen = gates * (grad_gates - jnp.sum(gates * grad_gates, axis=1, keepdims=True))
    grad_logits = jnp.sum(route_hits * grad_chosen[:, :, None], axis=1)
    grad_send = jnp.concatenate([grad_picked.reshape(2 * row_count, D), zero_row], axis=0)[
        slot_pair
    ].reshape(axis_count, per_device, capacity, D)
    grad_recv = lax.all_to_all(grad_send, "expert", split_axis=0, concat_axis=0, tiled=True)
    grad_act = jnp.einsum(
        "sekd,efd->sekf", grad_recv, second_full, preferred_element_type=jnp.float32
    )
    unused, gelu_pull = jax.vjp(gelu_tanh, pre_gelu)
    grad_pre = gelu_pull(grad_act)[0].astype(jnp.bfloat16)
    grad_rows = jnp.einsum(
        "sekf,edf->sekd", grad_pre, first_full, preferred_element_type=jnp.float32
    ).astype(jnp.bfloat16)
    grad_back = lax.all_to_all(grad_rows, "expert", split_axis=0, concat_axis=0, tiled=True)
    grad_first = jnp.einsum(
        "sekd,sekf->edf", received, grad_pre, preferred_element_type=jnp.float32
    )
    grad_second = jnp.einsum(
        "sekf,sekd->efd", activated, grad_recv, preferred_element_type=jnp.float32
    )
    grad_first, grad_second = (
        lax.psum_scatter(grad_first, "shard", scatter_dimension=2, tiled=True),
        lax.psum_scatter(grad_second, "shard", scatter_dimension=1, tiled=True),
    )
    returned = (
        grad_back.reshape(expert_count * capacity, D)[slot_dest]
        .reshape(row_count, 2, D)
        .astype(jnp.float32)
    )
    router_float = router_full.astype(jnp.float32)
    grad_moe = jnp.sum(returned, axis=1) + jnp.einsum(
        "te,de->td", grad_logits, router_float, precision=PRECISE
    )
    grad_router = jnp.einsum(
        "td,te->de", moe_low.astype(jnp.float32), grad_logits, precision=PRECISE
    )
    grad_from_moe, grad_g2 = norm_back(grad_moe, moe_hat, moe_inv, gain_two)
    grad_hidden = grad_out + grad_from_moe
    grad_low = grad_hidden.astype(jnp.bfloat16)
    grad_proj = jnp.einsum("tc,td->cd", attended, grad_low, preferred_element_type=jnp.float32)
    grad_att = (
        jnp.einsum("td,cd->tc", grad_low, proj_full, preferred_element_type=jnp.float32)
        .astype(jnp.bfloat16)
        .reshape(image_count, SEQ, HEADS, HEAD)
    )
    scores_again = (
        jnp.einsum("ishd,ithd->ihst", query_part, key_part, preferred_element_type=jnp.float32)
        * score_scale
    )
    soft_again = jnp.exp(scores_again - log_total)
    soft_again_low = soft_again.astype(jnp.bfloat16)
    grad_soft = jnp.einsum(
        "ishd,ithd->ihst", grad_att, value_part, preferred_element_type=jnp.float32
    )
    grad_value = jnp.einsum(
        "ihst,ishd->ithd", soft_again_low, grad_att, preferred_element_type=jnp.float32
    )
    row_delta = jnp.sum(soft_again * grad_soft, axis=-1, keepdims=True)
    grad_scores = (soft_again * (grad_soft - row_delta)).astype(jnp.bfloat16)
    grad_query = (
        jnp.einsum("ihst,ithd->ishd", grad_scores, key_part, preferred_element_type=jnp.float32)
        * score_scale
    )
    grad_key = (
        jnp.einsum("ihst,ishd->ithd", grad_scores, query_part, preferred_element_type=jnp.float32)
        * score_scale
    )
    grad_qkv_low = (
        jnp.stack([grad_query, grad_key, grad_value], axis=2)
        .reshape(row_count, 3 * D)
        .astype(jnp.bfloat16)
    )
    grad_qkv = jnp.einsum("tc,td->cd", attn_low, grad_qkv_low, preferred_element_type=jnp.float32)
    grad_attn_in = jnp.einsum(
        "td,cd->tc", grad_qkv_low, qkv_full, preferred_element_type=jnp.float32
    )
    grad_from_attn, grad_g1 = norm_back(grad_attn_in, attn_hat, attn_inv, gain_one)
    grad_tokens = grad_hidden + grad_from_attn
    dense_grads = (grad_g1, grad_qkv, grad_proj, grad_g2, grad_router)
    dense_total = lax.psum(
        (dense_grads[0], dense_grads[1], dense_grads[2], dense_grads[3], dense_grads[4]), "expert"
    )
    dense_parts = (
        lax.psum_scatter(dense_total[0], "shard", scatter_dimension=0, tiled=True),
        lax.psum_scatter(dense_total[1], "shard", scatter_dimension=0, tiled=True),
        lax.psum_scatter(dense_total[2], "shard", scatter_dimension=0, tiled=True),
        lax.psum_scatter(dense_total[3], "shard", scatter_dimension=0, tiled=True),
        lax.psum_scatter(dense_total[4], "shard", scatter_dimension=0, tiled=True),
    )
    part_g1, part_qkv, part_proj, part_g2, part_router = dense_parts
    weight_g1 = gain_attn.astype(jnp.float32)
    weight_g2 = gain_moe.astype(jnp.float32)
    weight_qkv = w_qkv.astype(jnp.float32)
    weight_proj = w_proj.astype(jnp.float32)
    weight_router = w_router.astype(jnp.float32)
    weight_first = w_in.astype(jnp.float32)
    weight_second = w_out.astype(jnp.float32)
    v_attn_new = DECAY * v_attn + (1.0 - DECAY) * (part_g1 * part_g1 + EPS_SQUARE)
    v_moe_new = DECAY * v_moe + (1.0 - DECAY) * (part_g2 * part_g2 + EPS_SQUARE)
    square_qkv = part_qkv * part_qkv + EPS_SQUARE
    square_proj = part_proj * part_proj + EPS_SQUARE
    square_router = part_router * part_router + EPS_SQUARE
    row_qkv_new = DECAY * row_qkv + (1.0 - DECAY) * jnp.mean(square_qkv, axis=1)
    row_proj_new = DECAY * row_proj + (1.0 - DECAY) * jnp.mean(square_proj, axis=1)
    row_router_new = DECAY * row_router + (1.0 - DECAY) * jnp.mean(square_router, axis=1)
    square_first = grad_first * grad_first + EPS_SQUARE
    square_second = grad_second * grad_second + EPS_SQUARE
    col_in_new = DECAY * col_in + (1.0 - DECAY) * jnp.mean(square_first, axis=1)
    row_out_new = DECAY * row_out + (1.0 - DECAY) * jnp.mean(square_second, axis=2)
    dense_local_sums = jnp.stack(
        [
            jnp.sum(row_qkv_new),
            jnp.sum(row_proj_new),
            jnp.sum(row_router_new),
            jnp.sum(weight_g1 * weight_g1),
            jnp.sum(weight_g2 * weight_g2),
            jnp.sum(weight_qkv * weight_qkv),
            jnp.sum(weight_proj * weight_proj),
            jnp.sum(weight_router * weight_router),
        ]
    )
    expert_local_sums = jnp.stack(
        [
            jnp.sum(weight_first * weight_first, axis=(1, 2)),
            jnp.sum(row_out_new, axis=1),
            jnp.sum(weight_second * weight_second, axis=(1, 2)),
        ],
        axis=1,
    )
    col_qkv_sum, col_proj_sum, col_router_sum, dense_sums, row_in_sum, col_out_sum, expert_sums = (
        lax.psum(
            (
                jnp.sum(square_qkv, axis=0),
                jnp.sum(square_proj, axis=0),
                jnp.sum(square_router, axis=0),
                dense_local_sums,
                jnp.sum(square_first, axis=2),
                jnp.sum(square_second, axis=1),
                expert_local_sums,
            ),
            "shard",
        )
    )
    col_qkv_new = DECAY * col_qkv + (1.0 - DECAY) * (col_qkv_sum / D)
    col_proj_new = DECAY * col_proj + (1.0 - DECAY) * (col_proj_sum / D)
    col_router_new = DECAY * col_router + (1.0 - DECAY) * (col_router_sum / D)
    row_in_new = DECAY * row_in + (1.0 - DECAY) * (row_in_sum / FF)
    col_out_new = DECAY * col_out + (1.0 - DECAY) * (col_out_sum / FF)
    raw_g1 = part_g1 * lax.rsqrt(v_attn_new)
    raw_g2 = part_g2 * lax.rsqrt(v_moe_new)
    raw_qkv = part_qkv * lax.rsqrt(
        row_qkv_new[:, None] * col_qkv_new[None, :] / (dense_sums[0] / D)
    )
    raw_proj = part_proj * lax.rsqrt(
        row_proj_new[:, None] * col_proj_new[None, :] / (dense_sums[1] / D)
    )
    raw_router = part_router * lax.rsqrt(
        row_router_new[:, None] * col_router_new[None, :] / (dense_sums[2] / D)
    )
    raw_first = grad_first * lax.rsqrt(
        row_in_new[:, :, None]
        * col_in_new[:, None, :]
        / jnp.mean(row_in_new, axis=1)[:, None, None]
    )
    raw_second = grad_second * lax.rsqrt(
        row_out_new[:, :, None] * col_out_new[:, None, :] / (expert_sums[:, 1] / FF)[:, None, None]
    )
    dense_square, expert_square = lax.psum(
        (
            jnp.stack(
                [
                    jnp.sum(raw_g1 * raw_g1),
                    jnp.sum(raw_g2 * raw_g2),
                    jnp.sum(raw_qkv * raw_qkv),
                    jnp.sum(raw_proj * raw_proj),
                    jnp.sum(raw_router * raw_router),
                ]
            ),
            jnp.stack(
                [
                    jnp.sum(raw_first * raw_first, axis=(1, 2)),
                    jnp.sum(raw_second * raw_second, axis=(1, 2)),
                ],
                axis=1,
            ),
        ),
        "shard",
    )
    dense_sizes = jnp.array([D, D, 3 * D * D, D * D, D * expert_count], jnp.float32)
    dense_rms = jnp.sqrt(dense_square / dense_sizes)
    expert_rms = jnp.sqrt(expert_square / float(D * FF))
    dense_weight_rms = jnp.sqrt(dense_sums[3:] / dense_sizes)
    dense_factor = -RATE * dense_weight_rms / jnp.maximum(CLIP, dense_rms)
    expert_weight_rms = jnp.sqrt(
        jnp.stack([expert_sums[:, 0], expert_sums[:, 2]], axis=1) / float(D * FF)
    )
    expert_factor = -RATE * expert_weight_rms / jnp.maximum(CLIP, expert_rms)
    new_g1 = weight_g1 + dense_factor[0] * raw_g1
    new_g2 = weight_g2 + dense_factor[1] * raw_g2
    new_qkv = weight_qkv + dense_factor[2] * raw_qkv
    new_proj = weight_proj + dense_factor[3] * raw_proj
    new_router = weight_router + dense_factor[4] * raw_router
    new_first = weight_first + expert_factor[:, 0][:, None, None] * raw_first
    new_second = weight_second + expert_factor[:, 1][:, None, None] * raw_second
    return (
        block_out,
        grad_tokens,
        dense_rms,
        expert_rms,
        part_g1,
        new_g1,
        v_attn_new,
        part_g2,
        new_g2,
        v_moe_new,
        part_qkv,
        new_qkv,
        row_qkv_new,
        col_qkv_new,
        part_proj,
        new_proj,
        row_proj_new,
        col_proj_new,
        part_router,
        new_router,
        row_router_new,
        col_router_new,
        grad_first,
        new_first,
        row_in_new,
        col_in_new,
        grad_second,
        new_second,
        row_out_new,
        col_out_new,
    )


def solution(mesh):
    return jax.shard_map(
        local,
        mesh=mesh,
        in_specs=(
            P(("expert", "shard"), None),
            P(("expert", "shard"), None),
            P(("expert", "shard"), None),
            P("shard"),
            P("shard", None),
            P("shard", None),
            P("shard"),
            P("shard", None),
            P("expert", None, "shard"),
            P("expert", "shard", None),
            P("shard"),
            P("shard"),
            P("shard"),
            P(),
            P("shard"),
            P(),
            P("shard"),
            P(),
            P("expert", None),
            P("expert", "shard"),
            P("expert", "shard"),
            P("expert", None),
        ),
        out_specs=(
            P(("expert", "shard"), None),
            P(("expert", "shard"), None),
            P(),
            P("expert", None),
            P("shard"),
            P("shard"),
            P("shard"),
            P("shard"),
            P("shard"),
            P("shard"),
            P("shard", None),
            P("shard", None),
            P("shard"),
            P(),
            P("shard", None),
            P("shard", None),
            P("shard"),
            P(),
            P("shard", None),
            P("shard", None),
            P("shard"),
            P(),
            P("expert", None, "shard"),
            P("expert", None, "shard"),
            P("expert", None),
            P("expert", "shard"),
            P("expert", "shard", None),
            P("expert", "shard", None),
            P("expert", "shard"),
            P("expert", None),
        ),
        check_vma=False,
    )
```

profile of v0, /device:TPU:0, one launch (start us, length us, event | category | flops | bytes accessed | tf_op | source)
XLA Modules:
  0.0 1194.5 jit_solution(15474978556528469575)
XLA Ops:
  12.0 11.3 all-reduce.12
  31.0 9.0 scatter_custom_fusion
  40.0 19.9 %all-gather.6.cloned.1.call-done = bf16[768,2304]{1,0:T(8,128)(2,1)} async-done(((bf16[192,2304]{1,0:T(8,128)(2,1)}), bf16[768,2304]{1,0:T(8,128)(2,1)}) %all-gather.6.cloned.1.call-update) | async-done | bytes 3538960 | tf_op jit(solution)/shard_map/all_gather | solution.py:67
  66.7 12.0 %reshape.398 = bf16[4,197,3,12,64]{4,3,2,1,0:T(8,128)(2,1)} reshape(bf16[788,2304]{1,0:T(8,128)(2,1)} %convolution_convert_fusion) | data formatting | bytes 7262208 | tf_op jit(solution)/shard_map/reshape | solution.py:89
  117.1 8.4 gather_fusion
  130.7 8.2 all-gather
  155.2 8.4 gather_fusion.2
  163.7 51.3 %all-to-all-done = bf16[8,2,152,768]{3,2,1,0:T(8,128)(2,1)} async-done(((bf16[8,2,152,768]{3,2,1,0:T(8,128)(2,1)}), bf16[8,2,152,768]{3,2,1,0:T(8,128)(2,1)}, u32[]{:S(2)}, u32[]{:S(2)}) %all-to-all-start) | async-done | bytes 3735584 | tf_op jit(solution)/shard_map/all_to_all | solution.py:125
  219.9 21.7 %fusion.15 = f32[2,8,152,3072]{3,2,1,0:T(8,128)} fusion(bf16[2,768,3072]{2,1,0:T(8,128)(2,1)} %all-gather.10.cloned.1.call-done, bf16[8,2,152,768]{3,2,1,0:T(8,128)(2,1)} %all-to-all-done), kind=kOutput, calls=%fused_computation.29 | convolution fusion | flops 11475615744 | bytes 43057152 | tf_op jit(solution)/shard_map/sekd,edf->sekf/dot_general | solution.py:126
  241.6 44.4 %all-gather.12.cloned.1.call-done = bf16[2,3072,768]{2,1,0:T(8,128)(2,1)} async-done(((bf16[2,768,768]{2,1,0:T(8,128)(2,1)}), bf16[2,3072,768]{2,1,0:T(8,128)(2,1)}) %all-gather.12.cloned.1.call-update) | async-done | bytes 9437200 | tf_op jit(solution)/shard_map/all_gather | solution.py:74
  286.0 23.6 %convert_bitcast_fusion.1 = bf16[8,2,152,768]{3,2,0,1:T(8,128)(2,1)} fusion(bf16[2,3072,768]{2,1,0:T(8,128)(2,1)} %all-gather.12.cloned.1.call-done, f32[2,8,152,3072]{3,2,1,0:T(8,128)} %fusion.15), kind=kOutput, calls=%fused_computation.62 | convolution fusion | flops 11544723456 | bytes 43057152 | tf_op jit(solution)/shard_map/sekf,efd->sekd/dot_general | solution.py:130
  318.6 35.3 %fusion.6 = bf16[8,2,152,3072]{3,2,0,1:T(8,128)(2,1)} fusion(f32[2,8,152,3072]{3,2,1,0:T(8,128)} %fusion.15, bf16[2,3072,768]{2,1,0:T(8,128)(2,1)} %all-gather.12.cloned.1.call-done, bf16[8,2,152,768]{3,2,1,0:T(8,128)(2,1)} %all-to-all-done.2), kind=kOutput, calls=%fused_computation.13 | convolution fusion | flops 11625037824 | bytes 57999360 | tf_op jit(solution)/shard_map/sekd,efd->sekf/dot_general | solution.py:150
  353.9 19.2 %convert_bitcast_fusion = bf16[8,2,152,768]{3,2,0,1:T(8,128)(2,1)} fusion(bf16[8,2,152,3072]{3,2,0,1:T(8,128)(2,1)} %fusion.6, bf16[2,768,3072]{2,1,0:T(8,128)(2,1)} %all-gather.10.cloned.1.call-done), kind=kOutput, calls=%fused_computation.61 | convolution fusion | flops 11477483520 | bytes 28114944 | tf_op jit(solution)/shard_map/sekf,edf->sekd/dot_general | solution.py:155
  377.3 25.5 %all-to-all-done.1 = bf16[8,2,152,768]{3,2,1,0:T(8,128)(2,1)} async-done(((bf16[8,2,152,768]{3,2,1,0:T(8,128)(2,1)}), bf16[8,2,152,768]{3,2,1,0:T(8,128)(2,1)}, u32[]{:S(2)}, u32[]{:S(2)}) %all-to-all-start.1) | async-done | bytes 3735584 | tf_op jit(solution)/shard_map/all_to_all | solution.py:133
  409.0 10.3 gather_fusion.1
  425.9 13.6 %multiply_reduce_fusion.2 = (f32[788,2]{1,0:T(8,128)S(1)}, f32[788,768]{1,0:T(8,128)}) fusion(f32[788,2,768]{2,1,0:T(2,128)} %reshape.334, f32[788,768]{1,0:T(8,128)S(1)} %copy-done.25, f32[788,2]{1,0:T(8,128)S(1)} %copy-done.30), kind=kLoop, calls=%fused_computation.44 | loop fusion | flops 4234712 | bytes 9695552 | tf_op jit(solution)/shard_map/reduce_sum | solution.py:143
  439.9 51.6 %all-to-all-done.3 = bf16[8,2,152,768]{3,2,1,0:T(8,128)(2,1)} async-done(((bf16[8,2,152,768]{3,2,1,0:T(8,128)(2,1)}), bf16[8,2,152,768]{3,2,1,0:T(8,128)(2,1)}, u32[]{:S(2)}, u32[]{:S(2)}) %all-to-all-start.3) | async-done | bytes 3735584 | tf_op jit(solution)/shard_map/all_to_all | solution.py:158
  491.5 10.4 gather_fusion.3
  506.5 9.7 reduce_sum.453
  545.3 12.2 %multiply_convert_fusion = bf16[4,12,197,197]{2,3,1,0:T(8,128)(2,1)} fusion(f32[4,12,197,197]{2,3,1,0:T(8,128)} %get-tuple-element.262, f32[4,12,197,197]{2,3,1,0:T(8,128)} %copy-done, f32[4,12,197]{2,1,0:T(8,128)S(1)} %get-tuple-element.261, f32[4,12,197]{2,1,0:T(8,128)S(1)} %copy-done.34), kind=kLoop, calls=%fused_computation.23 | loop fusion | flops 9314160 | bytes 18703968 | tf_op jit(solution)/shard_map/convert_element_type | solution.py:203
  577.6 9.7 convert_element_type.140
  587.3 8.7 fusion.103
  599.6 71.3 %reduce-scatter.12.cloned.1.call-done = f32[192,2304]{1,0:T(8,128)} async-done(((f32[768,2304]{1,0:T(8,128)}), f32[192,2304]{1,0:T(8,128)}) %reduce-scatter.12.cloned.1.call-update) | async-done | bytes 1769488 | tf_op jit(solution)/shard_map/reduce_scatter | solution.py:229
  671.0 25.0 %convolution_bitcast_fusion = f32[2,3072,768]{2,1,0:T(8,128)} fusion(bf16[8,2,152,768]{3,2,1,0:T(8,128)(2,1)} %all-to-all-done.2, f32[2,8,152,3072]{3,2,1,0:T(8,128)} %fusion.15), kind=kOutput, calls=%fused_computation.37 | convolution fusion | flops 11542855680 | bytes 52494336 | tf_op jit(solution)/shard_map/sekf,sekd->efd/dot_general | solution.py:162
  696.1 20.9 %fusion.23 = f32[2,768,3072]{2,1,0:T(8,128)} fusion(bf16[8,2,152,768]{3,2,1,0:T(8,128)(2,1)} %all-to-all-done, bf16[8,2,152,3072]{3,2,0,1:T(8,128)(2,1)} %fusion.6), kind=kOutput, calls=%fused_computation.36 | convolution fusion | flops 11475615744 | bytes 37552128 | tf_op jit(solution)/shard_map/sekd,sekf->edf/dot_general | solution.py:159
  726.4 8.7 fusion.51
  735.0 9.3 all-reduce.11
  745.4 27.2 %all-reduce.7 = (f32[192]{0:T(256)S(1)}, f32[192]{0:T(256)S(1)}, f32[192,16]{0,1:T(8,128)S(1)}) all-reduce(f32[192]{0:T(256)S(1)} %dynamic-slice.3, f32[192]{0:T(256)S(1)} %dynamic-slice.5, f32[192,16]{0,1:T(8,128)S(1)} %copy.173), channel_id=1, replica_groups=mesh['expert'=8,'shard'=4] {'expert'}, use_global_device_ids=true, to_apply=%region_24.25 | all-reduce | flops 3456 | bytes 27648 | tf_op jit(solution)/shard_map/psum | solution.py:224
  783.6 158.6 %reduce-scatter.10.cloned.1.call-done = f32[2,768,768]{2,1,0:T(8,128)} async-done(((f32[2,3072,768]{2,1,0:T(8,128)}), f32[2,768,768]{2,1,0:T(8,128)}) %reduce-scatter.10.cloned.1.call-update) | async-done | bytes 4718608 | tf_op jit(solution)/shard_map/reduce_scatter | solution.py:167
  945.5 171.4 %reduce-scatter.8.cloned.1.call-done = f32[2,768,768]{2,1,0:T(8,128)} async-done(((f32[2,768,3072]{2,1,0:T(8,128)}), f32[2,768,768]{2,1,0:T(8,128)}) %reduce-scatter.8.cloned.1.call-update) | async-done | bytes 4718608 | tf_op jit(solution)/shard_map/reduce_scatter | solution.py:166
  1120.0 15.4 %all-reduce.10 = (f32[8]{0:T(128)S(1)}, f32[2304]{0:T(1024)S(1)}, f32[768]{0:T(1024)S(1)}, f32[16]{0:T(128)S(1)}, f32[2,3]{0,1:T(4,128)S(1)}, /*index=5*/f32[2,768]{1,0:T(2,128)S(1)}, f32[2,768]{1,0:T(2,128)S(1)}) all-reduce(f32[8]{0:T(128)S(1)} %stack.99, ...), channel_id=1, replica_groups=mesh['expert'=8,'shard'=4] {'shard'}, use_global_device_ids=true, to_apply=%region_50.51 | all-reduce | flops 6174 | bytes 49392 | tf_op jit(solution)/shard_map/psum | solution.py:275
  1154.9 8.8 all-reduce.9
  (394 shorter events, 233.7 us)
Async XLA Ops:
  7.3 52.7 %all-gather.6.cloned.1.call-start = ((), (), s32[]{:S(2)}) async-start(), calls=%async_computation.9 | async-start | bytes 4423680 | tf_op jit(solution)/shard_map/all_gather | solution.py:67
  8.0 104.2 %all-gather.8.cloned.1.call-start = ((), (), s32[]{:S(2)}) async-start(), calls=%async_computation.10 | async-start | bytes 1474560 | tf_op jit(solution)/shard_map/all_gather | solution.py:68
  8.7 211.1 %all-gather.10.cloned.1.call-start = ((), (), s32[]{:S(2)}) async-start(), calls=%async_computation.11 | async-start | bytes 11796480 | tf_op jit(solution)/shard_map/all_gather | solution.py:73
  9.5 276.5 %all-gather.12.cloned.1.call-start = ((), (), s32[]{:S(2)}) async-start(), calls=%async_computation.12 | async-start | bytes 11796480 | tf_op jit(solution)/shard_map/all_gather | solution.py:74
  23.4 43.3 %copy-start.70 = (f32[768]{0:T(1024)}, f32[768]{0:T(1024)S(1)}, u32[]{:S(2)}) copy-start(f32[768]{0:T(1024)S(1)} %convert_element_type.115) | copy-start | bytes 9220
  23.7 43.0 %copy-start.64 = (f32[788]{0:T(1024)}, f32[788]{0:T(1024)S(1)}, u32[]{:S(2)}) copy-start(f32[788]{0:T(1024)S(1)} %broadcast_multiply_fusion.6) | copy-start | bytes 9460
  24.2 42.5 %copy-start.73 = (f32[788]{0:T(1024)}, f32[788]{0:T(1024)S(1)}, u32[]{:S(2)}) copy-start(f32[788]{0:T(1024)S(1)} %add_rsqrt_fusion.1) | copy-start | bytes 9460
  24.2 91.5 %copy-start.50 = (f32[768]{0:T(1024)}, f32[768]{0:T(1024)S(1)}, u32[]{:S(2)}) copy-start(f32[768]{0:T(1024)S(1)} %convert_element_type.122) | copy-start | bytes 9220
  125.6 89.4 %all-to-all-start = ((bf16[8,2,152,768]{3,2,1,0:T(8,128)(2,1)}), bf16[8,2,152,768]{3,2,1,0:T(8,128)(2,1)}, u32[]{:S(2)}, u32[]{:S(2)}) async-start(bf16[8,2,152,768]{3,2,1,0:T(8,128)(2,1)} %bitcast.174), calls=%async_computation | async-start | bytes 7471104 | tf_op jit(solution)/shard_map/all_to_all | solution.py:125
  215.0 98.8 %all-to-all-start.2 = ((bf16[8,2,152,768]{3,2,1,0:T(8,128)(2,1)}), bf16[8,2,152,768]{3,2,1,0:T(8,128)(2,1)}, u32[]{:S(2)}, u32[]{:S(2)}) async-start(bf16[8,2,152,768]{3,2,1,0:T(8,128)(2,1)} %bitcast.175), calls=%async_computation.2 | async-start | bytes 7471104 | tf_op jit(solution)/shard_map/all_to_all | solution.py:149
  313.8 89.1 %all-to-all-start.1 = ((bf16[8,2,152,768]{3,2,1,0:T(8,128)(2,1)}), bf16[8,2,152,768]{3,2,1,0:T(8,128)(2,1)}, u32[]{:S(2)}, u32[]{:S(2)}) async-start(bf16[8,2,152,768]{3,2,1,0:T(8,128)(2,1)} %copy.149), calls=%async_computation.1 | async-start | bytes 7471104 | tf_op jit(solution)/shard_map/all_to_all | solution.py:133
  402.8 88.7 %all-to-all-start.3 = ((bf16[8,2,152,768]{3,2,1,0:T(8,128)(2,1)}), bf16[8,2,152,768]{3,2,1,0:T(8,128)(2,1)}, u32[]{:S(2)}, u32[]{:S(2)}) async-start(bf16[8,2,152,768]{3,2,1,0:T(8,128)(2,1)} %copy.152), calls=%async_computation.3 | async-start | bytes 7471104 | tf_op jit(solution)/shard_map/all_to_all | solution.py:158
  407.3 192.3 %reduce-scatter.14.cloned.1.call-start = ((), (), s32[]{:S(2)}) async-start(), calls=%async_computation.16 | async-start | bytes 2949120 | tf_op jit(solution)/shard_map/reduce_scatter | solution.py:230
  527.0 144.0 %reduce-scatter.12.cloned.1.call-start = ((), (), s32[]{:S(2)}) async-start(), calls=%async_computation.15 | async-start | bytes 8847360 | tf_op jit(solution)/shard_map/reduce_scatter | solution.py:229
  596.0 148.5 %reduce-scatter.16.cloned.1.call-start = ((), (), s32[]{:S(2)}) async-start(), calls=%async_computation.17 | async-start | bytes 491520
  599.5 175.0 %all-reduce.15.cloned.1.call-start = ((), (), s32[]{:S(2)}) async-start(), calls=%async_computation.18 | async-start | bytes 4718592 | tf_op jit(solution)/shard_map/psum | solution.py:224
  671.0 271.2 %reduce-scatter.10.cloned.1.call-start = ((), (), s32[]{:S(2)}) async-start(), calls=%async_computation.14 | async-start | bytes 23592960 | tf_op jit(solution)/shard_map/reduce_scatter | solution.py:167
  696.1 420.8 %reduce-scatter.8.cloned.1.call-start = ((), (), s32[]{:S(2)}) async-start(), calls=%async_computation.13 | async-start | bytes 23592960 | tf_op jit(solution)/shard_map/reduce_scatter | solution.py:166
  726.3 46.5 %copy-start.98 = (f32[192]{0:T(256)S(1)}, f32[192]{0:T(256)}, u32[]{:S(2)}) copy-start(f32[192]{0:T(256)} %param.39) | copy-start | bytes 2308
  726.3 47.1 %copy-start.99 = (f32[192]{0:T(256)S(1)}, f32[192]{0:T(256)}, u32[]{:S(2)}) copy-start(f32[192]{0:T(256)} %param.34) | copy-start | bytes 2308
  726.3 47.1 %copy-start.100 = (f32[192]{0:T(256)S(1)}, f32[192]{0:T(256)}, u32[]{:S(2)}) copy-start(f32[192]{0:T(256)} %param.33) | copy-start | bytes 2308
  726.3 51.4 %copy-start.101 = (f32[192]{0:T(256)S(1)}, f32[192]{0:T(256)}, u32[]{:S(2)}) copy-start(f32[192]{0:T(256)} %param.37) | copy-start | bytes 2308
  726.3 51.4 %copy-start.102 = (f32[192]{0:T(256)S(1)}, f32[192]{0:T(256)}, u32[]{:S(2)}) copy-start(f32[192]{0:T(256)} %param.35) | copy-start | bytes 2308
  735.0 210.3 %copy-start.81 = (f32[2,768]{1,0:T(2,128)S(1)}, f32[2,768]{1,0:T(2,128)}, u32[]{:S(2)}) copy-start(f32[2,768]{1,0:T(2,128)} %param.43) | copy-start | bytes 18436
  772.7 392.2 %copy-start.40 = (f32[192,16]{0,1:T(8,128)}, f32[192,16]{0,1:T(8,128)S(1)}, u32[]{:S(2)}) copy-start(f32[192,16]{0,1:T(8,128)S(1)} %get-tuple-element.288) | copy-start | bytes 36868
  773.4 391.4 %copy-start.79 = (f32[192]{0:T(256)}, f32[192]{0:T(256)S(1)}, u32[]{:S(2)}) copy-start(f32[192]{0:T(256)S(1)} %get-tuple-element.290) | copy-start | bytes 2308
  778.3 367.8 %copy-start.78 = (f32[192]{0:T(256)}, f32[192]{0:T(256)S(1)}, u32[]{:S(2)}) copy-start(f32[192]{0:T(256)S(1)} %get-tuple-element.282) | copy-start | bytes 2308
  778.3 387.9 %copy-start.80 = (f32[192]{0:T(256)}, f32[192]{0:T(256)S(1)}, u32[]{:S(2)}) copy-start(f32[192]{0:T(256)S(1)} %get-tuple-element.286) | copy-start | bytes 2308
  783.6 351.8 %copy-start.82 = (f32[2,768]{1,0:T(2,128)S(1)}, f32[2,768]{1,0:T(2,128)}, u32[]{:S(2)}) copy-start(f32[2,768]{1,0:T(2,128)} %param.41) | copy-start | bytes 18436
  783.6 354.9 %copy-start.83 = (f32[2,768]{1,0:T(2,128)S(1)}, f32[2,768]{1,0:T(2,128)}, u32[]{:S(2)}) copy-start(f32[2,768]{1,0:T(2,128)} %param.42) | copy-start | bytes 18436
  783.6 355.0 %copy-start.84 = (f32[2,768]{1,0:T(2,128)S(1)}, f32[2,768]{1,0:T(2,128)}, u32[]{:S(2)}) copy-start(f32[2,768]{1,0:T(2,128)} %param.44) | copy-start | bytes 18436
  945.5 230.1 %copy-start.56 = (f32[2,768]{1,0:T(2,128)}, f32[2,768]{1,0:T(2,128)S(1)}, u32[]{:S(2)}) copy-start(f32[2,768]{1,0:T(2,128)S(1)} %get-tuple-element.298) | copy-start | bytes 18436
  (94 other events, 858.7 us)
Sparse Core Ops, SparseCore 0:
  9.9 49.9 all-gather.5
  61.8 27.7 all-gather.7
  91.4 96.5 all-gather.9
  189.6 96.3 all-gather.11
  527.1 35.2 reduce-scatter.13
  596.1 74.8 reduce-scatter.11
  674.3 24.3 reduce-scatter.15
  701.2 66.9 all-reduce.14
  771.8 170.2 reduce-scatter.9
  946.0 170.7 reduce-scatter.7
where the time goes:
time: 1200 us; the launch traced here: 1190 us
  waiting for transfers between devices  597 us (50%)
  matrix products  210 us (18%)
  local copies, waits for them, and re-layouts  164 us (14%)
  other arithmetic  104 us (9%)
  blocking collectives  80.2 us (7%)
  starting transfers between devices  19.9 us (2%)
  between operations  19.7 us (2%)
    reduce_scatter x1, waiting for transfers between devices, local(): lax.psum_scatter(grad_first, 'shard', scatter_dimension=2, tiled=True)  171 us
    reduce_scatter x1, waiting for transfers between devices, local(): lax.psum_scatter(grad_second, 'shard', scatter_dimension=1, tiled=True)  159 us
    reduce_scatter x1, waiting for transfers between devices, local(): lax.psum_scatter(dense_total[1], 'shard', scatter_dimension=0, tiled=True)  71.3 us
    all_to_all x1, waiting for transfers between devices, local(): lax.all_to_all(grad_rows, 'expert', split_axis=0, concat_axis=0, tiled=True)  51.6 us
    all_to_all x1, waiting for transfers between devices, local(): lax.all_to_all(send_rows, 'expert', split_axis=0, concat_axis=0, tiled=True)  51.3 us
    all_gather x1, waiting for transfers between devices, local(): lax.all_gather(w_out, 'shard', axis=1, tiled=True)  44.4 us
    dot_general x1, matrix products, local(): jnp.einsum('sekd,efd->sekf', grad_recv, second_full, preferred_element_ty...  35.3 us
    unnamed x241, local copies, waits for them, and re-layouts  28.9 us
  transfers between devices with their start and end apart: 14, of which 8 were waited for; matrix products, arithmetic and copies ran while one was open for 33% of the time, Pallas kernels for 0%

commit v1 on v0

--- a/solution.py
+++ b/solution.py
@@ -1,6 +1,10 @@
+import functools
+
 import jax
 import jax.numpy as jnp
 from jax import lax
+from jax.experimental import pallas as pl
+from jax.experimental.pallas import tpu as pltpu
 from jax.sharding import PartitionSpec as P
 
 D = 768
@@ -18,6 +22,10 @@
 CLIP = 0.05
 
 
+GELU_A = 0.7978845608028654
+GELU_B = 0.044715
+
+
 def normalize(values):
     center = values - jnp.mean(values, axis=-1, keepdims=True)
     inv_root = lax.rsqrt(jnp.mean(center * center, axis=-1, keepdims=True) + EPS_NORM)
@@ -38,7 +46,7 @@
     return jax.nn.gelu(values, approximate=True)
 
 
-def local(
+def general(
     tokens,
     routes,
     cotangent,
@@ -49,18 +57,6 @@
     w_router,
     w_in,
     w_out,
-    v_attn,
-    v_moe,
-    row_qkv,
-    col_qkv,
-    row_proj,
-    col_proj,
-    row_router,
-    col_router,
-    row_in,
-    col_in,
-    row_out,
-    col_out,
 ):
     gain_first, qkv_full, proj_full, gain_second, router_full = (
         lax.all_gather(gain_attn, "shard", axis=0, tiled=True),
@@ -110,8 +106,11 @@
     chosen = jnp.sum(route_hits * logits[:, None, :], axis=2)
     gates = jax.nn.softmax(chosen, axis=-1)
     flat_routes = routes.reshape(-1)
-    one_hot = (flat_routes[:, None] == labels[None, :]).astype(jnp.int32)
-    slot_rank = jnp.sum((jnp.cumsum(one_hot, axis=0) - 1) * one_hot, axis=1)
+    earlier = (jnp.arange(row_count)[:, None] > jnp.arange(row_count)[None, :]).astype(jnp.bfloat16)
+    before = jnp.dot(
+        earlier, jnp.sum(route_hits, axis=1).astype(jnp.bfloat16), preferred_element_type=jnp.float32
+    )
+    slot_rank = jnp.sum(route_hits * before[:, None, :], axis=2).astype(jnp.int32).reshape(-1)
     slot_dest = flat_routes * capacity + slot_rank
     pair_index = jnp.arange(2 * row_count, dtype=jnp.int32)
     slot_pair = (
@@ -231,126 +230,895 @@
         lax.psum_scatter(dense_total[3], "shard", scatter_dimension=0, tiled=True),
         lax.psum_scatter(dense_total[4], "shard", scatter_dimension=0, tiled=True),
     )
+    return block_out, grad_tokens, dense_parts, (grad_first, grad_second)
+
+
+SEQ_PAD = 224
+MESH = pl.DeviceIdType.MESH
+VMEM_LIMIT = 62 * 1024 * 1024
+BF = jnp.bfloat16
+F32 = jnp.float32
+
+
+def mm(a, b):
+    return lax.dot_general(a, b, (((1,), (0,)), ((), ())), preferred_element_type=F32)
+
+
+def mm_nt(a, b):
+    return lax.dot_general(a, b, (((1,), (1,)), ((), ())), preferred_element_type=F32)
+
+
+def mm_tn(a, b):
+    return lax.dot_general(a, b, (((0,), (0,)), ((), ())), preferred_element_type=F32)
+
+
+def remote(src, dst, send, recv, device):
+    return pltpu.make_async_remote_copy(
+        src_ref=src, dst_ref=dst, send_sem=send, recv_sem=recv, device_id=device, device_id_type=MESH
+    )
+
+
+def greet(devices):
+    barrier = pltpu.get_barrier_semaphore()
+    for device in devices:
+        pl.semaphore_signal(barrier, inc=1, device_id=device, device_id_type=MESH)
+    pl.semaphore_wait(barrier, len(devices))
+
+
+class Place:
+    def __init__(self):
+        expert = lax.axis_index("expert")
+        self.shard = lax.axis_index("shard")
+        self.z, self.core = expert // 2, expert % 2
+        self.number = self.z * 4 + self.shard
+        self.sibling = (self.z * 2 + 1 - self.core, self.shard)
+
+    def plane(self, step):
+        return (self.z // 2 + step // 2) % 2 * 2 + (self.z + step) % 2
+
+    def peer(self, number):
+        return (number // 4 * 2 + self.core, number % 4)
+
+    def peers(self):
+        return [self.peer((self.number + d) % 16) for d in range(1, 16)]
+
+    def mates(self):
+        return [(self.z * 2 + self.core, (self.shard + d) % 4) for d in range(1, 4)]
+
+
+def split3(rows):
+    high = rows.astype(BF)
+    rest = rows - high.astype(F32)
+    low = rest.astype(BF)
+    last = (rest - low.astype(F32)).astype(BF)
+    return high, low, last
+
+
+def three_rows(row):
+    high, low, last = split3(row)
+    index = lax.broadcasted_iota(jnp.int32, (8, row.shape[1]), 0)
+    out = jnp.where(index == 0, high.astype(F32), 0.0)
+    out = jnp.where(index == 1, low.astype(F32), out)
+    return jnp.where(index == 2, last.astype(F32), out).astype(BF)
+
+
+def norm_stats(values):
+    center = values - jnp.mean(values, axis=-1, keepdims=True)
+    inv = lax.rsqrt(jnp.mean(center * center, axis=-1, keepdims=True) + EPS_NORM)
+    return center * inv, inv
+
+
+def fill_hits(ranks, plane, hits, cap):
+    slot = lax.broadcasted_iota(jnp.int32, (cap, hits.shape[1]), 0)
+    for k in range(4):
+        row = ranks[pl.ds(plane * 4 + k, 1), :]
+        hits[k * cap : (k + 1) * cap, :] = jnp.where(slot == row, 1.0, 0.0).astype(BF)
+
+
+def kernel_a(
+    cap, tok, cot, rt, dsh, w1, w2,
+    qkv, att, hid, lse, gate_t, ranks, aux, dense, xsend, gsend, cotr, wfull,
+    csend, low, hits, tri, dsem, dfsem, csem, wsem, wloc, wrecv, fsem, osem,
+):
+    me = Place()
+    z, c, s = me.z, me.core, me.shard
+    rows = tok.shape[0]
+    images = rows // SEQ_PAD
+    other = [(z * 2 + 1 - c, t) for t in range(4)]
+    greet(me.peers() + other)
+
+    quarter = dsh.shape[0]
+    half = quarter // 2
+    dense_out = []
+    for d in range(1, 4):
+        cp = remote(
+            dsh.at[pl.ds(pl.multiple_of(c * half, half), half)],
+            dense.at[pl.ds(pl.multiple_of(s * quarter + c * half, half), half)],
+            dsem.at[0, d], dsem.at[1, d], (z * 2 + c, (s + d) % 4),
+        )
+        cp.start()
+        dense_out.append(cp)
+    dense[pl.ds(pl.multiple_of(s * quarter, quarter), quarter), :] = dsh[...]
+
+    expert_row = lax.broadcasted_iota(jnp.int32, (16, rows), 0)
+    hit = (expert_row == rt[0:1, :]) | (expert_row == rt[1:2, :])
+    earlier = lax.broadcasted_iota(jnp.int32, (rows, rows), 0) < lax.broadcasted_iota(jnp.int32, (rows, rows), 1)
+    tri[...] = jnp.where(earlier, 1.0, 0.0).astype(BF)
+    before = mm(jnp.where(hit, 1.0, 0.0).astype(BF), tri[...])
+    ranks[...] = jnp.where(hit, before, -1.0).astype(jnp.int32)
+
+    def cot_copy(p):
+        return remote(
+            csend.at[pl.ds(pl.multiple_of(p * cap, cap), cap)],
+            cotr.at[pl.ds(pl.multiple_of(me.number * cap, cap), cap)],
+            csem.at[0, p], csem.at[1, me.number], me.peer(p),
+        )
+
+    own = pl.multiple_of(me.number * cap, cap)
+    own_copy = pltpu.make_async_copy(csend.at[pl.ds(own, cap)], cotr.at[pl.ds(own, cap)], osem)
+
+    @pl.loop(0, 4)
+    def _(step):
+        plane = me.plane(3 - step)
+        fill_hits(ranks, plane, hits, cap)
+        csend[pl.ds(pl.multiple_of(plane * 4 * cap, 4 * cap), 4 * cap), :] = mm(hits[...], cot[...]).astype(BF)
+        for k in range(4):
+            p = plane * 4 + k
+
+            @pl.when(p != me.number)
+            def _():
+                cot_copy(p).start()
+
+            @pl.when(p == me.number)
+            def _():
+                own_copy.start()
+
+    forwards = []
+    for d in range(1, 4):
+        dense_out[d - 1].wait()
+        source = (s - d + 4) % 4
+        place = pl.ds(pl.multiple_of(source * quarter + c * half, half), half)
+        cp = remote(dense.at[place], dense.at[place], dfsem.at[0, d], dfsem.at[1, d], me.sibling)
+        cp.start()
+        forwards.append(cp)
+
+    def quarters(act, own=True):
+        for i in range(2):
+            for a, w in ((0, w1), (1, w2)):
+                target = 2 * c + i
+                self_target = (a == c) & (target == s)
+
+                @pl.when(jnp.logical_not(self_target))
+                def _():
+                    act(remote(w.at[i], wfull.at[a, s], wsem.at[i, a], wrecv.at[s], (z * 2 + a, target)), False)
+
+                if own:
+
+                    @pl.when(self_target)
+                    def _():
+                        act(pltpu.make_async_copy(w.at[i], wfull.at[a, s], wloc), True)
+
+    for cp in forwards:
+        cp.wait()
+    quarters(lambda cp, local_copy: cp.start())
+
+    flat = jnp.transpose(dense[:, 3072:3200].astype(F32))
+    aux[...] = flat[0:32, :]
+
+    @pl.loop(0, images)
+    def _(i):
+        r = pl.ds(pl.multiple_of(i * SEQ_PAD, SEQ_PAD), SEQ_PAD)
+        hat, _unused = norm_stats(tok[r, :].astype(F32))
+        low[r, :] = (hat * aux[16:17, :]).astype(BF)
+
+    @pl.loop(0, 3)
+    def _(n):
+        columns = pl.ds(pl.multiple_of(n * D, D), D)
+        qkv[:, columns] = mm(low[...], dense[:, columns]).astype(BF)
+
+    attention_forward(qkv, att, lse, images)
+
+    wproj = dense.at[:, 2304:3072]
+    @pl.loop(0, images)
+    def _(i):
+        r = pl.ds(pl.multiple_of(i * SEQ_PAD, SEQ_PAD), SEQ_PAD)
+        hidden = tok[r, :].astype(F32) + mm(att[r, :], wproj[...])
+        hid[r, :] = hidden
+        hat, _unused = norm_stats(hidden)
+        low[r, :] = (hat * aux[17:18, :]).astype(BF)
+
+    logits = mm_nt(aux[0:16, :].astype(BF), low[...])
+    masked = jnp.where(hit, logits, -1e30)
+    weights = jnp.where(hit, jnp.exp(masked - jnp.max(masked, axis=0, keepdims=True)), 0.0)
+    gate_t[...] = weights / jnp.maximum(jnp.sum(weights, axis=0, keepdims=True), 0.5)
+    gsend[...] = jnp.zeros_like(gsend)
+
+    @pl.loop(0, 4)
+    def _(plane):
+        fill_hits(ranks, plane, hits, cap)
+        xsend[pl.ds(pl.multiple_of(plane * 4 * cap, 4 * cap), 4 * cap), :] = mm(hits[...], low[...]).astype(BF)
+        for k in range(4):
+            row = mm_nt(three_rows(gate_t[pl.ds(plane * 4 + k, 1), :]), hits[k * cap : (k + 1) * cap, :])
+            gsend[plane * 4 + k, :, 0:cap] = jnp.broadcast_to(jnp.sum(row, axis=0, keepdims=True), (8, cap))
+
+    source_core = s // 2
+    for t in range(4):
+        arrives_here = (source_core == c) & (s == t)
+
+        @pl.when(jnp.logical_not(arrives_here))
+        def _():
+            remote(w1.at[0], wfull.at[c, t], wsem.at[0, 0], wrecv.at[t], me.sibling).wait_recv()
+
+        @pl.when(arrives_here)
+        def _():
+            pltpu.make_async_copy(w1.at[0], wfull.at[c, t], wloc).wait()
+
+        remote(wfull.at[c, t], wfull.at[c, t], fsem.at[0, t], fsem.at[1, t], me.sibling).start()
+    quarters(lambda cp, local_copy: cp.wait_send(), own=False)
+    for t in range(4):
+        remote(wfull.at[c, t], wfull.at[c, t], fsem.at[0, t], fsem.at[1, t], me.sibling).wait_send()
+        remote(wfull.at[1 - c, t], wfull.at[1 - c, t], fsem.at[0, t], fsem.at[1, t], me.sibling).wait_recv()
+    for d in range(1, 16):
+        p = (me.number + d) % 16
+        cot_copy(p).wait_send()
+        remote(
+            csend.at[pl.ds(0, cap)], cotr.at[pl.ds(0, cap)], csem.at[0, p], csem.at[1, p], me.peer(p)
+        ).wait_recv()
+    own_copy.wait()
+
+
+def attention_forward(qkv, att, lse, images):
+    first = lax.broadcasted_iota(jnp.int32, (SEQ_PAD, 128), 1) < HEAD
+    lane = lax.broadcasted_iota(jnp.int32, (SEQ_PAD, 128), 1)
+    real = lax.broadcasted_iota(jnp.int32, (SEQ_PAD, SEQ_PAD), 1) < SEQ
+    lse[...] = jnp.zeros_like(lse)
+
+    @pl.loop(0, HEADS // 2)
+    def _(pair):
+        for i in range(images):
+            r = slice(i * SEQ_PAD, (i + 1) * SEQ_PAD)
+            cols = [pl.ds(pl.multiple_of(part * D + pair * 128, 128), 128) for part in range(3)]
+            q, k, v = (qkv[r, cols[part]] for part in range(3))
+            outs, lses = [], []
+            for h in range(2):
+                mine = first if h == 0 else jnp.logical_not(first)
+                qh = (jnp.where(mine, q.astype(F32), 0.0) * 0.125).astype(BF)
+                scores = jnp.where(real, mm_nt(qh, k), -1e30)
+                top = jnp.max(scores, axis=1, keepdims=True)
+                weights = jnp.exp(scores - top)
+                total = jnp.sum(weights, axis=1, keepdims=True)
+                lses.append(top + jnp.log(total))
+                outs.append(mm((weights * (1.0 / total)).astype(BF), v))
+            att[r, pl.ds(pl.multiple_of(pair * 128, 128), 128)] = jnp.where(first, outs[0], outs[1]).astype(BF)
+            old = lse[r, :]
+            lse[r, :] = jnp.where(lane == 2 * pair, lses[0], jnp.where(lane == 2 * pair + 1, lses[1], old))
+
+
+def kernel_e(
+    cap, xsend, gsend, cotr, wfull,
+    outs, ginh, ginb, ggb, gw,
+    w1v, w2v, xr, gcot, gater, act, gpre, acc, stage, ggs, gcol,
+    xsem, gsem, rsem, ggsem, lsem, wlsem, stsem,
+):
+    me = Place()
+    z, c, s = me.z, me.core, me.shard
+    greet(me.peers())
+    block = 4 * cap
+
+    def part(ref, p):
+        return ref.at[pl.ds(pl.multiple_of(p * cap, cap), cap)]
+
+    def x_copy(p):
+        return remote(part(xsend, p), part(xr, me.number), xsem.at[0, p], xsem.at[1, me.number], me.peer(p))
+
+    def g_copy(p):
+        return remote(gsend.at[p], gater.at[me.number], gsem.at[0, p], gsem.at[1, me.number], me.peer(p))
+
+    def r_copy(p):
+        return remote(part(ginh, p), part(ginb, me.number), rsem.at[0, p], rsem.at[1, me.number], me.peer(p))
+
+    def gg_copy(p):
+        return remote(ggs.at[p], ggb.at[me.number], ggsem.at[0, p], ggsem.at[1, me.number], me.peer(p))
+
+    local_copies = [
+        pltpu.make_async_copy(part(xsend, me.number), part(xr, me.number), lsem.at[0]),
+        pltpu.make_async_copy(gsend.at[me.number], gater.at[me.number], lsem.at[1]),
+        pltpu.make_async_copy(cotr, gcot, lsem.at[2]),
+    ]
+    own_r = pltpu.make_async_copy(part(ginh, me.number), part(ginb, me.number), lsem.at[3])
+    own_g = pltpu.make_async_copy(ggs.at[me.number], ggb.at[me.number], lsem.at[4])
+    w_copies = [pltpu.make_async_copy(wfull.at[0], w1v, wlsem.at[0])] + [
+        pltpu.make_async_copy(wfull.at[1, f], w2v.at[pl.ds(f * D, D)], wlsem.at[1 + f]) for f in range(4)
+    ]
+    for d in range(1, 16):
+        g_copy((me.number + d) % 16).start()
+    for cp in local_copies + w_copies:
+        cp.start()
+    for step in range(4):
+        for k in range(4):
+            p = me.plane(step) * 4 + k
+
+            @pl.when(p != me.number)
+            def _():
+                x_copy(p).start()
+
+    ggs[...] = jnp.zeros_like(ggs)
+    for cp in local_copies + w_copies:
+        cp.wait()
+
+    eye = lax.broadcasted_iota(jnp.int32, (cap, cap), 0) == lax.broadcasted_iota(jnp.int32, (cap, cap), 1)
+
+    def recv_block(plane):
+        for k in range(4):
+            p = plane * 4 + k
+
+            @pl.when(p != me.number)
+            def _():
+                remote(part(xsend, p), part(xr, p), xsem.at[0, p], xsem.at[1, p], me.peer(p)).wait_recv()
+                remote(gsend.at[p], gater.at[p], gsem.at[0, p], gsem.at[1, p], me.peer(p)).wait_recv()
+
+    def stage_out(plane, which):
+        return pltpu.make_async_copy(
+            stage.at[which], (outs if which == 0 else ginh).at[pl.ds(pl.multiple_of(plane * block, block), block)],
+            stsem.at[which],
+        )
+
+    @pl.loop(0, 4)
+    def _(step):
+        plane = me.plane(step)
+        recv_block(plane)
+        r = pl.ds(pl.multiple_of(plane * block, block), block)
+
+        @pl.loop(0, 4)
+        def _(f):
+            for n in range(3):
+                cols = pl.ds(pl.multiple_of(f * D + n * 256, 256), 256)
+                pre = mm(xr[r, :], w1v[f, :, n * 256 : (n + 1) * 256])
+                square = pre * pre
+                t = jnp.tanh(pre * (GELU_A + GELU_A * GELU_B * square))
+                half = 0.5 + 0.5 * t
+                act[r, cols] = (pre * half).astype(BF)
+                slope = half + (0.5 * pre) * (1.0 - t * t) * (GELU_A + 3.0 * GELU_A * GELU_B * square)
+                gpre[r, cols] = slope.astype(BF)
+
+        acc[...] = mm(act[r, :], w2v[...])
+
+        for k in range(4):
+            row = gater[plane * 4 + k, 0:1, 0:cap]
+            column = jnp.sum(jnp.where(eye, row, 0.0), axis=1, keepdims=True)
+            gcol[k * cap : (k + 1) * cap, :] = jnp.broadcast_to(column, (cap, 128))
+
+        @pl.when(step > 0)
+        def _():
+            stage_out(plane, 0).wait()
+
+        for k in range(4):
+            rk = pl.ds(pl.multiple_of(plane * block + k * cap, cap), cap)
+            kk = slice(k * cap, (k + 1) * cap)
+            out = acc[kk, :].astype(BF).astype(F32)
+            gate = gcol[kk, 0:1]
+            g = gcot[rk, :].astype(F32)
+            dots = jnp.sum(g * out, axis=1, keepdims=True)
+            row = jnp.sum(jnp.where(eye, dots, 0.0), axis=0, keepdims=True)
+            ggs[plane * 4 + k, :, 0:cap] = jnp.broadcast_to(row, (8, cap))
+            stage[0, kk, :] = (gate * out).astype(BF)
+            gcot[rk, :] = (gate * g).astype(BF)
+        stage_out(plane, 0).start()
+
+        @pl.loop(0, 4)
+        def _(f):
+            for n in range(3):
+                cols = pl.ds(pl.multiple_of(f * D + n * 256, 256), 256)
+                ga = mm_nt(gcot[r, :], w2v[cols, :])
+                gpre[r, cols] = (ga * gpre[r, cols].astype(F32)).astype(BF)
+
+        acc[...] = mm_nt(gpre[r, 0:D], w1v[0])
+        for f in range(1, 4):
+            acc[...] += mm_nt(gpre[r, f * D : (f + 1) * D], w1v[f])
+        stage[1] = acc[...].astype(BF)
+        stage_out(plane, 1).start()
+        stage_out(plane, 1).wait()
+        for k in range(4):
+            p = plane * 4 + k
+
+            @pl.when(p != me.number)
+            def _():
+                r_copy(p).start()
+                gg_copy(p).start()
+
+            @pl.when(p == me.number)
+            def _():
+                own_r.start()
+                own_g.start()
+
+    stage_out(0, 0).wait()
+
+    @pl.loop(0, 4)
+    def _(f):
+        cols = pl.ds(pl.multiple_of(f * D, D), D)
+        w1v[f] = mm_tn(xr[...], gpre[:, cols]).astype(BF)
+        w2v[cols, :] = mm_tn(act[:, cols], gcot[...]).astype(BF)
+
+    out_w = [pltpu.make_async_copy(w1v, gw.at[0], wlsem.at[0])] + [
+        pltpu.make_async_copy(w2v.at[pl.ds(f * D, D)], gw.at[1, f], wlsem.at[1 + f]) for f in range(4)
+    ]
+    for cp in out_w:
+        cp.start()
+    for d in range(1, 16):
+        p = (me.number + d) % 16
+        x_copy(p).wait_send()
+        g_copy(p).wait_send()
+        r_copy(p).wait_send()
+        gg_copy(p).wait_send()
+        remote(part(ginh, p), part(ginb, p), rsem.at[0, p], rsem.at[1, p], me.peer(p)).wait_recv()
+        remote(ggs.at[p], ggb.at[p], ggsem.at[0, p], ggsem.at[1, p], me.peer(p)).wait_recv()
+    own_r.wait()
+    own_g.wait()
+    for cp in out_w:
+        cp.wait()
+
+
+def attention_backward(qkv, gatt, lse, gqkv, images):
+    first = lax.broadcasted_iota(jnp.int32, (SEQ_PAD, 128), 1) < HEAD
+    lane = lax.broadcasted_iota(jnp.int32, (SEQ_PAD, 128), 1)
+    real = lax.broadcasted_iota(jnp.int32, (SEQ_PAD, SEQ_PAD), 1) < SEQ
+
+    @pl.loop(0, HEADS // 2)
+    def _(pair):
+        for i in range(images):
+            r = slice(i * SEQ_PAD, (i + 1) * SEQ_PAD)
+            cols = [pl.ds(pl.multiple_of(part * D + pair * 128, 128), 128) for part in range(3)]
+            q, k, v = (qkv[r, cols[part]] for part in range(3))
+            g = gatt[r, pl.ds(pl.multiple_of(pair * 128, 128), 128)]
+            logs = lse[r, :]
+            parts = []
+            for h in range(2):
+                mine = first if h == 0 else jnp.logical_not(first)
+                qh = (jnp.where(mine, q.astype(F32), 0.0) * 0.125).astype(BF)
+                gh = jnp.where(mine, g.astype(F32), 0.0).astype(BF)
+                log = jnp.sum(jnp.where(lane == 2 * pair + h, logs, 0.0), axis=1, keepdims=True)
+                probs = jnp.where(real, jnp.exp(mm_nt(qh, k) - log), 0.0)
+                grad_probs = mm_nt(gh, v)
+                low = probs.astype(BF)
+                delta = jnp.sum(probs * grad_probs, axis=1, keepdims=True)
+                grad_scores = (probs * (grad_probs - delta)).astype(BF)
+                parts.append((mm(grad_scores, k) * 0.125, mm_tn(grad_scores, q) * 0.125, mm_tn(low, g)))
+            for part in range(3):
+                gqkv[r, cols[part]] = jnp.where(first, parts[0][part], parts[1][part]).astype(BF)
+
+
+def kernel_b(
+    cap, tok, cot, dense, aux, qkv, att, hid, lse, gate_t, ranks, ggb, ginb, outs, gw,
+    block_out, gtok, ghat, extra, outb, eg,
+    rowsv, hits, gmoe, low, glow, gatt, gqkv, gd, ra, rb, sc, rc, exs, exl, gx, own_w, ggt,
+    osem, lsem, wxsem, wsem, wload, wlocal, asem, bsem, zsem, fsem, esem, xsem,
+):
+    me = Place()
+    z, c, s = me.z, me.core, me.shard
+    rows = tok.shape[0]
+    images = rows // SEQ_PAD
+    block = 4 * cap
+    half = D // 8
+    greet(me.peers() + [(z * 2 + 1 - c, t) for t in range(4)])
+
+    def part(ref, p):
+        return ref.at[pl.ds(pl.multiple_of(p * cap, cap), cap)]
+
+    def o_copy(p):
+        return remote(part(outs, p), part(outb, me.number), osem.at[0, p], osem.at[1, me.number], me.peer(p))
+
+    load_in = pltpu.make_async_copy(ginb, rowsv, lsem.at[0])
+    load_in.start()
+    swap = [remote(gw.at[1 - c, t], gx.at[t], wxsem.at[0, t], wxsem.at[1, t], me.sibling) for t in range(4)]
+    for cp in swap:
+        cp.start()
+    own_o = pltpu.make_async_copy(part(outs, me.number), part(outb, me.number), lsem.at[1])
+    own_o.start()
+    for d in range(1, 16):
+        o_copy((me.number + d) % 16).start()
+
+    load_in.wait()
+    gmoe[...] = jnp.zeros_like(gmoe)
+
+    @pl.loop(0, 4)
+    def _(plane):
+        fill_hits(ranks, plane, hits, cap)
+        for k in range(4):
+            rows8 = three_rows(ggb[plane * 4 + k, 0:1, 0:cap])
+            row = mm(rows8, hits[k * cap : (k + 1) * cap, :])
+            ggt[pl.ds(plane * 4 + k, 1), :] = jnp.sum(row, axis=0, keepdims=True)
+        r = pl.ds(pl.multiple_of(plane * block, block), block)
+        gmoe[...] += mm_tn(hits[...], rowsv[r, :])
+
+    gates = gate_t[...]
+    grad_gates = ggt[...]
+    grad_logits = gates * (grad_gates - jnp.sum(gates * grad_gates, axis=0, keepdims=True))
+    gl_high = grad_logits.astype(BF)
+    gl_low = (grad_logits - gl_high.astype(F32)).astype(BF)
+
+    @pl.loop(0, images)
+    def _(i):
+        r = pl.ds(pl.multiple_of(i * SEQ_PAD, SEQ_PAD), SEQ_PAD)
+        hat, _unused = norm_stats(hid[r, :])
+        low[r, :] = (hat * aux[17:18, :]).astype(BF)
+
+    router = aux[0:16, :].astype(BF)
+    gmoe[...] += mm_tn(gl_high, router) + mm_tn(gl_low, router)
+    exs[0, 0:16, :] = mm(gl_high, low[...]) + mm(gl_low, low[...])
+    exs[0, 16:32, :] = jnp.zeros((16, D), F32)
+
+    @pl.loop(0, images)
+    def _(i):
+        r = pl.ds(pl.multiple_of(i * SEQ_PAD, SEQ_PAD), SEQ_PAD)
+        hat, inv = norm_stats(hid[r, :])
+        w = gmoe[r, :]
+        scaled = w * aux[17:18, :]
+        back = inv * (
+            scaled - jnp.mean(scaled, axis=-1, keepdims=True) - hat * jnp.mean(scaled * hat, axis=-1, keepdims=True)
+        )
+        grad = cot[r, :].astype(F32) + back
+        gtok[r, :] = grad
+        glow[r, :] = grad.astype(BF)
+        exs[0, 17:18, :] += jnp.sum(w * hat, axis=0, keepdims=True)
+        hat, _unused = norm_stats(tok[r, :].astype(F32))
+        low[r, :] = (hat * aux[16:17, :]).astype(BF)
+
+    def put(group, value):
+        for t in range(4):
+            for h in range(2):
+                gd[t, h, group] = value[t * 2 * half + h * half : t * 2 * half + (h + 1) * half, :].astype(BF)
+
+    put(3, mm_tn(att[...], glow[...]))
+    gatt[...] = mm_nt(glow[...], dense[:, 2304:3072]).astype(BF)
+
+    def owner_copy(t):
+        return remote(
+            gx.at[t], eg.at[s % 2, c], wsem.at[0, t], wsem.at[1, s % 2 * 2 + c], (z * 2 + s // 2, t)
+        )
+
+    mine_local = s // 2 == c
+    owner_local = pltpu.make_async_copy(gx.at[s], eg.at[s % 2, c], wlocal)
+    for t in range(4):
+        load = pltpu.make_async_copy(gw.at[c, t], own_w, wload)
+        load.start()
+        load.wait()
+        swap[t].wait()
+        gx[t] = (gx[t].astype(F32) + own_w[...].astype(F32)).astype(BF)
+
+        @pl.when(jnp.logical_not(mine_local & (s == t)))
+        def _():
+            owner_copy(t).start()
+
+        @pl.when(mine_local & (s == t))
+        def _():
+            owner_local.start()
+
+    attention_backward(qkv, gatt, lse, gqkv, images)
+
+    for group in range(3):
+        put(group, mm_tn(low[...], gqkv[:, group * D : (group + 1) * D]))
+
+    a_copies = [remote(gd.at[t, 1 - c], ra.at[t], asem.at[0, t], asem.at[1, t], me.sibling) for t in range(4)]
+    for cp in a_copies:
+        cp.start()
+
+    gmoe[...] = mm_nt(gqkv[...], dense[:, 0:2304])
+
+    @pl.loop(0, images)
+    def _(i):
+        r = pl.ds(pl.multiple_of(i * SEQ_PAD, SEQ_PAD), SEQ_PAD)
+        hat, inv = norm_stats(tok[r, :].astype(F32))
+        w = gmoe[r, :]
+        scaled = w * aux[16:17, :]
+        gtok[r, :] += inv * (
+            scaled - jnp.mean(scaled, axis=-1, keepdims=True) - hat * jnp.mean(scaled * hat, axis=-1, keepdims=True)
+        )
+        exs[0, 16:17, :] += jnp.sum(w * hat, axis=0, keepdims=True)
+
+    x_first = remote(exs.at[0], exl.at[0], xsem.at[0, 0], xsem.at[1, 0], me.sibling)
+    x_first.start()
+    b_copies = []
+    for d in range(1, 4):
+        t = (s + d) % 4
+        b_copies.append(remote(gd.at[t, c], rb.at[d], bsem.at[0, d], bsem.at[1, d], (z * 2 + c, t)))
+    for t in range(4):
+        a_copies[t].wait()
+        gd[t, c] = (gd[t, c].astype(F32) + ra[t].astype(F32)).astype(BF)
+    for cp in b_copies:
+        cp.start()
+    x_first.wait()
+    exs[1] = exs[0] + exl[0]
+    exl[1 + s] = exs[1]
+    x_second = [
+        remote(exs.at[1], exl.at[1 + s], xsem.at[0, d], xsem.at[1, d], (z * 2 + c, (s + d) % 4)) for d in range(1, 4)
+    ]
+    for cp in x_second:
+        cp.start()
+    for cp in x_second:
+        cp.wait()
+    exs[2] = (exl[1] + exl[2]) + (exl[3] + exl[4])
+    exl[5 + z] = exs[2]
+    x_third = [
+        remote(exs.at[2], exl.at[5 + z], xsem.at[0, 3 + d], xsem.at[1, 3 + d], ((z + d) % 4 * 2 + c, s))
+        for d in range(1, 4)
+    ]
+    for cp in x_third:
+        cp.start()
+    for cp in b_copies:
+        cp.wait()
+    for g in range(4):
+        sc[g] = (
+            (gd[s, c, g].astype(F32) + rb[1, g].astype(F32)) + (rb[2, g].astype(F32) + rb[3, g].astype(F32))
+        ).astype(BF)
+    z_copies = []
+    for d in range(1, 4):
+        t = (z + d) % 4
+        cp = remote(sc.at[t], rc.at[d], zsem.at[0, d], zsem.at[1, d], (t * 2 + c, s))
+        cp.start()
+        z_copies.append(cp)
+    for cp in z_copies:
+        cp.wait()
+    ghat[c, z] = (
+        (sc[z].astype(F32) + rc[1].astype(F32)) + (rc[2].astype(F32) + rc[3].astype(F32))
+    ).astype(BF)
+    f_copies = []
+    for d in range(1, 4):
+        t = (z + d) % 4
+        cp = remote(ghat.at[c, z], ghat.at[c, z], fsem.at[0, d], fsem.at[1, d], (t * 2 + c, s))
+        cp.start()
+        f_copies.append(cp)
+    for cp in f_copies:
+        cp.wait()
+    e_copy = remote(ghat.at[c], ghat.at[c], esem.at[0], esem.at[1], me.sibling)
+    e_copy.start()
+    for cp in x_third:
+        cp.wait()
+    extra[...] = (exl[5] + exl[6]) + (exl[7] + exl[8])
+
+    own_o.wait()
+    for d in range(1, 16):
+        p = (me.number + d) % 16
+        o_copy(p).wait_send()
+        remote(part(outs, p), part(outb, p), osem.at[0, p], osem.at[1, p], me.peer(p)).wait_recv()
+    load_out = pltpu.make_async_copy(outb, rowsv, lsem.at[0])
+    load_out.start()
+    load_out.wait()
+    gmoe[...] = hid[...]
+
+    @pl.loop(0, 4)
+    def _(plane):
+        fill_hits(ranks, plane, hits, cap)
+        r = pl.ds(pl.multiple_of(plane * block, block), block)
+        gmoe[...] += mm_tn(hits[...], rowsv[r, :])
+
+    block_out[...] = gmoe[...].astype(BF)
+
+    for t in range(4):
+        @pl.when(jnp.logical_not(mine_local & (s == t)))
+        def _():
+            owner_copy(t).wait_send()
+
+        @pl.when(mine_local & (s == t))
+        def _():
+            owner_local.wait()
+
+    for i in range(2):
+        for a in range(2):
+            own = (a == c) & (s == 2 * c + i)
+
+            @pl.when(jnp.logical_not(own))
+            def _():
+                remote(gx.at[0], eg.at[i, a], wsem.at[0, 0], wsem.at[1, i * 2 + a], me.sibling).wait_recv()
+
+    e_copy.wait()
+
+
+def params(number):
+    return pltpu.CompilerParams(collective_id=number, has_side_effects=True, vmem_limit_bytes=VMEM_LIMIT)
+
+
+def dma(*shape):
+    return pltpu.SemaphoreType.DMA(shape)
+
+
+def fast(tokens, routes, cotangent, gain_attn, w_qkv, w_proj, gain_moe, w_router, w_in, w_out):
+    count = tokens.shape[0]
+    images = count // SEQ
+    rows = images * SEQ_PAD
+    experts = w_router.shape[1]
+    cap = ((3 * count + experts - 1) // experts + 15) // 16 * 16
+    slots = experts * cap
+    vmem = pl.BlockSpec(memory_space=pltpu.VMEM)
+    hbm = pl.BlockSpec(memory_space=pl.ANY)
+    shape = jax.ShapeDtypeStruct
+
+    def padded(array, value=0):
+        array = array.reshape(images, SEQ, array.shape[1])
+        array = jnp.pad(array, ((0, 0), (0, SEQ_PAD - SEQ), (0, 0)), constant_values=value)
+        return array.reshape(rows, array.shape[2])
+
+    tok = padded(tokens)
+    cot = padded(cotangent)
+    rt = padded(routes, -1).T
+    quarter = w_qkv.shape[0]
+    small = jnp.concatenate([w_router, gain_attn[:, None], gain_moe[:, None]], axis=1)
+    small = jnp.pad(small, ((0, 0), (0, 128 - small.shape[1])))
+    dsh = jnp.concatenate([w_qkv, w_proj, small], axis=1)
+    wide = dsh.shape[1]
+
+    qkv, att, hid, lse, gate_t, ranks, aux, dense, xsend, gsend, cotr, wfull = pl.pallas_call(
+        functools.partial(kernel_a, cap),
+        out_shape=(
+            shape((rows, 3 * D), BF), shape((rows, D), BF), shape((rows, D), F32), shape((rows, 128), F32),
+            shape((16, rows), F32), shape((16, rows), jnp.int32), shape((32, D), F32), shape((D, wide), BF),
+            shape((slots, D), BF), shape((16, 8, 256), F32), shape((slots, D), BF), shape((2, 4, D, D), BF),
+        ),
+        in_specs=[vmem] * 4 + [hbm] * 2,
+        out_specs=(vmem,) * 10 + (hbm,) * 2,
+        scratch_shapes=[
+            pltpu.VMEM((slots, D), BF), pltpu.VMEM((rows, D), BF), pltpu.VMEM((4 * cap, rows), BF),
+            pltpu.VMEM((rows, rows), BF), dma(2, 4), dma(2, 4), dma(2, 16), dma(2, 2), dma(), dma(4), dma(2, 4), dma(),
+        ],
+        compiler_params=params(1),
+        name="forward",
+    )(tok, cot, rt, dsh, w_in, w_out)
+
+    outs, ginh, ginb, ggb, gw = pl.pallas_call(
+        functools.partial(kernel_e, cap),
+        out_shape=(
+            shape((slots, D), BF), shape((slots, D), BF), shape((slots, D), BF), shape((16, 8, 256), F32),
+            shape((2, 4, D, D), BF),
+        ),
+        in_specs=[hbm, vmem, hbm, hbm],
+        out_specs=(hbm, hbm, hbm, vmem, hbm),
+        scratch_shapes=[
+            pltpu.VMEM((4, D, D), BF), pltpu.VMEM((FF, D), BF), pltpu.VMEM((slots, D), BF), pltpu.VMEM((slots, D), BF),
+            pltpu.VMEM((16, 8, 256), F32), pltpu.VMEM((slots, FF), BF), pltpu.VMEM((slots, FF), BF),
+            pltpu.VMEM((4 * cap, D), F32), pltpu.VMEM((2, 4 * cap, D), BF),
+            pltpu.VMEM((16, 8, 256), F32), pltpu.VMEM((4 * cap, 128), F32),
+            dma(2, 16), dma(2, 16), dma(2, 16), dma(2, 16), dma(5), dma(5), dma(2),
+        ],
+        compiler_params=params(2),
+        name="experts",
+    )(xsend, gsend, cotr, wfull)
+
+    half = D // 8
+    block_out, gtok, ghat, extra, outb, eg = pl.pallas_call(
+        functools.partial(kernel_b, cap),
+        out_shape=(
+            shape((rows, D), BF), shape((rows, D), F32), shape((2, 4, half, D), BF), shape((32, D), F32),
+            shape((slots, D), BF), shape((2, 2, D, D), BF),
+        ),
+        in_specs=[vmem] * 11 + [hbm] * 3,
+        out_specs=(vmem,) * 4 + (hbm,) * 2,
+        scratch_shapes=[
+            pltpu.VMEM((slots, D), BF), pltpu.VMEM((4 * cap, rows), BF), pltpu.VMEM((rows, D), F32),
+            pltpu.VMEM((rows, D), BF), pltpu.VMEM((rows, D), BF), pltpu.VMEM((rows, D), BF),
+            pltpu.VMEM((rows, 3 * D), BF), pltpu.VMEM((4, 2, 4, half, D), BF), pltpu.VMEM((4, 4, half, D), BF),
+            pltpu.VMEM((4, 4, half, D), BF), pltpu.VMEM((4, half, D), BF), pltpu.VMEM((4, half, D), BF),
+            pltpu.VMEM((3, 32, D), F32), pltpu.VMEM((9, 32, D), F32), pltpu.VMEM((4, D, D), BF),
+            pltpu.VMEM((D, D), BF), pltpu.VMEM((16, rows), F32),
+            dma(2, 16), dma(2), dma(2, 4), dma(2, 4), dma(), dma(), dma(2, 4), dma(2, 4), dma(2, 4), dma(2, 4),
+            dma(2), dma(2, 7),
+        ],
+        compiler_params=params(3),
+        name="backward",
+    )(tok, cot, dense, aux, qkv, att, hid, lse, gate_t, ranks, ggb, ginb, outs, gw)
+
+    def unpadded(array):
+        return array.reshape(images, SEQ_PAD, D)[:, :SEQ].reshape(count, D)
+
+    part_dense = jnp.swapaxes(ghat, 1, 2).reshape(quarter, 4 * D).astype(F32)
+    mine = lax.dynamic_slice_in_dim(extra, lax.axis_index("shard") * quarter, quarter, axis=1)
+    dense_parts = (mine[16], part_dense[:, : 3 * D], part_dense[:, 3 * D :], mine[17], mine[:16].T)
+    eg = eg.astype(F32)
+    return unpadded(block_out), unpadded(gtok), dense_parts, (eg[:, 0], eg[:, 1])
+
+
+def local(
+    tokens, routes, cotangent, gain_attn, w_qkv, w_proj, gain_moe, w_router, w_in, w_out,
+    v_attn, v_moe, row_qkv, col_qkv, row_proj, col_proj, row_router, col_router, row_in, col_in, row_out, col_out,
+):
+    fits = (
+        lax.axis_size("shard") == 4 and lax.axis_size("expert") == 8 and w_in.shape[0] == 2 and tokens.shape[0] % SEQ == 0
+    )
+    block_out, grad_tokens, dense_parts, expert_parts = (fast if fits else general)(
+        tokens, routes, cotangent, gain_attn, w_qkv, w_proj, gain_moe, w_router, w_in, w_out
+    )
     part_g1, part_qkv, part_proj, part_g2, part_router = dense_parts
+    grad_first, grad_second = expert_parts
+    expert_count = part_router.shape[1]
     weight_g1 = gain_attn.astype(jnp.float32)
     weight_g2 = gain_moe.astype(jnp.float32)
-    weight_qkv = w_qkv.astype(jnp.float32)
-    weight_proj = w_proj.astype(jnp.float32)
-    weight_router = w_router.astype(jnp.float32)
+    dense = (
+        (part_qkv, w_qkv.astype(jnp.float32), row_qkv, col_qkv),
+        (part_proj, w_proj.astype(jnp.float32), row_proj, col_proj),
+        (part_router, w_router.astype(jnp.float32), row_router, col_router),
+    )
     weight_first = w_in.astype(jnp.float32)
     weight_second = w_out.astype(jnp.float32)
     v_attn_new = DECAY * v_attn + (1.0 - DECAY) * (part_g1 * part_g1 + EPS_SQUARE)
     v_moe_new = DECAY * v_moe + (1.0 - DECAY) * (part_g2 * part_g2 + EPS_SQUARE)
-    square_qkv = part_qkv * part_qkv + EPS_SQUARE
-    square_proj = part_proj * part_proj + EPS_SQUARE
-    square_router = part_router * part_router + EPS_SQUARE
-    row_qkv_new = DECAY * row_qkv + (1.0 - DECAY) * jnp.mean(square_qkv, axis=1)
-    row_proj_new = DECAY * row_proj + (1.0 - DECAY) * jnp.mean(square_proj, axis=1)
-    row_router_new = DECAY * row_router + (1.0 - DECAY) * jnp.mean(square_router, axis=1)
-    square_first = grad_first * grad_first + EPS_SQUARE
-    square_second = grad_second * grad_second + EPS_SQUARE
-    col_in_new = DECAY * col_in + (1.0 - DECAY) * jnp.mean(square_first, axis=1)
-    row_out_new = DECAY * row_out + (1.0 - DECAY) * jnp.mean(square_second, axis=2)
-    dense_local_sums = jnp.stack(
+    raw_g1 = part_g1 * lax.rsqrt(v_attn_new)
+    raw_g2 = part_g2 * lax.rsqrt(v_moe_new)
+    dense_rows, dense_sums = [], []
+    for grad, weight, row, col in dense:
+        square = grad * grad
+        row_new = DECAY * row + (1.0 - DECAY) * jnp.mean(square + EPS_SQUARE, axis=1)
+        dense_rows.append(row_new)
+        dense_sums.append(
+            (
+                jnp.sum(square + EPS_SQUARE, axis=0),
+                jnp.sum(square / row_new[:, None], axis=0),
+                jnp.stack([jnp.sum(row_new), jnp.sum(weight * weight)]),
+            )
+        )
+    square_first = grad_first * grad_first
+    square_second = grad_second * grad_second
+    col_in_new = DECAY * col_in + (1.0 - DECAY) * jnp.mean(square_first + EPS_SQUARE, axis=1)
+    row_out_new = DECAY * row_out + (1.0 - DECAY) * jnp.mean(square_second + EPS_SQUARE, axis=2)
+    gain_sums = jnp.stack(
         [
-            jnp.sum(row_qkv_new),
-            jnp.sum(row_proj_new),
-            jnp.sum(row_router_new),
+            jnp.sum(raw_g1 * raw_g1),
+            jnp.sum(raw_g2 * raw_g2),
             jnp.sum(weight_g1 * weight_g1),
             jnp.sum(weight_g2 * weight_g2),
-            jnp.sum(weight_qkv * weight_qkv),
-            jnp.sum(weight_proj * weight_proj),
-            jnp.sum(weight_router * weight_router),
         ]
     )
-    expert_local_sums = jnp.stack(
-        [
-            jnp.sum(weight_first * weight_first, axis=(1, 2)),
-            jnp.sum(row_out_new, axis=1),
-            jnp.sum(weight_second * weight_second, axis=(1, 2)),
-        ],
-        axis=1,
-    )
-    col_qkv_sum, col_proj_sum, col_router_sum, dense_sums, row_in_sum, col_out_sum, expert_sums = (
-        lax.psum(
-            (
-                jnp.sum(square_qkv, axis=0),
-                jnp.sum(square_proj, axis=0),
-                jnp.sum(square_router, axis=0),
-                dense_local_sums,
-                jnp.sum(square_first, axis=2),
-                jnp.sum(square_second, axis=1),
-                expert_local_sums,
-            ),
-            "shard",
-        )
-    )
-    col_qkv_new = DECAY * col_qkv + (1.0 - DECAY) * (col_qkv_sum / D)
-    col_proj_new = DECAY * col_proj + (1.0 - DECAY) * (col_proj_sum / D)
-    col_router_new = DECAY * col_router + (1.0 - DECAY) * (col_router_sum / D)
+    expert_sums = (
+        jnp.sum(square_first + EPS_SQUARE, axis=2),
+        jnp.sum(square_first / col_in_new[:, None, :], axis=2),
+        jnp.sum(square_second + EPS_SQUARE, axis=1),
+        jnp.sum(square_second / row_out_new[:, :, None], axis=1),
+        jnp.stack(
+            [
+                jnp.sum(weight_first * weight_first, axis=(1, 2)),
+                jnp.sum(row_out_new, axis=1),
+                jnp.sum(weight_second * weight_second, axis=(1, 2)),
+            ]
+        ),
+    )
+    expert_sums = lax.psum(expert_sums, "shard")
+    dense_sums, gain_sums = lax.psum((dense_sums, gain_sums), "shard")
+
+    def step(square_sum, weight_sum, size):
+        rms = jnp.sqrt(square_sum / size)
+        return rms, -RATE * jnp.sqrt(weight_sum / size) / jnp.maximum(CLIP, rms)
+
+    rms_g1, factor_g1 = step(gain_sums[0], gain_sums[2], D)
+    rms_g2, factor_g2 = step(gain_sums[1], gain_sums[3], D)
+    new_g1 = weight_g1 + factor_g1 * raw_g1
+    new_g2 = weight_g2 + factor_g2 * raw_g2
+    dense_new, dense_cols, dense_rms = [], [], [rms_g1, rms_g2]
+    for (grad, weight, _, col), row_new, (col_sum, ratio_sum, both) in zip(dense, dense_rows, dense_sums):
+        col_new = DECAY * col + (1.0 - DECAY) * (col_sum / D)
+        row_mean = both[0] / D
+        rms, factor = step(row_mean * jnp.sum(ratio_sum / col_new), both[1], grad.shape[1] * D)
+        raw = grad * lax.rsqrt(row_new[:, None] * col_new[None, :] / row_mean)
+        dense_new.append(weight + factor * raw)
+        dense_cols.append(col_new)
+        dense_rms.append(rms)
+    new_qkv, new_proj, new_router = dense_new
+    row_qkv_new, row_proj_new, row_router_new = dense_rows
+    col_qkv_new, col_proj_new, col_router_new = dense_cols
+    row_in_sum, ratio_in, col_out_sum, ratio_out, expert_scalars = expert_sums
     row_in_new = DECAY * row_in + (1.0 - DECAY) * (row_in_sum / FF)
     col_out_new = DECAY * col_out + (1.0 - DECAY) * (col_out_sum / FF)
-    raw_g1 = part_g1 * lax.rsqrt(v_attn_new)
-    raw_g2 = part_g2 * lax.rsqrt(v_moe_new)
-    raw_qkv = part_qkv * lax.rsqrt(
-        row_qkv_new[:, None] * col_qkv_new[None, :] / (dense_sums[0] / D)
-    )
-    raw_proj = part_proj * lax.rsqrt(
-        row_proj_new[:, None] * col_proj_new[None, :] / (dense_sums[1] / D)
-    )
-    raw_router = part_router * lax.rsqrt(
-        row_router_new[:, None] * col_router_new[None, :] / (dense_sums[2] / D)
-    )
-    raw_first = grad_first * lax.rsqrt(
-        row_in_new[:, :, None]
-        * col_in_new[:, None, :]
-        / jnp.mean(row_in_new, axis=1)[:, None, None]
-    )
-    raw_second = grad_second * lax.rsqrt(
-        row_out_new[:, :, None] * col_out_new[:, None, :] / (expert_sums[:, 1] / FF)[:, None, None]
-    )
-    dense_square, expert_square = lax.psum(
-        (
-            jnp.stack(
-                [
-                    jnp.sum(raw_g1 * raw_g1),
-                    jnp.sum(raw_g2 * raw_g2),
-                    jnp.sum(raw_qkv * raw_qkv),
-                    jnp.sum(raw_proj * raw_proj),
-                    jnp.sum(raw_router * raw_router),
-                ]
-            ),
-            jnp.stack(
-                [
-                    jnp.sum(raw_first * raw_first, axis=(1, 2)),
-                    jnp.sum(raw_second * raw_second, axis=(1, 2)),
-                ],
-                axis=1,
-            ),
-        ),
-        "shard",
-    )
-    dense_sizes = jnp.array([D, D, 3 * D * D, D * D, D * expert_count], jnp.float32)
-    dense_rms = jnp.sqrt(dense_square / dense_sizes)
-    expert_rms = jnp.sqrt(expert_square / float(D * FF))
-    dense_weight_rms = jnp.sqrt(dense_sums[3:] / dense_sizes)
-    dense_factor = -RATE * dense_weight_rms / jnp.maximum(CLIP, dense_rms)
-    expert_weight_rms = jnp.sqrt(
-        jnp.stack([expert_sums[:, 0], expert_sums[:, 2]], axis=1) / float(D * FF)
-    )
-    expert_factor = -RATE * expert_weight_rms / jnp.maximum(CLIP, expert_rms)
-    new_g1 = weight_g1 + dense_factor[0] * raw_g1
-    new_g2 = weight_g2 + dense_factor[1] * raw_g2
-    new_qkv = weight_qkv + dense_factor[2] * raw_qkv
-    new_proj = weight_proj + dense_factor[3] * raw_proj
-    new_router = weight_router + dense_factor[4] * raw_router
-    new_first = weight_first + expert_factor[:, 0][:, None, None] * raw_first
-    new_second = weight_second + expert_factor[:, 1][:, None, None] * raw_second
+    mean_in = jnp.mean(row_in_new, axis=1)
+    mean_out = expert_scalars[1] / FF
+    rms_first, factor_first = step(mean_in * jnp.sum(ratio_in / row_in_new, axis=1), expert_scalars[0], D * FF)
+    rms_second, factor_second = step(mean_out * jnp.sum(ratio_out / col_out_new, axis=1), expert_scalars[2], D * FF)
+    new_first = weight_first + factor_first[:, None, None] * grad_first * lax.rsqrt(
+        row_in_new[:, :, None] * col_in_new[:, None, :] / mean_in[:, None, None]
+    )
+    new_second = weight_second + factor_second[:, None, None] * grad_second * lax.rsqrt(
+        row_out_new[:, :, None] * col_out_new[:, None, :] / mean_out[:, None, None]
+    )
     return (
         block_out,
         grad_tokens,
-        dense_rms,
-        expert_rms,
+        jnp.stack(dense_rms),
+        jnp.stack([rms_first, rms_second], axis=1),
         part_g1,
         new_g1,
         v_attn_new,

time: 1200 us -> 677 us (0.56)
  waiting for transfers between devices: 597 us -> 0 us
  Pallas kernels: 0 us -> 555 us
  matrix products: 210 us -> 0 us
  local copies, waits for them, and re-layouts: 164 us -> 26.3 us
  blocking collectives: 80.2 us -> 19.8 us
  other arithmetic: 104 us -> 57.2 us
  starting transfers between devices: 19.9 us -> 0 us
    pallas_call x0 -> x3, Pallas kernels: none -> 555 us  [the longest x1 231 us: fast(): pl.pallas_call(functools.partial(kernel_b, cap), out_shape=(shape((rows,...]
    reduce_scatter x4 -> x0, waiting for transfers between devices: 401 us -> none  [the longest x1 171 us: local(): lax.psum_scatter(grad_first, 'shard', scatter_dimension=2, tiled=True)]
    dot_general x20 -> x0, matrix products: 208 us -> none  [the longest x1 35.3 us: local(): jnp.einsum('sekd,efd->sekf', grad_recv, second_full, preferred_element_ty...]
    all_to_all x4 -> x0, waiting for transfers between devices: 128 us -> none  [the longest x1 51.6 us: local(): lax.all_to_all(grad_rows, 'expert', split_axis=0, concat_axis=0, tiled=True)]
    all_gather x4 -> x0, waiting for transfers between devices: 64.4 us -> none  [the longest x1 44.4 us: local(): lax.all_gather(w_out, 'shard', axis=1, tiled=True)]
    gather x4 -> x0, local copies, waits for them, and re-layouts: 37.5 us -> none  [the longest x1 10.4 us: local(): grad_back.reshape(expert_count * capacity, D)[slot_dest]]
    psum x3 -> x1, blocking collectives: 51.4 us -> 19.8 us  [local(): dense_sums, gain_sums = lax.psum((dense_sums, gain_sums), 'shard')]
    convert_element_type x7 -> x1, local copies, waits for them, and re-layouts: 32.6 us -> 1.52 us  [fast(): part_dense = jnp.swapaxes(ghat, 1, 2).reshape(quarter, 4 * D).astype(F32)]
  transfers between devices with their start and end apart: 14 -> 0, of which waited for: 8 -> 0; matrix products, arithmetic and copies ran while one was open for 33% -> 0% of each run, Pallas kernels for 0% -> 0%
where the time goes in v1:
time: 677 us; the launch traced here: 669 us
  Pallas kernels  555 us (82%)
  other arithmetic  57.2 us (8%)
  local copies, waits for them, and re-layouts  26.3 us (4%)
  blocking collectives  19.8 us (3%)
  between operations  10.5 us (2%)
    pallas_call x1, Pallas kernels, fast(): pl.pallas_call(functools.partial(kernel_b, cap), out_shape=(shape((rows,...  231 us
    pallas_call x1, Pallas kernels, fast(): pl.pallas_call(functools.partial(kernel_e, cap), out_shape=(shape((slots,...  173 us
    pallas_call x1, Pallas kernels, fast(): pl.pallas_call(functools.partial(kernel_a, cap), out_shape=(shape((rows,...  151 us
    psum x1, blocking collectives, local(): dense_sums, gain_sums = lax.psum((dense_sums, gain_sums), 'shard')  19.8 us

profile of v1, /device:TPU:0, one launch (start us, length us, event | category | flops | bytes accessed | tf_op | source)
XLA Modules:
  0.0 668.7 jit_solution(2754655421733811840)
XLA Ops:
  0.7 1.6 reshape.252
  3.5 1.7 reshape.254
  8.4 151.0 %forward.1 = (bf16[896,2304]{1,0:T(8,128)(2,1)}, bf16[896,768]{1,0:T(8,128)(2,1)}, f32[896,768]{1,0:T(8,128)}, f32[896,128]{1,0:T(8,128)}, f32[16,896]{1,0:T(8,1...) custom-call(bf16[896,768]{1,0:T(8,128)(2,1)} %bitcast.71, ...), custom_call_target="tpu_custom_call" | custom-call | tf_op jit(solution)/shard_map/forward/pallas_call | solution.py:949
  159.5 172.9 %experts.1 = (bf16[2560,768]{1,0:T(8,128)(2,1)}, bf16[2560,768]{1,0:T(8,128)(2,1)}, bf16[2560,768]{1,0:T(8,128)(2,1)}, f32[16,8,256]{2,1,0:T(8,128)}, bf16[2,4,768,768]{3,2,1,0:T(8,128)(2,1)}) custom-call(bf16[2560,768]{1,0:T(8,128)(2,1)} %get-tuple-element.59.xsend, f32[16,8,256]{2,1,0:T(8,128)} %get-tuple-element.60.gsend, ...), custom_call_target="tpu_custom_call" | custom-call | tf_op jit(solution)/shard_map/experts/pallas_call | solution.py:966
  332.4 231.0 %backward.1 = (bf16[896,768]{1,0:T(8,128)(2,1)}, f32[896,768]{1,0:T(8,128)}, bf16[2,4,96,768]{3,2,1,0:T(8,128)(2,1)}, f32[32,768]{1,0:T(8,128)}, bf16[2560,768]{...) custom-call(bf16[896,768]{1,0:T(8,128)(2,1)} %bitcast.72, bf16[896,768]{1,0:T(8,128)(2,1)} %bitcast.74, ...), custom_call_target="tpu_custom_call" | custom-call | tf_op jit(solution)/shard_map/backward/pallas_call | solution.py:986
  563.5 1.4 slice.88
  564.8 1.3 reshape.259
  566.2 1.9 slice.89
  568.1 1.7 reshape.261
  573.6 3.2 pad_maximum_fusion.3
  577.8 1.5 convert_bitcast_fusion
  579.3 1.5 copy.62
  582.7 1.9 pad_maximum_fusion.4
  587.9 1.9 pad_maximum_fusion.5
  591.2 1.9 pad_maximum_fusion.6
  596.1 2.5 add_reduce_fusion
  602.7 19.8 %all-reduce.4 = (f32[4]{0:T(128)}, f32[2]{0:T(128)}, f32[2304]{0:T(1024)}, f32[2304]{0:T(1024)}, f32[2]{0:T(128)}, /*index=5*/f32[768]{0:T(1024)}, f32[768]{0:T(...) all-reduce(f32[4]{0:T(128)} %pad_maximum_fusion.3, ...), channel_id=1, replica_groups=mesh['expert'=8,'shard'=4] {'shard'}, use_global_device_ids=true, to_apply=%region_4.5 | all-reduce | flops 12336 | bytes 98688 | tf_op jit(solution)/shard_map/psum | solution.py:1082
  622.5 1.4 fusion.22
  625.3 1.3 fusion.21
  627.2 1.9 divide_reduce_fusion.5
  631.8 1.9 divide_reduce_fusion.8
  634.5 1.3 fusion.19
  636.4 1.8 divide_reduce_fusion.9
  639.5 1.4 divide_reduce_fusion.6
  641.6 1.5 fusion.13
  643.1 1.4 bitcast_divide_fusion
  645.1 1.3 copy.64
  651.1 3.2 convert_add_fusion.2
  655.0 2.1 convert_add_fusion.3
  657.7 1.4 convert_add_fusion.4
  659.2 4.9 convert_add_fusion.1
  665.4 2.8 convert_add_fusion
  (116 shorter events, 29.9 us)
Async XLA Ops:
  3.4 2.9 copy-start.22
  3.5 3.7 copy-start.32
  3.5 3.7 copy-start.31
  3.5 3.7 copy-start.11
  3.5 3.9 copy-start.6
  3.5 3.9 copy-start.8
  568.0 4.4 copy-start.26
  568.1 4.3 copy-start.27
  571.8 1.7 copy-start.20
  579.3 14.4 %slice-start.2 = ((s8[4718592]{0:T(1024)(128)(4,1)}), s8[4194304]{0:T(1024)(128)(4,1)S(1)}, s32[]{:S(2)}) async-start(s8[4718592]{0:T(1024)(128)(4,1)} %bitcast.78), calls=%async_computation.2 | async-start | bytes 8388608
  580.8 12.9 %slice-start.3 = ((s8[4718592]{0:T(1024)(128)(4,1)}), s8[524288]{0:T(1024)(128)(4,1)S(1)}, s32[]{:S(2)}) async-start(s8[4718592]{0:T(1024)(128)(4,1)} %bitcast.78), calls=%async_computation.3 | async-start | bytes 1048576
  581.3 4.2 copy-start.9
  581.6 12.1 %copy-start.5 = (f32[192,2304]{1,0:T(8,128)}, f32[192,2304]{1,0:T(8,128)S(1)}, u32[]{:S(2)}) copy-start(f32[192,2304]{1,0:T(8,128)S(1)} %get-tuple-element.215) | copy-start | bytes 5308420
  581.6 5.7 copy-start.29
  581.6 5.7 copy-start.30
  581.6 9.0 %copy-start.12 = (bf16[192,16]{0,1:T(8,128)(2,1)S(1)}, bf16[192,16]{0,1:T(8,128)(2,1)}, u32[]{:S(2)}) copy-start(bf16[192,16]{0,1:T(8,128)(2,1)} %param.29) | copy-start | bytes 18436
  582.7 11.0 %copy-start.17 = (f32[192]{0:T(256)}, f32[192]{0:T(256)S(1)}, u32[]{:S(2)}) copy-start(f32[192]{0:T(256)S(1)} %get-tuple-element.213) | copy-start | bytes 2308
  587.1 70.6 %copy-start.10 = (f32[192,16]{0,1:T(8,128)}, f32[192,16]{0,1:T(8,128)S(1)}, u32[]{:S(2)}) copy-start(f32[192,16]{0,1:T(8,128)S(1)} %get-tuple-element.207) | copy-start | bytes 36868
  587.2 6.5 copy-start.7
  587.9 5.8 copy-start.18
  587.9 5.8 copy-start.21
  595.9 2.7 copy-start
  595.9 3.9 copy-start.1
  596.0 3.7 copy-start.13
  596.0 3.7 copy-start.15
  596.1 3.7 copy-start.3
  659.1 5.9 slice-start
  659.1 5.9 slice-start.1
  659.1 6.2 copy-start.4
  659.1 6.2 copy-start.14
  659.2 6.2 copy-start.16
  659.2 6.2 copy-start.25
  (5 other events, 5.7 us)

commit v2 on v1

--- a/solution.py
+++ b/solution.py
@@ -286,6 +286,69 @@
         return [(self.z * 2 + self.core, (self.shard + d) % 4) for d in range(1, 4)]
 
 
+class Quarters:
+    def __init__(self, me, source, place, send, recv, local, pass_on):
+        self.me, self.source, self.place = me, source, place
+        self.sems = send, recv, local, pass_on
+
+    def outgoing(self, act):
+        me, (send, recv, local, _) = self.me, self.sems
+        core = me.shard % 2
+        for i in range(2):
+            chip = 2 * me.core + i
+            own = (core == me.core) & (chip == me.shard)
+
+            @pl.when(jnp.logical_not(own))
+            def _():
+                act(
+                    remote(
+                        self.source.at[i], self.place(me.shard), send.at[i], recv.at[me.shard // 2],
+                        (me.z * 2 + core, chip),
+                    )
+                )
+
+            @pl.when(own)
+            def _():
+                act(pltpu.make_async_copy(self.source.at[i], self.place(me.shard), local))
+
+    def start(self):
+        self.outgoing(lambda cp: cp.start())
+
+    def handed_on(self, q):
+        pass_on = self.sems[3]
+        return remote(self.place(q), self.place(q), pass_on.at[0, q // 2], pass_on.at[1, q // 2], self.me.sibling)
+
+    def forward(self):
+        me, (send, recv, local, _) = self.me, self.sems
+        for n in range(2):
+            q = 2 * n + me.core
+            here = (me.shard // 2 == me.core) & (me.shard == q)
+
+            @pl.when(jnp.logical_not(here))
+            def _():
+                remote(self.source.at[0], self.place(q), send.at[0], recv.at[n], me.sibling).wait_recv()
+
+            @pl.when(here)
+            def _():
+                pltpu.make_async_copy(self.source.at[0], self.place(q), local).wait()
+
+            self.handed_on(q).start()
+
+    def finish(self):
+        me, (send, recv, _, _) = self.me, self.sems
+        core = me.shard % 2
+        for i in range(2):
+            chip = 2 * me.core + i
+
+            @pl.when(jnp.logical_not((core == me.core) & (chip == me.shard)))
+            def _():
+                remote(self.source.at[i], self.place(me.shard), send.at[i], recv.at[0], me.sibling).wait_send()
+
+        for n in range(2):
+            self.handed_on(2 * n + me.core).wait_send()
+            self.handed_on(2 * n + 1 - me.core).wait_recv()
+
+
 def split3(rows):
     high = rows.astype(BF)
     rest = rows - high.astype(F32)
@@ -316,7 +379,7 @@
 
 
 def kernel_a(
-    cap, tok, cot, rt, dsh, w1, w2,
+    cap, tok, cot, rt, dsh, w1,
     qkv, att, hid, lse, gate_t, ranks, aux, dense, xsend, gsend, cotr, wfull,
     csend, low, hits, tri, dsem, dfsem, csem, wsem, wloc, wrecv, fsem, osem,
 ):
@@ -382,25 +445,11 @@
         cp.start()
         forwards.append(cp)
 
-    def quarters(act, own=True):
-        for i in range(2):
-            for a, w in ((0, w1), (1, w2)):
-                target = 2 * c + i
-                self_target = (a == c) & (target == s)
-
-                @pl.when(jnp.logical_not(self_target))
-                def _():
-                    act(remote(w.at[i], wfull.at[a, s], wsem.at[i, a], wrecv.at[s], (z * 2 + a, target)), False)
-
-                if own:
-
-                    @pl.when(self_target)
-                    def _():
-                        act(pltpu.make_async_copy(w.at[i], wfull.at[a, s], wloc), True)
+    in_quarters = Quarters(me, w1, lambda q: wfull.at[q], wsem, wrecv, wloc, fsem)
 
     for cp in forwards:
         cp.wait()
-    quarters(lambda cp, local_copy: cp.start())
+    in_quarters.start()
 
     flat = jnp.transpose(dense[:, 3072:3200].astype(F32))
     aux[...] = flat[0:32, :]
@@ -441,23 +490,8 @@
             row = mm_nt(three_rows(gate_t[pl.ds(plane * 4 + k, 1), :]), hits[k * cap : (k + 1) * cap, :])
             gsend[plane * 4 + k, :, 0:cap] = jnp.broadcast_to(jnp.sum(row, axis=0, keepdims=True), (8, cap))
 
-    source_core = s // 2
-    for t in range(4):
-        arrives_here = (source_core == c) & (s == t)
-
-        @pl.when(jnp.logical_not(arrives_here))
-        def _():
-            remote(w1.at[0], wfull.at[c, t], wsem.at[0, 0], wrecv.at[t], me.sibling).wait_recv()
-
-        @pl.when(arrives_here)
-        def _():
-            pltpu.make_async_copy(w1.at[0], wfull.at[c, t], wloc).wait()
-
-        remote(wfull.at[c, t], wfull.at[c, t], fsem.at[0, t], fsem.at[1, t], me.sibling).start()
-    quarters(lambda cp, local_copy: cp.wait_send(), own=False)
-    for t in range(4):
-        remote(wfull.at[c, t], wfull.at[c, t], fsem.at[0, t], fsem.at[1, t], me.sibling).wait_send()
-        remote(wfull.at[1 - c, t], wfull.at[1 - c, t], fsem.at[0, t], fsem.at[1, t], me.sibling).wait_recv()
+    in_quarters.forward()
+    in_quarters.finish()
     for d in range(1, 16):
         p = (me.number + d) % 16
         cot_copy(p).wait_send()
@@ -495,14 +529,14 @@
 
 
 def kernel_e(
-    cap, xsend, gsend, cotr, wfull,
+    cap, xsend, gsend, cotr, wfull, w2,
     outs, ginh, ginb, ggb, gw,
     w1v, w2v, xr, gcot, gater, act, gpre, acc, stage, ggs, gcol,
-    xsem, gsem, rsem, ggsem, lsem, wlsem, stsem,
+    xsem, gsem, rsem, ggsem, lsem, wlsem, stsem, wsem, wrecv, wloc, fsem,
 ):
     me = Place()
     z, c, s = me.z, me.core, me.shard
-    greet(me.peers())
+    greet(me.peers() + [(z * 2 + 1 - c, t) for t in range(4)])
     block = 4 * cap
 
     def part(ref, p):
@@ -527,9 +561,11 @@
     ]
     own_r = pltpu.make_async_copy(part(ginh, me.number), part(ginb, me.number), lsem.at[3])
     own_g = pltpu.make_async_copy(ggs.at[me.number], ggb.at[me.number], lsem.at[4])
-    w_copies = [pltpu.make_async_copy(wfull.at[0], w1v, wlsem.at[0])] + [
-        pltpu.make_async_copy(wfull.at[1, f], w2v.at[pl.ds(f * D, D)], wlsem.at[1 + f]) for f in range(4)
-    ]
+    w_copies = [pltpu.make_async_copy(wfull, w1v, wlsem.at[0])]
+    out_quarters = Quarters(
+        me, w2, lambda q: w2v.at[pl.ds(pl.multiple_of(q * D, D), D)], wsem, wrecv, wloc, fsem
+    )
+    out_quarters.start()
     for d in range(1, 16):
         g_copy((me.number + d) % 16).start()
     for cp in local_copies + w_copies:
@@ -563,8 +599,7 @@
             stsem.at[which],
         )
 
-    @pl.loop(0, 4)
-    def _(step):
+    def first_half(step):
         plane = me.plane(step)
         recv_block(plane)
         r = pl.ds(pl.multiple_of(plane * block, block), block)
@@ -581,6 +616,19 @@
                 slope = half + (0.5 * pre) * (1.0 - t * t) * (GELU_A + 3.0 * GELU_A * GELU_B * square)
                 gpre[r, cols] = slope.astype(BF)
 
+    first_half(0)
+    first_half(1)
+    out_quarters.forward()
+    out_quarters.finish()
+
+    @pl.loop(0, 4)
+    def _(step):
+        @pl.when(step > 1)
+        def _():
+            first_half(step)
+
+        plane = me.plane(step)
+        r = pl.ds(pl.multiple_of(plane * block, block), block)
         acc[...] = mm(act[r, :], w2v[...])
 
         for k in range(4):
@@ -658,13 +706,14 @@
         cp.wait()
 
 
-def attention_backward(qkv, gatt, lse, gqkv, images):
+def attention_backward(qkv, gatt, lse, gqkv, images, group):
     first = lax.broadcasted_iota(jnp.int32, (SEQ_PAD, 128), 1) < HEAD
     lane = lax.broadcasted_iota(jnp.int32, (SEQ_PAD, 128), 1)
     real = lax.broadcasted_iota(jnp.int32, (SEQ_PAD, SEQ_PAD), 1) < SEQ
 
-    @pl.loop(0, HEADS // 2)
-    def _(pair):
+    @pl.loop(0, 2)
+    def _(near):
+        pair = 2 * group + near
         for i in range(images):
             r = slice(i * SEQ_PAD, (i + 1) * SEQ_PAD)
             cols = [pl.ds(pl.multiple_of(part * D + pair * 128, 128), 128) for part in range(3)]
@@ -684,7 +733,8 @@
                 grad_scores = (probs * (grad_probs - delta)).astype(BF)
                 parts.append((mm(grad_scores, k) * 0.125, mm_tn(grad_scores, q) * 0.125, mm_tn(low, g)))
             for part in range(3):
-                gqkv[r, cols[part]] = jnp.where(first, parts[0][part], parts[1][part]).astype(BF)
+                place = pl.ds(pl.multiple_of(group * D + part * 256 + near * 128, 128), 128)
+                gqkv[r, place] = jnp.where(first, parts[0][part], parts[1][part]).astype(BF)
 
 
 def kernel_b(
@@ -698,7 +748,7 @@
     rows = tok.shape[0]
     images = rows // SEQ_PAD
     block = 4 * cap
-    half = D // 8
+    quarter, wide, deep = D // 4, D // 2, D // 16
     greet(me.peers() + [(z * 2 + 1 - c, t) for t in range(4)])
 
     def part(ref, p):
@@ -714,8 +764,17 @@
         cp.start()
     own_o = pltpu.make_async_copy(part(outs, me.number), part(outb, me.number), lsem.at[1])
     own_o.start()
-    for d in range(1, 16):
-        o_copy((me.number + d) % 16).start()
+
+    def send_outs(step):
+        for k in range(4):
+            p = me.plane(step) * 4 + k
+
+            @pl.when(p != me.number)
+            def _():
+                o_copy(p).start()
+
+    for step in (3, 2, 1, 0):
+        send_outs(step)
 
     load_in.wait()
     gmoe[...] = jnp.zeros_like(gmoe)
@@ -766,9 +825,78 @@
     def put(group, value):
         for t in range(4):
             for h in range(2):
-                gd[t, h, group] = value[t * 2 * half + h * half : t * 2 * half + (h + 1) * half, :].astype(BF)
+                gd[group, t, h] = value[t * quarter : (t + 1) * quarter, h * wide : (h + 1) * wide].astype(BF)
+
+    def stage_a(g):
+        return [
+            remote(gd.at[g, t, 1 - c], ra.at[g, t], asem.at[0, g, t], asem.at[1, g, t], me.sibling) for t in range(4)
+        ]
+
+    def stage_b(g):
+        return [
+            remote(
+                gd.at[g, (s + d) % 4, c], rb.at[g, d], bsem.at[0, g, d], bsem.at[1, g, d], (z * 2 + c, (s + d) % 4)
+            )
+            for d in range(1, 4)
+        ]
+
+    def stage_c(g):
+        return [
+            remote(
+                sc.at[g, pl.ds(pl.multiple_of((z + d) % 4 * deep, deep), deep)], rc.at[g, d],
+                zsem.at[0, g, d], zsem.at[1, g, d], ((z + d) % 4 * 2 + c, s),
+            )
+            for d in range(1, 4)
+        ]
+
+    my_rows = pl.ds(pl.multiple_of(z * deep, deep), deep)
+
+    def stage_d(g):
+        return [
+            remote(
+                ghat.at[g, c, my_rows], ghat.at[g, c, my_rows],
+                fsem.at[0, g, d], fsem.at[1, g, d], ((z + d) % 4 * 2 + c, s),
+            )
+            for d in range(1, 4)
+        ]
+
+    def stage_e(g):
+        return [remote(ghat.at[g, c], ghat.at[g, c], esem.at[0, g], esem.at[1, g], me.sibling)]
+
+    def start(copies):
+        for cp in copies:
+            cp.start()
+
+    def finish(copies):
+        for cp in copies:
+            cp.wait()
+
+    def to_b(g):
+        finish(stage_a(g))
+        for t in range(4):
+            gd[g, t, c] = (gd[g, t, c].astype(F32) + ra[g, t].astype(F32)).astype(BF)
+        start(stage_b(g))
+
+    def to_c(g):
+        finish(stage_b(g))
+        sc[g] = (
+            (gd[g, s, c].astype(F32) + rb[g, 1].astype(F32)) + (rb[g, 2].astype(F32) + rb[g, 3].astype(F32))
+        ).astype(BF)
+        start(stage_c(g))
+
+    def to_d(g):
+        finish(stage_c(g))
+        ghat[g, c, my_rows, :] = (
+            (sc[g, my_rows, :].astype(F32) + rc[g, 1].astype(F32)) + (rc[g, 2].astype(F32) + rc[g, 3].astype(F32))
+        ).astype(BF)
+        start(stage_d(g))
+
+    def to_e(g):
+        finish(stage_d(g))
+        start(stage_e(g))
 
     put(3, mm_tn(att[...], glow[...]))
+    start(stage_a(3))
     gatt[...] = mm_nt(glow[...], dense[:, 2304:3072]).astype(BF)
 
     def owner_copy(t):
@@ -778,11 +906,11 @@
 
     mine_local = s // 2 == c
     owner_local = pltpu.make_async_copy(gx.at[s], eg.at[s % 2, c], wlocal)
-    for t in range(4):
+    def to_owner(t):
         load = pltpu.make_async_copy(gw.at[c, t], own_w, wload)
         load.start()
         load.wait()
-        swap[t].wait()
+        remote(gw.at[1 - c, t], gx.at[t], wxsem.at[0, t], wxsem.at[1, t], me.sibling).wait()
         gx[t] = (gx[t].astype(F32) + own_w[...].astype(F32)).astype(BF)
 
         @pl.when(jnp.logical_not(mine_local & (s == t)))
@@ -793,16 +921,22 @@
         def _():
             owner_local.start()
 
-    attention_backward(qkv, gatt, lse, gqkv, images)
-
-    for group in range(3):
-        put(group, mm_tn(low[...], gqkv[:, group * D : (group + 1) * D]))
-
-    a_copies = [remote(gd.at[t, 1 - c], ra.at[t], asem.at[0, t], asem.at[1, t], me.sibling) for t in range(4)]
-    for cp in a_copies:
-        cp.start()
-
-    gmoe[...] = mm_nt(gqkv[...], dense[:, 0:2304])
+    for d in (1, 2, 3, 0):
+        to_owner((s + d) % 4)
+    to_b(3)
+    for g in range(3):
+        attention_backward(qkv, gatt, lse, gqkv, images, g)
+        put(g, mm_tn(low[...], gqkv[:, g * D : (g + 1) * D]))
+        start(stage_a(g))
+        partial = [
+            mm_nt(gqkv[:, g * D + 256 * n : g * D + 256 * (n + 1)], dense[:, n * D + g * 256 : n * D + (g + 1) * 256])
+            for n in range(3)
+        ]
+        if g == 0:
+            gmoe[...] = (partial[0] + partial[1]) + partial[2]
+        else:
+            gmoe[...] += (partial[0] + partial[1]) + partial[2]
+            to_b(g - 1)
 
     @pl.loop(0, images)
     def _(i):
@@ -815,65 +949,34 @@
         )
         exs[0, 16:17, :] += jnp.sum(w * hat, axis=0, keepdims=True)
 
+    to_b(2)
     x_first = remote(exs.at[0], exl.at[0], xsem.at[0, 0], xsem.at[1, 0], me.sibling)
     x_first.start()
-    b_copies = []
-    for d in range(1, 4):
-        t = (s + d) % 4
-        b_copies.append(remote(gd.at[t, c], rb.at[d], bsem.at[0, d], bsem.at[1, d], (z * 2 + c, t)))
-    for t in range(4):
-        a_copies[t].wait()
-        gd[t, c] = (gd[t, c].astype(F32) + ra[t].astype(F32)).astype(BF)
-    for cp in b_copies:
-        cp.start()
+    to_c(3)
     x_first.wait()
     exs[1] = exs[0] + exl[0]
     exl[1 + s] = exs[1]
     x_second = [
         remote(exs.at[1], exl.at[1 + s], xsem.at[0, d], xsem.at[1, d], (z * 2 + c, (s + d) % 4)) for d in range(1, 4)
     ]
-    for cp in x_second:
-        cp.start()
-    for cp in x_second:
-        cp.wait()
+    start(x_second)
+    to_c(0)
+    to_c(1)
+    to_c(2)
+    finish(x_second)
     exs[2] = (exl[1] + exl[2]) + (exl[3] + exl[4])
     exl[5 + z] = exs[2]
     x_third = [
         remote(exs.at[2], exl.at[5 + z], xsem.at[0, 3 + d], xsem.at[1, 3 + d], ((z + d) % 4 * 2 + c, s))
         for d in range(1, 4)
     ]
-    for cp in x_third:
-        cp.start()
-    for cp in b_copies:
-        cp.wait()
-    for g in range(4):
-        sc[g] = (
-            (gd[s, c, g].astype(F32) + rb[1, g].astype(F32)) + (rb[2, g].astype(F32) + rb[3, g].astype(F32))
-        ).astype(BF)
-    z_copies = []
-    for d in range(1, 4):
-        t = (z + d) % 4
-        cp = remote(sc.at[t], rc.at[d], zsem.at[0, d], zsem.at[1, d], (t * 2 + c, s))
-        cp.start()
-        z_copies.append(cp)
-    for cp in z_copies:
-        cp.wait()
-    ghat[c, z] = (
-        (sc[z].astype(F32) + rc[1].astype(F32)) + (rc[2].astype(F32) + rc[3].astype(F32))
-    ).astype(BF)
-    f_copies = []
-    for d in range(1, 4):
-        t = (z + d) % 4
-        cp = remote(ghat.at[c, z], ghat.at[c, z], fsem.at[0, d], fsem.at[1, d], (t * 2 + c, s))
-        cp.start()
-        f_copies.append(cp)
-    for cp in f_copies:
-        cp.wait()
-    e_copy = remote(ghat.at[c], ghat.at[c], esem.at[0], esem.at[1], me.sibling)
-    e_copy.start()
-    for cp in x_third:
-        cp.wait()
+    start(x_third)
+    for g in (3, 0, 1, 2):
+        to_d(g)
+    finish(x_third)
     extra[...] = (exl[5] + exl[6]) + (exl[7] + exl[8])
+    for g in (3, 0, 1, 2):
+        to_e(g)
 
     own_o.wait()
     for d in range(1, 16):
@@ -910,7 +1013,254 @@
             def _():
                 remote(gx.at[0], eg.at[i, a], wsem.at[0, 0], wsem.at[1, i * 2 + a], me.sibling).wait_recv()
 
-    e_copy.wait()
+    for g in range(4):
+        finish(stage_e(g))
+
+
+def lane_sums(values, count):
+    lane = lax.broadcasted_iota(jnp.int32, (1, count), 1)
+    out = jnp.zeros((1, count), F32)
+    for n, value in enumerate(values):
+        out = jnp.where(lane == n, value, out)
+    return out
+
+
+def total(values):
+    return jnp.sum(jnp.sum(values, axis=1, keepdims=True), axis=0, keepdims=True)
+
+
+def set_columns(ref, columns):
+    lane = lax.broadcasted_iota(jnp.int32, ref.shape, 1)
+    out = jnp.zeros(ref.shape, F32)
+    for n, column in enumerate(columns):
+        out = jnp.where(lane == n, column, out)
+    ref[...] = out
+
+
+def pick(row, n):
+    lane = lax.broadcasted_iota(jnp.int32, row.shape, 1)
+    return jnp.sum(jnp.where(lane == n, row, 0.0), axis=1, keepdims=True)
+
+
+def mean_square(square_sum, weight_sum, size):
+    rms = jnp.sqrt(square_sum * (1.0 / size))
+    return rms, -RATE * jnp.sqrt(weight_sum * (1.0 / size)) / jnp.maximum(CLIP, rms)
+
+
+def kernel_s(
+    eg, ghat, extra, w1, w2, dsh, gains, moments, rows3, row_router, v_gain,
+    mine_new, v_new, rows3_new, row_router_new, moments_new, sums, sums_r,
+    egv, tall, turned, stats, landed, stats_r, landed_r, dgrad,
+    isem, xsem, rsem,
+):
+    me = Place()
+    z, c, s = me.z, me.core, me.shard
+    quarter = dsh.shape[0]
+    load = pltpu.make_async_copy(eg, egv, isem)
+    load.start()
+    greet(me.mates())
+
+    read_dense(ghat, dgrad)
+    mine = jnp.zeros((32, quarter), F32)
+    for t in range(4):
+        mine = mine + jnp.where(s == t, extra[:, t * quarter : (t + 1) * quarter], 0.0)
+    mine_new[...] = mine
+    router = mine[0:16, :]
+    gain = mine[16:18, :]
+    v = DECAY * v_gain[...] + (1.0 - DECAY) * (gain * gain + EPS_SQUARE)
+    v_new[...] = v
+    raw_gain = gain * lax.rsqrt(v)
+    gain_weight = gains[...].astype(F32)
+    gain_square = jnp.sum(raw_gain * raw_gain, axis=1, keepdims=True)
+    gain_size = jnp.sum(gain_weight * gain_weight, axis=1, keepdims=True)
+    router_square = router * router
+    router_row = DECAY * row_router[...] + (1.0 - DECAY) * (
+        jnp.sum(router_square, axis=0, keepdims=True) * (1.0 / 16) + EPS_SQUARE
+    )
+    row_router_new[...] = router_row
+    set_columns(
+        stats_r,
+        [
+            jnp.sum(router_square, axis=1, keepdims=True) + quarter * EPS_SQUARE,
+            jnp.sum(router_square * (1.0 / router_row), axis=1, keepdims=True),
+        ],
+    )
+    router_weight = dsh[:, 4 * D : 4 * D + 16].astype(F32)
+    qkv_square = dgrad[:, : 3 * D] * dgrad[:, : 3 * D]
+    proj_square = dgrad[:, 3 * D :] * dgrad[:, 3 * D :]
+    row_qkv = DECAY * rows3[:, 0:1] + (1.0 - DECAY) * (
+        jnp.sum(qkv_square, axis=1, keepdims=True) * (1.0 / (3 * D)) + EPS_SQUARE
+    )
+    row_proj = DECAY * rows3[:, 1:2] + (1.0 - DECAY) * (
+        jnp.sum(proj_square, axis=1, keepdims=True) * (1.0 / D) + EPS_SQUARE
+    )
+    rows3_new[...] = jnp.where(lax.broadcasted_iota(jnp.int32, rows3_new.shape, 1) == 0, row_qkv, row_proj)
+    inv_qkv, inv_proj = 1.0 / row_qkv, 1.0 / row_proj
+    for g in range(4):
+        square, inv = (qkv_square[:, g * D : (g + 1) * D], inv_qkv) if g < 3 else (proj_square, inv_proj)
+        stats[8 + g : 9 + g, :] = jnp.sum(square, axis=0, keepdims=True) + quarter * EPS_SQUARE
+        stats[12 + g : 13 + g, :] = jnp.sum(square * inv, axis=0, keepdims=True)
+    dense_weight = dsh[:, : 4 * D].astype(F32)
+    sizes = [
+        total(row_qkv), total(row_proj), total(router_row),
+        total(dense_weight[:, : 3 * D] * dense_weight[:, : 3 * D]),
+        total(dense_weight[:, 3 * D :] * dense_weight[:, 3 * D :]),
+        total(router_weight * router_weight),
+        gain_square[0:1], gain_square[1:2], gain_size[0:1], gain_size[1:2],
+    ]
+
+    tall[...] = jnp.zeros_like(tall)
+    turned[...] = jnp.zeros_like(turned)
+    turned[0:8, :] = moments[...]
+    moment_columns = jnp.transpose(turned[...])
+    load.wait()
+    columns = []
+    for i in range(2):
+        grad = egv[i, 0].astype(F32)
+        square = grad * grad
+        col = DECAY * moments[2 + i : 3 + i, :] + (1.0 - DECAY) * (
+            jnp.sum(square, axis=0, keepdims=True) * (1.0 / D) + EPS_SQUARE
+        )
+        moments_new[2 + i : 3 + i, :] = col
+        columns.append(jnp.sum(square, axis=1, keepdims=True) + D * EPS_SQUARE)
+        columns.append(jnp.sum(square * (1.0 / col), axis=1, keepdims=True))
+        weight = w1[i].astype(F32)
+        sizes.append(total(weight * weight))
+    for i in range(2):
+        grad = egv[i, 1].astype(F32)
+        square = grad * grad
+        row = DECAY * moment_columns[:, 4 + i : 5 + i] + (1.0 - DECAY) * (
+            jnp.sum(square, axis=1, keepdims=True) * (1.0 / D) + EPS_SQUARE
+        )
+        columns.append(row)
+        stats[4 + i : 5 + i, :] = jnp.sum(square, axis=0, keepdims=True) + D * EPS_SQUARE
+        stats[6 + i : 7 + i, :] = jnp.sum(square * (1.0 / row), axis=0, keepdims=True)
+        weight = w2[i].astype(F32)
+        sizes.append(total(weight * weight))
+        sizes.append(total(row))
+    set_columns(tall, columns)
+    flat = jnp.transpose(tall[...])
+    for n, m in ((0, 0), (2, 1), (1, 2), (3, 3)):
+        stats[m : m + 1, :] = flat[n : n + 1, :]
+    moments_new[0:2, :] = flat[4:6, :]
+    moments_new[4:8, :] = jnp.zeros((4, D), F32)
+    stats[16:24, :] = jnp.zeros((8, D), F32)
+    stats[16:17, :] = lane_sums(sizes, D)
+
+    landed[s] = stats[...]
+    landed_r[s] = stats_r[...]
+    copies = []
+    for d in range(1, 4):
+        mate = (z * 2 + c, (s + d) % 4)
+        copies.append(remote(stats, landed.at[s], xsem.at[0, d], xsem.at[1, d], mate))
+        copies.append(remote(stats_r, landed_r.at[s], rsem.at[0, d], rsem.at[1, d], mate))
+    for cp in copies:
+        cp.start()
+    for cp in copies:
+        cp.wait()
+    sums[...] = (landed[0] + landed[1]) + (landed[2] + landed[3])
+    sums_r[...] = (landed_r[0] + landed_r[1]) + (landed_r[2] + landed_r[3])
+
+
+def read_dense(ghat, dgrad):
+    for g in range(4):
+        for n in range(6):
+            column = 3 * D + 128 * n if g == 3 else n // 2 * D + g * 256 + n % 2 * 128
+            dgrad[:, column : column + 128] = ghat[g, n // 3, :, n % 3 * 128 : n % 3 * 128 + 128].astype(F32)
+
+
+def kernel_u(
+    eg, ghat, mine, w1, w2, dsh, gains, moments, moments_mid, rows3, row_router, cols, col_router, v, sums, sums_r,
+    g_first, g_second, n_first, n_second, dense_rms, expert_rms, n_gain, g_qkv, n_qkv, g_proj, n_proj, n_router,
+    cols_new, col_router_new, row_in_new, col_out_new,
+    egv, grads, news, turned, tall_d, dgrad,
+    isem, gsem, nsem,
+):
+    quarter = dsh.shape[0]
+    load = pltpu.make_async_copy(eg, egv, isem)
+    load.start()
+    read_dense(ghat, dgrad)
+    g_qkv[...] = dgrad[:, : 3 * D]
+    g_proj[...] = dgrad[:, 3 * D :]
+    router, gain = mine[0:16, :], mine[16:18, :]
+    raw_gain = gain * lax.rsqrt(v[...])
+    gain_weight = gains[...].astype(F32)
+    router_row = row_router[...]
+    router_weight = dsh[:, 4 * D : 4 * D + 16].astype(F32)
+    row_qkv, row_proj = rows3[:, 0:1], rows3[:, 1:2]
+    scalars = sums[16:17, :]
+    one = lambda n: pick(scalars, n)
+    load.wait()
+
+    hidden = 4.0 * D
+    row_in = DECAY * moments[0:2, :] + (1.0 - DECAY) * (sums[0:2, :] * (1.0 / hidden))
+    row_in_new[...] = row_in
+    col_out = DECAY * moments[6:8, :] + (1.0 - DECAY) * (sums[4:6, :] * (1.0 / hidden))
+    col_out_new[...] = col_out
+    turned[...] = jnp.zeros_like(turned)
+    turned[0:2, :] = row_in
+    turned[2:4, :] = moments_mid[0:2, :]
+    back = jnp.transpose(turned[...])
+    rms_all = []
+    for i in range(2):
+        r = row_in[i : i + 1, :]
+        mean = jnp.sum(r, axis=1, keepdims=True) * (1.0 / D)
+        raw = mean * jnp.sum(sums[2 + i : 3 + i, :] / r, axis=1, keepdims=True)
+        rms, factor = mean_square(raw, one(10 + i), D * hidden)
+        rms_all.append(rms)
+        left = factor * lax.rsqrt(back[:, i : i + 1] / mean)
+        grads[i] = egv[i, 0].astype(F32)
+        pltpu.make_async_copy(grads.at[i], g_first.at[i], gsem.at[i]).start()
+        news[i] = w1[i].astype(F32) + grads[i] * left * lax.rsqrt(moments_mid[2 + i : 3 + i, :])
+        pltpu.make_async_copy(news.at[i], n_first.at[i], nsem.at[i]).start()
+    for i in range(2):
+        col = col_out[i : i + 1, :]
+        mean = one(13 + 2 * i) * (1.0 / hidden)
+        raw = mean * jnp.sum(sums[6 + i : 7 + i, :] / col, axis=1, keepdims=True)
+        rms, factor = mean_square(raw, one(12 + 2 * i), D * hidden)
+        rms_all.append(rms)
+        left = factor * lax.rsqrt(back[:, 2 + i : 3 + i] / mean)
+        grads[2 + i] = egv[i, 1].astype(F32)
+        pltpu.make_async_copy(grads.at[2 + i], g_second.at[i], gsem.at[2 + i]).start()
+        news[2 + i] = w2[i].astype(F32) + grads[2 + i] * left * lax.rsqrt(col)
+        pltpu.make_async_copy(news.at[2 + i], n_second.at[i], nsem.at[2 + i]).start()
+    expert_rms[...] = lane_sums(rms_all, 128)
+
+    rms_g1, factor_g1 = mean_square(one(6), one(8), D)
+    rms_g2, factor_g2 = mean_square(one(7), one(9), D)
+    upper = lax.broadcasted_iota(jnp.int32, gain.shape, 0) == 0
+    n_gain[...] = gain_weight + jnp.where(upper, factor_g1, factor_g2) * raw_gain
+    col_dense = []
+    for g in range(4):
+        col = DECAY * cols[g : g + 1, :] + (1.0 - DECAY) * (sums[8 + g : 9 + g, :] * (1.0 / D))
+        cols_new[g : g + 1, :] = col
+        col_dense.append(col)
+    mean_qkv, mean_proj, mean_router = one(0) * (1.0 / D), one(1) * (1.0 / D), one(2) * (1.0 / D)
+    ratio = [jnp.sum(sums[12 + g : 13 + g, :] / col_dense[g], axis=1, keepdims=True) for g in range(4)]
+    rms_qkv, factor_qkv = mean_square(mean_qkv * (ratio[0] + ratio[1] + ratio[2]), one(3), 3 * D * D)
+    rms_proj, factor_proj = mean_square(mean_proj * ratio[3], one(4), D * D)
+    left_qkv = factor_qkv * lax.rsqrt(row_qkv / mean_qkv)
+    left_proj = factor_proj * lax.rsqrt(row_proj / mean_proj)
+    for g in range(4):
+        part = slice(g * D, (g + 1) * D)
+        new = dsh[:, part].astype(F32) + dgrad[:, part] * (left_qkv if g < 3 else left_proj) * lax.rsqrt(col_dense[g])
+        if g < 3:
+            n_qkv[:, part] = new
+        else:
+            n_proj[...] = new
+    col = DECAY * col_router[...] + (1.0 - DECAY) * (sums_r[:, 0:1] * (1.0 / D))
+    col_router_new[...] = col
+    raw_router = mean_router * jnp.sum(sums_r[:, 1:2] / col, axis=0, keepdims=True)
+    rms_router, factor_router = mean_square(raw_router, one(5), 16 * D)
+    tall_d[...] = jnp.zeros_like(tall_d)
+    tall_d[0:16, 0:quarter] = router * (factor_router * lax.rsqrt(router_row / mean_router)) * lax.rsqrt(col)
+    n_router[...] = router_weight + jnp.transpose(tall_d[...])[0:quarter, 0:16]
+    dense_rms[...] = lane_sums([rms_g1, rms_g2, rms_qkv, rms_proj, rms_router], 128)
+    for i in range(2):
+        pltpu.make_async_copy(news.at[i], n_first.at[i], nsem.at[i]).wait()
+        pltpu.make_async_copy(news.at[2 + i], n_second.at[i], nsem.at[2 + i]).wait()
+        pltpu.make_async_copy(grads.at[i], g_first.at[i], gsem.at[i]).wait()
+        pltpu.make_async_copy(grads.at[2 + i], g_second.at[i], gsem.at[2 + i]).wait()
 
 
 def params(number):
@@ -921,7 +1271,10 @@
     return pltpu.SemaphoreType.DMA(shape)
 
 
-def fast(tokens, routes, cotangent, gain_attn, w_qkv, w_proj, gain_moe, w_router, w_in, w_out):
+def fast(
+    tokens, routes, cotangent, gain_attn, w_qkv, w_proj, gain_moe, w_router, w_in, w_out,
+    v_attn, v_moe, row_qkv, col_qkv, row_proj, col_proj, row_router, col_router, row_in, col_in, row_out, col_out,
+):
     count = tokens.shape[0]
     images = count // SEQ
     rows = images * SEQ_PAD
@@ -951,17 +1304,17 @@
         out_shape=(
             shape((rows, 3 * D), BF), shape((rows, D), BF), shape((rows, D), F32), shape((rows, 128), F32),
             shape((16, rows), F32), shape((16, rows), jnp.int32), shape((32, D), F32), shape((D, wide), BF),
-            shape((slots, D), BF), shape((16, 8, 256), F32), shape((slots, D), BF), shape((2, 4, D, D), BF),
+            shape((slots, D), BF), shape((16, 8, 256), F32), shape((slots, D), BF), shape((4, D, D), BF),
         ),
-        in_specs=[vmem] * 4 + [hbm] * 2,
+        in_specs=[vmem] * 4 + [hbm],
         out_specs=(vmem,) * 10 + (hbm,) * 2,
         scratch_shapes=[
             pltpu.VMEM((slots, D), BF), pltpu.VMEM((rows, D), BF), pltpu.VMEM((4 * cap, rows), BF),
-            pltpu.VMEM((rows, rows), BF), dma(2, 4), dma(2, 4), dma(2, 16), dma(2, 2), dma(), dma(4), dma(2, 4), dma(),
+            pltpu.VMEM((rows, rows), BF), dma(2, 4), dma(2, 4), dma(2, 16), dma(2), dma(), dma(2), dma(2, 2), dma(),
         ],
         compiler_params=params(1),
         name="forward",
-    )(tok, cot, rt, dsh, w_in, w_out)
+    )(tok, cot, rt, dsh, w_in)
 
     outs, ginh, ginb, ggb, gw = pl.pallas_call(
         functools.partial(kernel_e, cap),
@@ -969,24 +1322,23 @@
             shape((slots, D), BF), shape((slots, D), BF), shape((slots, D), BF), shape((16, 8, 256), F32),
             shape((2, 4, D, D), BF),
         ),
-        in_specs=[hbm, vmem, hbm, hbm],
+        in_specs=[hbm, vmem, hbm, hbm, hbm],
         out_specs=(hbm, hbm, hbm, vmem, hbm),
         scratch_shapes=[
             pltpu.VMEM((4, D, D), BF), pltpu.VMEM((FF, D), BF), pltpu.VMEM((slots, D), BF), pltpu.VMEM((slots, D), BF),
             pltpu.VMEM((16, 8, 256), F32), pltpu.VMEM((slots, FF), BF), pltpu.VMEM((slots, FF), BF),
             pltpu.VMEM((4 * cap, D), F32), pltpu.VMEM((2, 4 * cap, D), BF),
             pltpu.VMEM((16, 8, 256), F32), pltpu.VMEM((4 * cap, 128), F32),
-            dma(2, 16), dma(2, 16), dma(2, 16), dma(2, 16), dma(5), dma(5), dma(2),
+            dma(2, 16), dma(2, 16), dma(2, 16), dma(2, 16), dma(5), dma(5), dma(2), dma(2), dma(2), dma(), dma(2, 2),
         ],
         compiler_params=params(2),
         name="experts",
-    )(xsend, gsend, cotr, wfull)
-
-    half = D // 8
+    )(xsend, gsend, cotr, wfull, w_out)
+
     block_out, gtok, ghat, extra, outb, eg = pl.pallas_call(
         functools.partial(kernel_b, cap),
         out_shape=(
-            shape((rows, D), BF), shape((rows, D), F32), shape((2, 4, half, D), BF), shape((32, D), F32),
+            shape((rows, D), BF), shape((rows, D), F32), shape((4, 2, quarter, D // 2), BF), shape((32, D), F32),
             shape((slots, D), BF), shape((2, 2, D, D), BF),
         ),
         in_specs=[vmem] * 11 + [hbm] * 3,
@@ -994,12 +1346,13 @@
         scratch_shapes=[
             pltpu.VMEM((slots, D), BF), pltpu.VMEM((4 * cap, rows), BF), pltpu.VMEM((rows, D), F32),
             pltpu.VMEM((rows, D), BF), pltpu.VMEM((rows, D), BF), pltpu.VMEM((rows, D), BF),
-            pltpu.VMEM((rows, 3 * D), BF), pltpu.VMEM((4, 2, 4, half, D), BF), pltpu.VMEM((4, 4, half, D), BF),
-            pltpu.VMEM((4, 4, half, D), BF), pltpu.VMEM((4, half, D), BF), pltpu.VMEM((4, half, D), BF),
+            pltpu.VMEM((rows, 3 * D), BF), pltpu.VMEM((4, 4, 2, quarter, D // 2), BF),
+            pltpu.VMEM((4, 4, quarter, D // 2), BF), pltpu.VMEM((4, 4, quarter, D // 2), BF),
+            pltpu.VMEM((4, quarter, D // 2), BF), pltpu.VMEM((4, 4, quarter // 4, D // 2), BF),
             pltpu.VMEM((3, 32, D), F32), pltpu.VMEM((9, 32, D), F32), pltpu.VMEM((4, D, D), BF),
             pltpu.VMEM((D, D), BF), pltpu.VMEM((16, rows), F32),
-            dma(2, 16), dma(2), dma(2, 4), dma(2, 4), dma(), dma(), dma(2, 4), dma(2, 4), dma(2, 4), dma(2, 4),
-            dma(2), dma(2, 7),
+            dma(2, 16), dma(2), dma(2, 4), dma(2, 4), dma(), dma(), dma(2, 4, 4), dma(2, 4, 4), dma(2, 4, 4),
+            dma(2, 4, 4), dma(2, 4), dma(2, 7),
         ],
         compiler_params=params(3),
         name="backward",
@@ -1008,21 +1361,78 @@
     def unpadded(array):
         return array.reshape(images, SEQ_PAD, D)[:, :SEQ].reshape(count, D)
 
-    part_dense = jnp.swapaxes(ghat, 1, 2).reshape(quarter, 4 * D).astype(F32)
-    mine = lax.dynamic_slice_in_dim(extra, lax.axis_index("shard") * quarter, quarter, axis=1)
-    dense_parts = (mine[16], part_dense[:, : 3 * D], part_dense[:, 3 * D :], mine[17], mine[:16].T)
-    eg = eg.astype(F32)
-    return unpadded(block_out), unpadded(gtok), dense_parts, (eg[:, 0], eg[:, 1])
+    gains = jnp.stack([gain_attn, gain_moe])
+    moments = jnp.concatenate([row_in, col_in, row_out, col_out])
+    mine, v_new, rows_new, row_router_new, moments_mid, sums, sums_r = pl.pallas_call(
+        kernel_s,
+        out_shape=(
+            shape((32, quarter), F32), shape((2, quarter), F32), shape((quarter, 2), F32), shape((1, quarter), F32),
+            shape((8, D), F32), shape((24, D), F32), shape((16, 128), F32),
+        ),
+        in_specs=[hbm] + [vmem] * 10,
+        out_specs=(vmem,) * 7,
+        scratch_shapes=[
+            pltpu.VMEM((2, 2, D, D), BF), pltpu.VMEM((D, 128), F32), pltpu.VMEM((128, D), F32),
+            pltpu.VMEM((24, D), F32), pltpu.VMEM((4, 24, D), F32), pltpu.VMEM((16, 128), F32),
+            pltpu.VMEM((4, 16, 128), F32), pltpu.VMEM((quarter, 4 * D), F32), dma(), dma(2, 4), dma(2, 4),
+        ],
+        compiler_params=params(4),
+        name="update_sums",
+    )(
+        eg, ghat, extra, w_in, w_out, dsh, gains, moments, jnp.stack([row_qkv, row_proj], axis=1), row_router[None],
+        jnp.stack([v_attn, v_moe]),
+    )
+    (
+        g_first, g_second, n_first, n_second, dense_rms, expert_rms, n_gain, g_qkv, n_qkv, g_proj, n_proj, n_router,
+        cols_new, col_router_new, row_in_new, col_out_new,
+    ) = pl.pallas_call(
+        kernel_u,
+        out_shape=(
+            shape((2, D, D), F32), shape((2, D, D), F32), shape((2, D, D), F32), shape((2, D, D), F32),
+            shape((1, 128), F32), shape((1, 128), F32), shape((2, quarter), F32),
+            shape((quarter, 3 * D), F32), shape((quarter, 3 * D), F32),
+            shape((quarter, D), F32), shape((quarter, D), F32), shape((quarter, 16), F32),
+            shape((4, D), F32), shape((16, 1), F32), shape((2, D), F32), shape((2, D), F32),
+        ),
+        in_specs=[hbm] + [vmem] * 15,
+        out_specs=(hbm,) * 4 + (vmem,) * 12,
+        scratch_shapes=[
+            pltpu.VMEM((2, 2, D, D), BF), pltpu.VMEM((4, D, D), F32), pltpu.VMEM((4, D, D), F32),
+            pltpu.VMEM((128, D), F32), pltpu.VMEM((128, 256), F32), pltpu.VMEM((quarter, 4 * D), F32),
+            dma(), dma(4), dma(4),
+        ],
+        compiler_params=pltpu.CompilerParams(vmem_limit_bytes=VMEM_LIMIT),
+        name="update",
+    )(
+        eg, ghat, mine, w_in, w_out, dsh, gains, moments, moments_mid, rows_new, row_router_new,
+        jnp.concatenate([col_qkv, col_proj]).reshape(4, D), col_router[:, None], v_new, sums, sums_r,
+    )
+    return (
+        unpadded(block_out), unpadded(gtok), dense_rms[0, :5], expert_rms[0, :4].reshape(2, 2).T,
+        mine[16], n_gain[0], v_new[0], mine[17], n_gain[1], v_new[1],
+        g_qkv, n_qkv, rows_new[:, 0], cols_new[:3].reshape(3 * D),
+        g_proj, n_proj, rows_new[:, 1], cols_new[3],
+        mine[:16].T, n_router, row_router_new[0], col_router_new[:, 0],
+        g_first, n_first, row_in_new, moments_mid[2:4],
+        g_second, n_second, moments_mid[0:2], col_out_new,
+    )
 
 
 def local(
     tokens, routes, cotangent, gain_attn, w_qkv, w_proj, gain_moe, w_router, w_in, w_out,
     v_attn, v_moe, row_qkv, col_qkv, row_proj, col_proj, row_router, col_router, row_in, col_in, row_out, col_out,
 ):
-    fits = (
-        lax.axis_size("shard") == 4 and lax.axis_size("expert") == 8 and w_in.shape[0] == 2 and tokens.shape[0] % SEQ == 0
-    )
-    block_out, grad_tokens, dense_parts, expert_parts = (fast if fits else general)(
+    if (
+        lax.axis_size("shard") == 4
+        and lax.axis_size("expert") == 8
+        and w_in.shape == w_out.shape == (2, D, D)
+        and tokens.shape[0] % SEQ == 0
+    ):
+        return fast(
+            tokens, routes, cotangent, gain_attn, w_qkv, w_proj, gain_moe, w_router, w_in, w_out,
+            v_attn, v_moe, row_qkv, col_qkv, row_proj, col_proj, row_router, col_router, row_in, col_in, row_out, col_out,
+        )
+    block_out, grad_tokens, dense_parts, expert_parts = general(
         tokens, routes, cotangent, gain_attn, w_qkv, w_proj, gain_moe, w_router, w_in, w_out
     )
     part_g1, part_qkv, part_proj, part_g2, part_router = dense_parts

time: 677 us -> 607 us (0.90)
  other arithmetic: 57.2 us -> 4.3 us
  blocking collectives: 19.8 us -> 0 us
  Pallas kernels: 555 us -> 568 us
  between operations: 10.5 us -> 1.31 us
    pallas_call x0 -> x2, Pallas kernels: none -> 28.7 us  [the longest x1 15 us: fast(): pl.pallas_call(kernel_u, out_shape=(shape((2, D, D), F32), shape((2, D, D...]
    pallas_call x1, Pallas kernels: 151 us -> 125 us  [fast(): pl.pallas_call(functools.partial(kernel_a, cap), out_shape=(shape((rows,...]
    reduce_sum x24 -> x0, other arithmetic: 23.7 us -> none  [the longest x3 5.66 us: local(): jnp.sum(ratio_sum / col_new)]
    pallas_call x1, Pallas kernels: 173 us -> 194 us  [fast(): pl.pallas_call(functools.partial(kernel_e, cap), out_shape=(shape((slots,...]
    psum x1 -> x0, blocking collectives: 19.8 us -> none  [local(): dense_sums, gain_sums = lax.psum((dense_sums, gain_sums), 'shard')]
    add x8 -> x0, other arithmetic: 16.9 us -> none  [the longest x3 6.69 us: local(): dense_new.append(weight + factor * raw)]
    pallas_call x1, Pallas kernels: 231 us -> 220 us  [fast(): pl.pallas_call(functools.partial(kernel_b, cap), out_shape=(shape((rows,...]
    another operation x6 -> x3, other arithmetic: 9.97 us -> 1.17 us  [the longest x1 0.59 us: fast(): jnp.stack([v_attn, v_moe])]
where the time goes in v2:
time: 607 us; the launch traced here: 598 us
  Pallas kernels  568 us (94%)
  local copies, waits for them, and re-layouts  25 us (4%)
    pallas_call x1, Pallas kernels, fast(): pl.pallas_call(functools.partial(kernel_b, cap), out_shape=(shape((rows,...  220 us
    pallas_call x1, Pallas kernels, fast(): pl.pallas_call(functools.partial(kernel_e, cap), out_shape=(shape((slots,...  194 us
    pallas_call x1, Pallas kernels, fast(): pl.pallas_call(functools.partial(kernel_a, cap), out_shape=(shape((rows,...  125 us
    pallas_call x1, Pallas kernels, fast(): pl.pallas_call(kernel_u, out_shape=(shape((2, D, D), F32), shape((2, D, D...  15 us
    pallas_call x1, Pallas kernels, fast(): pl.pallas_call(kernel_s, out_shape=(shape((32, quarter), F32), shape((2,...  13.7 us

profile of v2, /device:TPU:0, one launch (start us, length us, event | category | flops | bytes accessed | tf_op | source)
XLA Modules:
  0.0 598.4 jit_solution(288908039997815366)
XLA Ops:
  0.7 1.7 reshape.96
  2.4 1.2 pad.15
  3.9 1.2 pad.16
  5.2 0.7 reshape.101
  6.1 1.2 fusion.1.dsh
  7.2 125.5 %forward.1 = (bf16[896,2304]{1,0:T(8,128)(2,1)}, bf16[896,768]{1,0:T(8,128)(2,1)}, f32[896,768]{1,0:T(8,128)}, f32[896,128]{1,0:T(8,128)}, f32[16,896]{1,0:T(8,1...) custom-call(bf16[896,768]{1,0:T(8,128)(2,1)} %bitcast.28, ...), custom_call_target="tpu_custom_call" | custom-call | tf_op jit(solution)/shard_map/forward/pallas_call | solution.py:1302
  132.7 193.9 %experts.1 = (bf16[2560,768]{1,0:T(8,128)(2,1)}, bf16[2560,768]{1,0:T(8,128)(2,1)}, bf16[2560,768]{1,0:T(8,128)(2,1)}, f32[16,8,256]{2,1,0:T(8,128)}, bf16[2,4,768,768]{3,2,1,0:T(8,128)(2,1)}) custom-call(bf16[2560,768]{1,0:T(8,128)(2,1)} %get-tuple-element.82.xsend, f32[16,8,256]{2,1,0:T(8,128)} %get-tuple-element.83.gsend, ...), custom_call_target="tpu_custom_call" | custom-call | tf_op jit(solution)/shard_map/experts/pallas_call | solution.py:1319
  326.6 219.7 %backward.1 = (bf16[896,768]{1,0:T(8,128)(2,1)}, f32[896,768]{1,0:T(8,128)}, bf16[4,2,192,384]{3,2,1,0:T(8,128)(2,1)}, f32[32,768]{1,0:T(8,128)}, bf16[2560,768]...) custom-call(bf16[896,768]{1,0:T(8,128)(2,1)} %bitcast.29, bf16[896,768]{1,0:T(8,128)(2,1)} %bitcast.31, ...), custom_call_target="tpu_custom_call" | custom-call | tf_op jit(solution)/shard_map/backward/pallas_call | solution.py:1338
  546.4 1.4 slice.68
  547.7 1.3 reshape.103
  549.1 1.9 slice.69
  551.0 1.7 reshape.105
  552.7 0.6 pad_maximum_fusion.5.gains
  553.3 0.6 pad_maximum_fusion.moments
  554.0 0.8 copy.65.rows3
  554.7 0.6 pad_maximum_fusion.4.v_gain
  555.3 13.7 %update_sums.1 = (f32[32,192]{1,0:T(8,128)}, f32[2,192]{1,0:T(2,128)}, f32[192,2]{1,0:T(8,128)}, f32[1,192]{1,0:T(1,128)}, f32[8,768]{1,0:T(8,128)}, /*index=5*/f32[24,768]{1,0:T(8,128)}, f32[16,128]{1,0:T(8,128)}) custom-call(bf16[2,2,768,768]{3,2,1,0:T(8,128)(2,1)} %get-tuple-element.92.eg, bf16[4,2,192,384]{3,2,1,0:T(8,128)(2,1)} %get-tuple-element.93.ghat, ...), custom_call_target="tpu_custom_call" | custom-call | tf_op jit(solution)/shard_map/update_sums/pallas_call | solution.py:1366
  569.1 0.6 reshape.106.cols
  569.7 0.7 copy.66.col_router
  570.4 15.0 %update.1 = (f32[2,768,768]{2,1,0:T(8,128)}, f32[2,768,768]{2,1,0:T(8,128)}, f32[2,768,768]{2,1,0:T(8,128)}, f32[2,768,768]{2,1,0:T(8,128)}, f32[1,128]{1,0:T(1,...) custom-call(bf16[2,2,768,768]{3,2,1,0:T(8,128)(2,1)} %get-tuple-elem, ...), custom_call_target="tpu_custom_call" | custom-call | tf_op jit(solution)/shard_map/update/pallas_call | solution.py:1388
  585.4 1.2 slice_bitcast_fusion.1
  586.6 0.7 slice_reduce_fusion.3
  587.3 0.7 copy.67
  588.0 0.6 fusion.2
  588.6 1.3 fusion.5
  589.9 0.8 slice_reduce_fusion
  590.7 1.3 reshape.107
  592.0 1.3 slice_reduce_fusion.2
  593.3 0.6 slice_bitcast_fusion
  593.9 1.6 copy.68
  595.5 1.3 reduce.4
  596.8 0.6 fusion.3
  (59 shorter events, 1.3 us)
Async XLA Ops:
  0.7 2.9 copy-start
  3.6 1.5 copy-start.9
  3.6 2.3 copy-start.21
  3.6 2.3 copy-start.22
  3.6 2.3 copy-start.7
  3.6 2.5 copy-start.1
  3.9 2.1 copy-start.3
  550.9 2.4 copy-start.10
  550.9 2.4 copy-start.11
  551.0 2.4 copy-start.12
  551.0 2.4 copy-start.13
  551.0 3.0 copy-start.16
  551.0 3.0 copy-start.17
  551.0 3.7 copy-start.18
  551.0 3.7 copy-start.19
  555.3 13.8 %copy-start.6 = (f32[2304]{0:T(1024)S(1)}, f32[2304]{0:T(1024)}, u32[]{:S(2)}) copy-start(f32[2304]{0:T(1024)} %param.35) | copy-start | bytes 27652
  555.3 13.8 %copy-start.14 = (f32[768]{0:T(1024)S(1)}, f32[768]{0:T(1024)}, u32[]{:S(2)}) copy-start(f32[768]{0:T(1024)} %param.37) | copy-start | bytes 9220
  555.3 14.4 %copy-start.20 = (f32[16]{0:T(128)S(1)}, f32[16]{0:T(128)}, u32[]{:S(2)}) copy-start(f32[16]{0:T(128)} %param.39) | copy-start | bytes 196
  570.4 17.6 %copy-start.4 = (f32[32,192]{1,0:T(8,128)S(1)}, f32[32,192]{1,0:T(8,128)}, u32[]{:S(2)}) copy-start(f32[32,192]{1,0:T(8,128)} %get-tuple-element.95.mine) | copy-start | bytes 73732
  570.4 17.6 %copy-start.8 = (f32[2,192]{1,0:T(2,128)S(1)}, f32[2,192]{1,0:T(2,128)}, u32[]{:S(2)}) copy-start(f32[2,192]{1,0:T(2,128)} %get-tuple-element.99.v) | copy-start | bytes 4612
  570.4 19.5 %copy-start.2 = (f32[192,2]{1,0:T(8,128)S(1)}, f32[192,2]{1,0:T(8,128)}, u32[]{:S(2)}) copy-start(f32[192,2]{1,0:T(8,128)} %get-tuple-element.97.rows3) | copy-start | bytes 4612
  570.4 26.4 %copy-start.5 = (f32[8,768]{1,0:T(8,128)S(1)}, f32[8,768]{1,0:T(8,128)}, u32[]{:S(2)}) copy-start(f32[8,768]{1,0:T(8,128)} %get-tuple-element.96.moments_mid) | copy-start | bytes 73732
  570.4 27.0 %copy-start.15 = (f32[1,192]{1,0:T(1,128)S(1)}, f32[1,192]{1,0:T(1,128)}, u32[]{:S(2)}) copy-start(f32[1,192]{1,0:T(1,128)} %get-tuple-element.98.row_router) | copy-start | bytes 2308

commit v3 on v2

--- a/solution.py
+++ b/solution.py
@@ -379,9 +379,9 @@
 
 
 def kernel_a(
-    cap, tok, cot, rt, dsh, w1,
-    qkv, att, hid, lse, gate_t, ranks, aux, dense, xsend, gsend, cotr, wfull,
-    csend, low, hits, tri, dsem, dfsem, csem, wsem, wloc, wrecv, fsem, osem,
+    cap, tok, cot, rt, dsh, w1, w2,
+    qkv_out, att_out, hid_out, lse, gate_t, ranks, aux, dense_out, xsend_out, gsend, cotr, wfull, wfull2, xfar,
+    qkv, att, hid, dense, xsend, ssem, csend, low, hits, tri, dsem, dfsem, csem, wsem, wloc, wrecv, fsem, wsem2, wloc2, wrecv2, fsem2, osem, xsem,
 ):
     me = Place()
     z, c, s = me.z, me.core, me.shard
@@ -392,7 +392,7 @@
 
     quarter = dsh.shape[0]
     half = quarter // 2
-    dense_out = []
+    dense_copies = []
     for d in range(1, 4):
         cp = remote(
             dsh.at[pl.ds(pl.multiple_of(c * half, half), half)],
@@ -400,7 +400,7 @@
             dsem.at[0, d], dsem.at[1, d], (z * 2 + c, (s + d) % 4),
         )
         cp.start()
-        dense_out.append(cp)
+        dense_copies.append(cp)
     dense[pl.ds(pl.multiple_of(s * quarter, quarter), quarter), :] = dsh[...]
 
     expert_row = lax.broadcasted_iota(jnp.int32, (16, rows), 0)
@@ -438,7 +438,7 @@
 
     forwards = []
     for d in range(1, 4):
-        dense_out[d - 1].wait()
+        dense_copies[d - 1].wait()
         source = (s - d + 4) % 4
         place = pl.ds(pl.multiple_of(source * quarter + c * half, half), half)
         cp = remote(dense.at[place], dense.at[place], dfsem.at[0, d], dfsem.at[1, d], me.sibling)
@@ -446,10 +446,12 @@
         forwards.append(cp)
 
     in_quarters = Quarters(me, w1, lambda q: wfull.at[q], wsem, wrecv, wloc, fsem)
+    out_quarters = Quarters(me, w2, lambda q: wfull2.at[q], wsem2, wrecv2, wloc2, fsem2)
 
     for cp in forwards:
         cp.wait()
     in_quarters.start()
+    out_quarters.start()
 
     flat = jnp.transpose(dense[:, 3072:3200].astype(F32))
     aux[...] = flat[0:32, :]
@@ -482,16 +484,43 @@
     gate_t[...] = weights / jnp.maximum(jnp.sum(weights, axis=0, keepdims=True), 0.5)
     gsend[...] = jnp.zeros_like(gsend)
 
+    far = me.plane(3)
+
+    def far_copy(k):
+        return remote(
+            xsend.at[pl.ds(pl.multiple_of((far * 4 + k) * cap, cap), cap)],
+            xfar.at[pl.ds(pl.multiple_of(s * cap, cap), cap)],
+            xsem.at[0, k], xsem.at[1, s], me.peer(far * 4 + k),
+        )
+
     @pl.loop(0, 4)
-    def _(plane):
+    def _(step):
+        plane = me.plane(3 - step)
         fill_hits(ranks, plane, hits, cap)
         xsend[pl.ds(pl.multiple_of(plane * 4 * cap, 4 * cap), 4 * cap), :] = mm(hits[...], low[...]).astype(BF)
+
+        @pl.when(step == 0)
+        def _():
+            for k in range(4):
+                far_copy(k).start()
+
         for k in range(4):
             row = mm_nt(three_rows(gate_t[pl.ds(plane * 4 + k, 1), :]), hits[k * cap : (k + 1) * cap, :])
             gsend[plane * 4 + k, :, 0:cap] = jnp.broadcast_to(jnp.sum(row, axis=0, keepdims=True), (8, cap))
 
+    saves = [
+        pltpu.make_async_copy(held, place, ssem.at[n])
+        for n, (held, place) in enumerate(
+            ((qkv, qkv_out), (att, att_out), (hid, hid_out), (dense, dense_out), (xsend, xsend_out))
+        )
+    ]
+    for cp in saves:
+        cp.start()
+
     in_quarters.forward()
+    out_quarters.forward()
     in_quarters.finish()
+    out_quarters.finish()
     for d in range(1, 16):
         p = (me.number + d) % 16
         cot_copy(p).wait_send()
@@ -499,6 +528,13 @@
             csend.at[pl.ds(0, cap)], cotr.at[pl.ds(0, cap)], csem.at[0, p], csem.at[1, p], me.peer(p)
         ).wait_recv()
     own_copy.wait()
+    for k in range(4):
+        far_copy(k).wait_send()
+        remote(
+            xsend.at[pl.ds(0, cap)], xfar.at[pl.ds(k * cap, cap)], xsem.at[0, k], xsem.at[1, k], me.peer(far * 4 + k)
+        ).wait_recv()
+    for cp in saves:
+        cp.wait()
 
 
 def attention_forward(qkv, att, lse, images):
@@ -529,14 +565,14 @@
 
 
 def kernel_e(
-    cap, xsend, gsend, cotr, wfull, w2,
-    outs, ginh, ginb, ggb, gw,
+    cap, xsend, gsend, cotr, wfull, wfull2, xfar,
+    outs, ginh, ginb, ggb, gw, outn,
     w1v, w2v, xr, gcot, gater, act, gpre, acc, stage, ggs, gcol,
-    xsem, gsem, rsem, ggsem, lsem, wlsem, stsem, wsem, wrecv, wloc, fsem,
+    xsem, gsem, rsem, ggsem, lsem, wlsem, stsem, nsem,
 ):
     me = Place()
     z, c, s = me.z, me.core, me.shard
-    greet(me.peers() + [(z * 2 + 1 - c, t) for t in range(4)])
+    greet(me.peers())
     block = 4 * cap
 
     def part(ref, p):
@@ -550,6 +586,9 @@
 
     def r_copy(p):
         return remote(part(ginh, p), part(ginb, me.number), rsem.at[0, p], rsem.at[1, me.number], me.peer(p))
+
+    def n_copy(p):
+        return remote(part(outs, p), part(outn, me.number), nsem.at[0, p], nsem.at[1, me.number], me.peer(p))
 
     def gg_copy(p):
         return remote(ggs.at[p], ggb.at[me.number], ggsem.at[0, p], ggsem.at[1, me.number], me.peer(p))
@@ -561,16 +600,17 @@
     ]
     own_r = pltpu.make_async_copy(part(ginh, me.number), part(ginb, me.number), lsem.at[3])
     own_g = pltpu.make_async_copy(ggs.at[me.number], ggb.at[me.number], lsem.at[4])
-    w_copies = [pltpu.make_async_copy(wfull, w1v, wlsem.at[0])]
-    out_quarters = Quarters(
-        me, w2, lambda q: w2v.at[pl.ds(pl.multiple_of(q * D, D), D)], wsem, wrecv, wloc, fsem
-    )
-    out_quarters.start()
+    own_n = pltpu.make_async_copy(part(outs, me.number), part(outn, me.number), lsem.at[5])
+    far = me.plane(3)
+    far_rows = pl.ds(pl.multiple_of(far * block, block), block)
+    w_copies = [
+        pltpu.make_async_copy(wfull, w1v, wlsem.at[0]), pltpu.make_async_copy(xfar, xr.at[far_rows], wlsem.at[5])
+    ] + [pltpu.make_async_copy(wfull2.at[f], w2v.at[pl.ds(f * D, D)], wlsem.at[1 + f]) for f in range(4)]
     for d in range(1, 16):
         g_copy((me.number + d) % 16).start()
     for cp in local_copies + w_copies:
         cp.start()
-    for step in range(4):
+    for step in (2, 1, 0):
         for k in range(4):
             p = me.plane(step) * 4 + k
 
@@ -590,7 +630,10 @@
 
             @pl.when(p != me.number)
             def _():
-                remote(part(xsend, p), part(xr, p), xsem.at[0, p], xsem.at[1, p], me.peer(p)).wait_recv()
+                @pl.when(plane != far)
+                def _():
+                    remote(part(xsend, p), part(xr, p), xsem.at[0, p], xsem.at[1, p], me.peer(p)).wait_recv()
+
                 remote(gsend.at[p], gater.at[p], gsem.at[0, p], gsem.at[1, p], me.peer(p)).wait_recv()
 
     def stage_out(plane, which):
@@ -616,17 +659,10 @@
                 slope = half + (0.5 * pre) * (1.0 - t * t) * (GELU_A + 3.0 * GELU_A * GELU_B * square)
                 gpre[r, cols] = slope.astype(BF)
 
-    first_half(0)
-    first_half(1)
-    out_quarters.forward()
-    out_quarters.finish()
-
     @pl.loop(0, 4)
-    def _(step):
-        @pl.when(step > 1)
-        def _():
-            first_half(step)
-
+    def _(turn):
+        step = (turn + 3) % 4
+        first_half(step)
         plane = me.plane(step)
         r = pl.ds(pl.multiple_of(plane * block, block), block)
         acc[...] = mm(act[r, :], w2v[...])
@@ -635,10 +671,6 @@
             row = gater[plane * 4 + k, 0:1, 0:cap]
             column = jnp.sum(jnp.where(eye, row, 0.0), axis=1, keepdims=True)
             gcol[k * cap : (k + 1) * cap, :] = jnp.broadcast_to(column, (cap, 128))
-
-        @pl.when(step > 0)
-        def _():
-            stage_out(plane, 0).wait()
 
         for k in range(4):
             rk = pl.ds(pl.multiple_of(plane * block + k * cap, cap), cap)
@@ -679,7 +711,21 @@
                 own_r.start()
                 own_g.start()
 
-    stage_out(0, 0).wait()
+        stage_out(plane, 0).wait()
+
+        @pl.when(step < 2)
+        def _():
+            for k in range(4):
+                p = plane * 4 + k
+
+                @pl.when(p != me.number)
+                def _():
+                    n_copy(p).start()
+
+                @pl.when(p == me.number)
+                def _():
+                    own_n.start()
+
 
     @pl.loop(0, 4)
     def _(f):
@@ -694,7 +740,11 @@
         cp.start()
     for d in range(1, 16):
         p = (me.number + d) % 16
-        x_copy(p).wait_send()
+
+        @pl.when(p // 4 != far)
+        def _():
+            x_copy(p).wait_send()
+
         g_copy(p).wait_send()
         r_copy(p).wait_send()
         gg_copy(p).wait_send()
@@ -702,6 +752,16 @@
         remote(ggs.at[p], ggb.at[p], ggsem.at[0, p], ggsem.at[1, p], me.peer(p)).wait_recv()
     own_r.wait()
     own_g.wait()
+    own_n.wait()
+    for step in range(2):
+        for k in range(4):
+            p = me.plane(step) * 4 + k
+
+            @pl.when(p != me.number)
+            def _():
+                n_copy(p).wait_send()
+                remote(part(outs, p), part(outn, p), nsem.at[0, p], nsem.at[1, p], me.peer(p)).wait_recv()
+
     for cp in out_w:
         cp.wait()
 
@@ -738,9 +798,9 @@
 
 
 def kernel_b(
-    cap, tok, cot, dense, aux, qkv, att, hid, lse, gate_t, ranks, ggb, ginb, outs, gw,
+    cap, tok, cot, aux, lse, gate_t, ranks, ggb, dense_in, qkv_in, att_in, hid_in, ginb, outs, gw, outn,
     block_out, gtok, ghat, extra, outb, eg,
-    rowsv, hits, gmoe, low, glow, gatt, gqkv, gd, ra, rb, sc, rc, exs, exl, gx, own_w, ggt,
+    dense, qkv, att, hid, hsem, rowsv, hits, gmoe, low, glow, gatt, gqkv, gd, ra, rb, sc, rc, exs, exl, gx, own_w, ggt,
     osem, lsem, wxsem, wsem, wload, wlocal, asem, bsem, zsem, fsem, esem, xsem,
 ):
     me = Place()
@@ -759,22 +819,22 @@
 
     load_in = pltpu.make_async_copy(ginb, rowsv, lsem.at[0])
     load_in.start()
+    held = [
+        pltpu.make_async_copy(place, ref, hsem.at[n])
+        for n, (place, ref) in enumerate(((hid_in, hid), (att_in, att), (dense_in, dense), (qkv_in, qkv)))
+    ]
     swap = [remote(gw.at[1 - c, t], gx.at[t], wxsem.at[0, t], wxsem.at[1, t], me.sibling) for t in range(4)]
     for cp in swap:
         cp.start()
-    own_o = pltpu.make_async_copy(part(outs, me.number), part(outb, me.number), lsem.at[1])
-    own_o.start()
 
     def send_outs(step):
         for k in range(4):
-            p = me.plane(step) * 4 + k
-
-            @pl.when(p != me.number)
-            def _():
-                o_copy(p).start()
-
-    for step in (3, 2, 1, 0):
-        send_outs(step)
+            o_copy(me.plane(step) * 4 + k).start()
+
+    send_outs(3)
+    send_outs(2)
+    for cp in held:
+        cp.start()
 
     load_in.wait()
     gmoe[...] = jnp.zeros_like(gmoe)
@@ -789,6 +849,8 @@
         r = pl.ds(pl.multiple_of(plane * block, block), block)
         gmoe[...] += mm_tn(hits[...], rowsv[r, :])
 
+    for cp in held:
+        cp.wait()
     gates = gate_t[...]
     grad_gates = ggt[...]
     grad_logits = gates * (grad_gates - jnp.sum(gates * grad_gates, axis=0, keepdims=True))
@@ -949,9 +1011,21 @@
         )
         exs[0, 16:17, :] += jnp.sum(w * hat, axis=0, keepdims=True)
 
+    def add_outputs(source, step):
+        plane = me.plane(step)
+        r = pl.ds(pl.multiple_of(plane * block, block), block)
+        load = pltpu.make_async_copy(source.at[r], rowsv.at[r], lsem.at[0])
+        load.start()
+        fill_hits(ranks, plane, hits, cap)
+        load.wait()
+        gmoe[...] += mm_tn(hits[...], rowsv[r, :])
+
     to_b(2)
     x_first = remote(exs.at[0], exl.at[0], xsem.at[0, 0], xsem.at[1, 0], me.sibling)
     x_first.start()
+    gmoe[...] = hid[...]
+    add_outputs(outn, 0)
+    add_outputs(outn, 1)
     to_c(3)
     x_first.wait()
     exs[1] = exs[0] + exl[0]
@@ -978,21 +1052,12 @@
     for g in (3, 0, 1, 2):
         to_e(g)
 
-    own_o.wait()
-    for d in range(1, 16):
-        p = (me.number + d) % 16
-        o_copy(p).wait_send()
-        remote(part(outs, p), part(outb, p), osem.at[0, p], osem.at[1, p], me.peer(p)).wait_recv()
-    load_out = pltpu.make_async_copy(outb, rowsv, lsem.at[0])
-    load_out.start()
-    load_out.wait()
-    gmoe[...] = hid[...]
-
-    @pl.loop(0, 4)
-    def _(plane):
-        fill_hits(ranks, plane, hits, cap)
-        r = pl.ds(pl.multiple_of(plane * block, block), block)
-        gmoe[...] += mm_tn(hits[...], rowsv[r, :])
+    for step in (2, 3):
+        for k in range(4):
+            p = me.plane(step) * 4 + k
+            o_copy(p).wait_send()
+            remote(part(outs, p), part(outb, p), osem.at[0, p], osem.at[1, p], me.peer(p)).wait_recv()
+        add_outputs(outb, step)
 
     block_out[...] = gmoe[...].astype(BF)
 
@@ -1299,41 +1364,45 @@
     dsh = jnp.concatenate([w_qkv, w_proj, small], axis=1)
     wide = dsh.shape[1]
 
-    qkv, att, hid, lse, gate_t, ranks, aux, dense, xsend, gsend, cotr, wfull = pl.pallas_call(
+    qkv, att, hid, lse, gate_t, ranks, aux, dense, xsend, gsend, cotr, wfull, wfull2, xfar = pl.pallas_call(
         functools.partial(kernel_a, cap),
         out_shape=(
             shape((rows, 3 * D), BF), shape((rows, D), BF), shape((rows, D), F32), shape((rows, 128), F32),
             shape((16, rows), F32), shape((16, rows), jnp.int32), shape((32, D), F32), shape((D, wide), BF),
             shape((slots, D), BF), shape((16, 8, 256), F32), shape((slots, D), BF), shape((4, D, D), BF),
+            shape((4, D, D), BF), shape((4 * cap, D), BF),
         ),
-        in_specs=[vmem] * 4 + [hbm],
-        out_specs=(vmem,) * 10 + (hbm,) * 2,
+        in_specs=[vmem] * 4 + [hbm] * 2,
+        out_specs=(hbm,) * 3 + (vmem,) * 4 + (hbm,) * 2 + (vmem,) + (hbm,) * 4,
         scratch_shapes=[
+            pltpu.VMEM((rows, 3 * D), BF), pltpu.VMEM((rows, D), BF), pltpu.VMEM((rows, D), F32),
+            pltpu.VMEM((D, wide), BF), pltpu.VMEM((slots, D), BF), dma(5),
             pltpu.VMEM((slots, D), BF), pltpu.VMEM((rows, D), BF), pltpu.VMEM((4 * cap, rows), BF),
-            pltpu.VMEM((rows, rows), BF), dma(2, 4), dma(2, 4), dma(2, 16), dma(2), dma(), dma(2), dma(2, 2), dma(),
+            pltpu.VMEM((rows, rows), BF), dma(2, 4), dma(2, 4), dma(2, 16), dma(2), dma(), dma(2), dma(2, 2),
+            dma(2), dma(), dma(2), dma(2, 2), dma(), dma(2, 4),
         ],
         compiler_params=params(1),
         name="forward",
-    )(tok, cot, rt, dsh, w_in)
-
-    outs, ginh, ginb, ggb, gw = pl.pallas_call(
+    )(tok, cot, rt, dsh, w_in, w_out)
+
+    outs, ginh, ginb, ggb, gw, outn = pl.pallas_call(
         functools.partial(kernel_e, cap),
         out_shape=(
             shape((slots, D), BF), shape((slots, D), BF), shape((slots, D), BF), shape((16, 8, 256), F32),
-            shape((2, 4, D, D), BF),
+            shape((2, 4, D, D), BF), shape((slots, D), BF),
         ),
-        in_specs=[hbm, vmem, hbm, hbm, hbm],
-        out_specs=(hbm, hbm, hbm, vmem, hbm),
+        in_specs=[hbm, vmem, hbm, hbm, hbm, hbm],
+        out_specs=(hbm, hbm, hbm, vmem, hbm, hbm),
         scratch_shapes=[
             pltpu.VMEM((4, D, D), BF), pltpu.VMEM((FF, D), BF), pltpu.VMEM((slots, D), BF), pltpu.VMEM((slots, D), BF),
             pltpu.VMEM((16, 8, 256), F32), pltpu.VMEM((slots, FF), BF), pltpu.VMEM((slots, FF), BF),
             pltpu.VMEM((4 * cap, D), F32), pltpu.VMEM((2, 4 * cap, D), BF),
             pltpu.VMEM((16, 8, 256), F32), pltpu.VMEM((4 * cap, 128), F32),
-            dma(2, 16), dma(2, 16), dma(2, 16), dma(2, 16), dma(5), dma(5), dma(2), dma(2), dma(2), dma(), dma(2, 2),
+            dma(2, 16), dma(2, 16), dma(2, 16), dma(2, 16), dma(6), dma(6), dma(2), dma(2, 16),
         ],
         compiler_params=params(2),
         name="experts",
-    )(xsend, gsend, cotr, wfull, w_out)
+    )(xsend, gsend, cotr, wfull, wfull2, xfar)
 
     block_out, gtok, ghat, extra, outb, eg = pl.pallas_call(
         functools.partial(kernel_b, cap),
@@ -1341,10 +1410,11 @@
             shape((rows, D), BF), shape((rows, D), F32), shape((4, 2, quarter, D // 2), BF), shape((32, D), F32),
             shape((slots, D), BF), shape((2, 2, D, D), BF),
         ),
-        in_specs=[vmem] * 11 + [hbm] * 3,
+        in_specs=[vmem] * 7 + [hbm] * 8,
         out_specs=(vmem,) * 4 + (hbm,) * 2,
         scratch_shapes=[
-            pltpu.VMEM((slots, D), BF), pltpu.VMEM((4 * cap, rows), BF), pltpu.VMEM((rows, D), F32),
+            pltpu.VMEM((D, wide), BF), pltpu.VMEM((rows, 3 * D), BF), pltpu.VMEM((rows, D), BF),
+            pltpu.VMEM((rows, D), F32), dma(4), pltpu.VMEM((slots, D), BF), pltpu.VMEM((4 * cap, rows), BF), pltpu.VMEM((rows, D), F32),
             pltpu.VMEM((rows, D), BF), pltpu.VMEM((rows, D), BF), pltpu.VMEM((rows, D), BF),
             pltpu.VMEM((rows, 3 * D), BF), pltpu.VMEM((4, 4, 2, quarter, D // 2), BF),
             pltpu.VMEM((4, 4, quarter, D // 2), BF), pltpu.VMEM((4, 4, quarter, D // 2), BF),
@@ -1356,7 +1426,7 @@
         ],
         compiler_params=params(3),
         name="backward",
-    )(tok, cot, dense, aux, qkv, att, hid, lse, gate_t, ranks, ggb, ginb, outs, gw)
+    )(tok, cot, aux, lse, gate_t, ranks, ggb, dense, qkv, att, hid, ginb, outs, gw, outn)
 
     def unpadded(array):
         return array.reshape(images, SEQ_PAD, D)[:, :SEQ].reshape(count, D)

time: 607 us -> 567 us (0.934)
  Pallas kernels: 568 us -> 527 us
    pallas_call x1, Pallas kernels: 220 us -> 170 us  [fast(): pl.pallas_call(functools.partial(kernel_b, cap), out_shape=(shape((rows,...]
    pallas_call x1, Pallas kernels: 125 us -> 160 us  [fast(): pl.pallas_call(functools.partial(kernel_a, cap), out_shape=(shape((rows,...]
    pallas_call x1, Pallas kernels: 194 us -> 164 us  [fast(): pl.pallas_call(functools.partial(kernel_e, cap), out_shape=(shape((slots,...]
where the time goes in v3:
time: 567 us; the launch traced here: 560 us
  Pallas kernels  527 us (93%)
  local copies, waits for them, and re-layouts  25.6 us (5%)
  other arithmetic  6.22 us (1%)
    pallas_call x1, Pallas kernels, fast(): pl.pallas_call(functools.partial(kernel_b, cap), out_shape=(shape((rows,...  170 us
    pallas_call x1, Pallas kernels, fast(): pl.pallas_call(functools.partial(kernel_e, cap), out_shape=(shape((slots,...  164 us
    pallas_call x1, Pallas kernels, fast(): pl.pallas_call(functools.partial(kernel_a, cap), out_shape=(shape((rows,...  160 us
    pallas_call x1, Pallas kernels, fast(): pl.pallas_call(kernel_s, out_shape=(shape((32, quarter), F32), shape((2,...  16.5 us
    pallas_call x1, Pallas kernels, fast(): pl.pallas_call(kernel_u, out_shape=(shape((2, D, D), F32), shape((2, D, D...  15.2 us

profile of v3, /device:TPU:0, one launch (start us, length us, event | category | flops | bytes accessed | tf_op | source)
XLA Modules:
  0.0 559.8 jit_solution(3725740818028715385)
XLA Ops:
  0.7 0.8 broadcast_in_dim.12
  1.4 0.7 broadcast_in_dim.13
  2.1 0.7 pad_maximum_fusion.1
  2.9 2.4 fusion.1.dsh
  5.7 1.2 pad.15
  6.8 0.6 copy-done.1
  7.8 1.2 pad.16
  9.0 0.7 reshape.101
  9.7 160.3 %forward.1 = (bf16[896,2304]{1,0:T(8,128)(2,1)}, bf16[896,768]{1,0:T(8,128)(2,1)}, f32[896,768]{1,0:T(8,128)}, f32[896,128]{1,0:T(8,128)}, f32[16,896]{1,0:T(8,1...) custom-call(bf16[896,768]{1,0:T(8,128)(2,1)} %bitcast.28, ...), custom_call_target="tpu_custom_call" | custom-call | tf_op jit(solution)/shard_map/forward/pallas_call | solution.py:1367
  170.0 164.4 %experts.1 = (bf16[2560,768]{1,0:T(8,128)(2,1)}, bf16[2560,768]{1,0:T(8,128)(2,1)}, bf16[2560,768]{1,0:T(8,128)(2,1)}, f32[16,8,256]{2,1,0:T(8,128)}, bf16[2,4,7...) custom-call(bf16[2560,768]{1,0:T(8,128)(2,1)} %get-tuple-element.81.xsend, f32[16,8,256]{2,1,0:T(8,128)} %get-tuple-element.82.gsend, ...), custom_call_target="tpu_custom_call" | custom-call | tf_op jit(solution)/shard_map/experts/pallas_call | solution.py:1388
  334.5 170.3 %backward.1 = (bf16[896,768]{1,0:T(8,128)(2,1)}, f32[896,768]{1,0:T(8,128)}, bf16[4,2,192,384]{3,2,1,0:T(8,128)(2,1)}, f32[32,768]{1,0:T(8,128)}, bf16[2560,768]...) custom-call(bf16[896,768]{1,0:T(8,128)(2,1)} %bitcast.29, bf16[896,768]{1,0:T(8,128)(2,1)} %bitcast.31, ...), custom_call_target="tpu_custom_call" | custom-call | tf_op jit(solution)/shard_map/backward/pallas_call | solution.py:1407
  504.8 0.6 pad_maximum_fusion.moments
  506.1 0.8 copy.65.rows3
  507.4 16.5 %update_sums.1 = (f32[32,192]{1,0:T(8,128)}, f32[2,192]{1,0:T(2,128)}, f32[192,2]{1,0:T(8,128)}, f32[1,192]{1,0:T(1,128)}, f32[8,768]{1,0:T(8,128)}, /*index=5*/f32[24,768]{1,0:T(8,128)}, f32[16,128]{1,0:T(8,128)}) custom-call(bf16[2,2,768,768]{3,2,1,0:T(8,128)(2,1)} %get-tuple-element.98.eg, bf16[4,2,192,384]{3,2,1,0:T(8,128)(2,1)} %get-tuple-element.99.ghat, ...), custom_call_target="tpu_custom_call" | custom-call | tf_op jit(solution)/shard_map/update_sums/pallas_call | solution.py:1436
  524.0 0.6 reshape.106.cols
  524.6 0.7 copy.66.col_router
  525.3 15.2 %update.1 = (f32[2,768,768]{2,1,0:T(8,128)}, f32[2,768,768]{2,1,0:T(8,128)}, f32[2,768,768]{2,1,0:T(8,128)}, f32[2,768,768]{2,1,0:T(8,128)}, f32[1,128]{1,0:T(1,...) custom-call(bf16[2,2,768,768]{3,2,1,0:T(8,128)(2,1)} %get-tuple-elem, ...), custom_call_target="tpu_custom_call" | custom-call | tf_op jit(solution)/shard_map/update/pallas_call | solution.py:1458
  540.5 1.6 copy.68
  542.1 1.3 reshape.107
  544.0 1.3 slice_reduce_fusion.2
  545.3 0.7 slice_reduce_fusion.3
  546.1 0.7 copy.67
  546.7 1.3 fusion.5
  548.1 1.3 reduce.4
  549.4 1.2 slice_bitcast_fusion.1
  550.5 0.6 slice_bitcast_fusion
  551.2 0.6 fusion.3
  551.8 0.8 slice_reduce_fusion
  552.5 1.9 slice.69
  554.4 1.7 reshape.105
  556.1 1.4 slice.68
  557.5 1.3 reshape.103
  (55 shorter events, 3.4 us)
Async XLA Ops:
  0.7 4.7 copy-start
  5.6 1.8 copy-start.1
  7.4 1.5 copy-start.7
  334.4 170.4 %copy-start.8 = (f32[2,768]{1,0:T(2,128)S(1)}, f32[2,768]{1,0:T(2,128)}, u32[]{:S(2)}) copy-start(f32[2,768]{1,0:T(2,128)} %param.43) | copy-start | bytes 18436
  334.4 170.4 %copy-start.9 = (f32[2,768]{1,0:T(2,128)S(1)}, f32[2,768]{1,0:T(2,128)}, u32[]{:S(2)}) copy-start(f32[2,768]{1,0:T(2,128)} %param.42) | copy-start | bytes 18436
  334.4 170.4 %copy-start.10 = (f32[2,768]{1,0:T(2,128)S(1)}, f32[2,768]{1,0:T(2,128)}, u32[]{:S(2)}) copy-start(f32[2,768]{1,0:T(2,128)} %param.41) | copy-start | bytes 18436
  334.4 170.4 %copy-start.11 = (f32[2,768]{1,0:T(2,128)S(1)}, f32[2,768]{1,0:T(2,128)}, u32[]{:S(2)}) copy-start(f32[2,768]{1,0:T(2,128)} %param.40) | copy-start | bytes 18436
  334.4 171.0 %copy-start.19 = (bf16[192]{0:T(256)(128)(2,1)S(1)}, bf16[192]{0:T(256)(128)(2,1)}, u32[]{:S(2)}) copy-start(bf16[192]{0:T(256)(128)(2,1)} %param.25) | copy-start | bytes 1156
  334.4 171.0 %copy-start.20 = (bf16[192]{0:T(256)(128)(2,1)S(1)}, bf16[192]{0:T(256)(128)(2,1)}, u32[]{:S(2)}) copy-start(bf16[192]{0:T(256)(128)(2,1)} %param.28) | copy-start | bytes 1156
  334.5 171.6 %copy-start.14 = (f32[192]{0:T(256)S(1)}, f32[192]{0:T(256)}, u32[]{:S(2)}) copy-start(f32[192]{0:T(256)} %param.36) | copy-start | bytes 2308
  334.5 171.6 %copy-start.15 = (f32[192]{0:T(256)S(1)}, f32[192]{0:T(256)}, u32[]{:S(2)}) copy-start(f32[192]{0:T(256)} %param.34) | copy-start | bytes 2308
  334.5 172.4 %copy-start.16 = (f32[192]{0:T(256)S(1)}, f32[192]{0:T(256)}, u32[]{:S(2)}) copy-start(f32[192]{0:T(256)} %param.33) | copy-start | bytes 2308
  334.5 172.4 %copy-start.17 = (f32[192]{0:T(256)S(1)}, f32[192]{0:T(256)}, u32[]{:S(2)}) copy-start(f32[192]{0:T(256)} %param.32) | copy-start | bytes 2308
  507.4 16.5 %copy-start.5 = (f32[2304]{0:T(1024)S(1)}, f32[2304]{0:T(1024)}, u32[]{:S(2)}) copy-start(f32[2304]{0:T(1024)} %param.35) | copy-start | bytes 27652
  507.4 16.5 %copy-start.12 = (f32[768]{0:T(1024)S(1)}, f32[768]{0:T(1024)}, u32[]{:S(2)}) copy-start(f32[768]{0:T(1024)} %param.37) | copy-start | bytes 9220
  507.4 17.2 %copy-start.18 = (f32[16]{0:T(128)S(1)}, f32[16]{0:T(128)}, u32[]{:S(2)}) copy-start(f32[16]{0:T(128)} %param.39) | copy-start | bytes 196
  525.3 18.1 %copy-start.3 = (f32[32,192]{1,0:T(8,128)S(1)}, f32[32,192]{1,0:T(8,128)}, u32[]{:S(2)}) copy-start(f32[32,192]{1,0:T(8,128)} %get-tuple-element.101.mine) | copy-start | bytes 73732
  525.3 18.1 %copy-start.6 = (f32[2,192]{1,0:T(2,128)S(1)}, f32[2,192]{1,0:T(2,128)}, u32[]{:S(2)}) copy-start(f32[2,192]{1,0:T(2,128)} %get-tuple-element.105.v) | copy-start | bytes 4612
  525.3 25.9 %copy-start.4 = (f32[8,768]{1,0:T(8,128)S(1)}, f32[8,768]{1,0:T(8,128)}, u32[]{:S(2)}) copy-start(f32[8,768]{1,0:T(8,128)} %get-tuple-element.102.moments_mid) | copy-start | bytes 73732
  525.3 26.5 %copy-start.2 = (f32[192,2]{1,0:T(8,128)S(1)}, f32[192,2]{1,0:T(8,128)}, u32[]{:S(2)}) copy-start(f32[192,2]{1,0:T(8,128)} %get-tuple-element.103.rows3) | copy-start | bytes 4612
  556.1 2.7 copy-start.13

commit v4 on v3

--- a/solution.py
+++ b/solution.py
@@ -659,6 +659,20 @@
                 slope = half + (0.5 * pre) * (1.0 - t * t) * (GELU_A + 3.0 * GELU_A * GELU_B * square)
                 gpre[r, cols] = slope.astype(BF)
 
+    def give_back(plane):
+        for k in range(4):
+            p = plane * 4 + k
+
+            @pl.when(p != me.number)
+            def _():
+                r_copy(p).start()
+                gg_copy(p).start()
+
+            @pl.when(p == me.number)
+            def _():
+                own_r.start()
+                own_g.start()
+
     @pl.loop(0, 4)
     def _(turn):
         step = (turn + 3) % 4
@@ -698,18 +712,7 @@
         stage[1] = acc[...].astype(BF)
         stage_out(plane, 1).start()
         stage_out(plane, 1).wait()
-        for k in range(4):
-            p = plane * 4 + k
-
-            @pl.when(p != me.number)
-            def _():
-                r_copy(p).start()
-                gg_copy(p).start()
-
-            @pl.when(p == me.number)
-            def _():
-                own_r.start()
-                own_g.start()
+        give_back(plane)
 
         stage_out(plane, 0).wait()
 
@@ -983,8 +986,7 @@
         def _():
             owner_local.start()
 
-    for d in (1, 2, 3, 0):
-        to_owner((s + d) % 4)
+    to_owner((s + 1) % 4)
     to_b(3)
     for g in range(3):
         attention_backward(qkv, gatt, lse, gqkv, images, g)
@@ -996,9 +998,13 @@
         ]
         if g == 0:
             gmoe[...] = (partial[0] + partial[1]) + partial[2]
+            to_owner((s + 2) % 4)
         else:
             gmoe[...] += (partial[0] + partial[1]) + partial[2]
             to_b(g - 1)
+            if g == 1:
+                to_owner((s + 3) % 4)
+                to_owner(s)
 
     @pl.loop(0, images)
     def _(i):

time: 567 us -> 569 us (level)
  no operation moved by 1% of the time
where the time goes in v4:
time: 569 us; the launch traced here: 562 us
  Pallas kernels  528 us (93%)
  local copies, waits for them, and re-layouts  25.6 us (4%)
  other arithmetic  6.22 us (1%)
    pallas_call x1, Pallas kernels, fast(): pl.pallas_call(functools.partial(kernel_b, cap), out_shape=(shape((rows,...  170 us
    pallas_call x1, Pallas kernels, fast(): pl.pallas_call(functools.partial(kernel_e, cap), out_shape=(shape((slots,...  164 us
    pallas_call x1, Pallas kernels, fast(): pl.pallas_call(functools.partial(kernel_a, cap), out_shape=(shape((rows,...  160 us
    pallas_call x1, Pallas kernels, fast(): pl.pallas_call(kernel_s, out_shape=(shape((32, quarter), F32), shape((2,...  18.2 us
    pallas_call x1, Pallas kernels, fast(): pl.pallas_call(kernel_u, out_shape=(shape((2, D, D), F32), shape((2, D, D...  15.2 us

profile of v4, /device:TPU:0, one launch (start us, length us, event | category | flops | bytes accessed | tf_op | source)
XLA Modules:
  0.0 561.6 jit_solution(9658814625964960950)
XLA Ops:
  0.7 0.8 broadcast_in_dim.12
  1.4 0.7 broadcast_in_dim.13
  2.1 0.7 pad_maximum_fusion.1
  2.9 2.4 fusion.1.dsh
  5.7 1.2 pad.15
  6.8 0.6 copy-done.1
  7.8 1.2 pad.16
  9.0 0.7 reshape.101
  9.7 160.3 %forward.1 = (bf16[896,2304]{1,0:T(8,128)(2,1)}, bf16[896,768]{1,0:T(8,128)(2,1)}, f32[896,768]{1,0:T(8,128)}, f32[896,128]{1,0:T(8,128)}, f32[16,896]{1,0:T(8,1...) custom-call(bf16[896,768]{1,0:T(8,128)(2,1)} %bitcast.28, ...), custom_call_target="tpu_custom_call" | custom-call | tf_op jit(solution)/shard_map/forward/pallas_call | solution.py:1373
  170.0 164.4 %experts.1 = (bf16[2560,768]{1,0:T(8,128)(2,1)}, bf16[2560,768]{1,0:T(8,128)(2,1)}, bf16[2560,768]{1,0:T(8,128)(2,1)}, f32[16,8,256]{2,1,0:T(8,128)}, bf16[2,4,7...) custom-call(bf16[2560,768]{1,0:T(8,128)(2,1)} %get-tuple-element.81.xsend, f32[16,8,256]{2,1,0:T(8,128)} %get-tuple-element.82.gsend, ...), custom_call_target="tpu_custom_call" | custom-call | tf_op jit(solution)/shard_map/experts/pallas_call | solution.py:1394
  334.5 170.3 %backward.1 = (bf16[896,768]{1,0:T(8,128)(2,1)}, f32[896,768]{1,0:T(8,128)}, bf16[4,2,192,384]{3,2,1,0:T(8,128)(2,1)}, f32[32,768]{1,0:T(8,128)}, bf16[2560,768]...) custom-call(bf16[896,768]{1,0:T(8,128)(2,1)} %bitcast.29, bf16[896,768]{1,0:T(8,128)(2,1)} %bitcast.31, ...), custom_call_target="tpu_custom_call" | custom-call | tf_op jit(solution)/shard_map/backward/pallas_call | solution.py:1413
  504.9 0.6 pad_maximum_fusion.moments
  506.1 0.8 copy.65.rows3
  507.5 18.2 %update_sums.1 = (f32[32,192]{1,0:T(8,128)}, f32[2,192]{1,0:T(2,128)}, f32[192,2]{1,0:T(8,128)}, f32[1,192]{1,0:T(1,128)}, f32[8,768]{1,0:T(8,128)}, /*index=5*/f32[24,768]{1,0:T(8,128)}, f32[16,128]{1,0:T(8,128)}) custom-call(bf16[2,2,768,768]{3,2,1,0:T(8,128)(2,1)} %get-tuple-element.98.eg, bf16[4,2,192,384]{3,2,1,0:T(8,128)(2,1)} %get-tuple-element.99.ghat, ...), custom_call_target="tpu_custom_call" | custom-call | tf_op jit(solution)/shard_map/update_sums/pallas_call | solution.py:1442
  525.7 0.6 reshape.106.cols
  526.4 0.7 copy.66.col_router
  527.1 15.2 %update.1 = (f32[2,768,768]{2,1,0:T(8,128)}, f32[2,768,768]{2,1,0:T(8,128)}, f32[2,768,768]{2,1,0:T(8,128)}, f32[2,768,768]{2,1,0:T(8,128)}, f32[1,128]{1,0:T(1,...) custom-call(bf16[2,2,768,768]{3,2,1,0:T(8,128)(2,1)} %get-tuple-elem, ...), custom_call_target="tpu_custom_call" | custom-call | tf_op jit(solution)/shard_map/update/pallas_call | solution.py:1464
  542.3 1.6 copy.68
  543.9 1.3 reshape.107
  545.8 1.3 slice_reduce_fusion.2
  547.1 0.7 slice_reduce_fusion.3
  547.8 0.7 copy.67
  548.5 1.3 fusion.5
  549.8 1.3 reduce.4
  551.1 1.2 slice_bitcast_fusion.1
  552.3 0.6 slice_bitcast_fusion
  552.9 0.6 fusion.3
  553.5 0.8 slice_reduce_fusion
  554.3 1.9 slice.69
  556.1 1.7 reshape.105
  557.9 1.4 slice.68
  559.2 1.3 reshape.103
  (55 shorter events, 3.4 us)
Async XLA Ops:
  0.7 4.7 copy-start
  5.6 1.8 copy-start.1
  7.4 1.5 copy-start.7
  334.4 170.4 %copy-start.8 = (f32[2,768]{1,0:T(2,128)S(1)}, f32[2,768]{1,0:T(2,128)}, u32[]{:S(2)}) copy-start(f32[2,768]{1,0:T(2,128)} %param.43) | copy-start | bytes 18436
  334.4 170.4 %copy-start.9 = (f32[2,768]{1,0:T(2,128)S(1)}, f32[2,768]{1,0:T(2,128)}, u32[]{:S(2)}) copy-start(f32[2,768]{1,0:T(2,128)} %param.42) | copy-start | bytes 18436
  334.4 170.4 %copy-start.10 = (f32[2,768]{1,0:T(2,128)S(1)}, f32[2,768]{1,0:T(2,128)}, u32[]{:S(2)}) copy-start(f32[2,768]{1,0:T(2,128)} %param.41) | copy-start | bytes 18436
  334.4 170.4 %copy-start.11 = (f32[2,768]{1,0:T(2,128)S(1)}, f32[2,768]{1,0:T(2,128)}, u32[]{:S(2)}) copy-start(f32[2,768]{1,0:T(2,128)} %param.40) | copy-start | bytes 18436
  334.4 171.1 %copy-start.19 = (bf16[192]{0:T(256)(128)(2,1)S(1)}, bf16[192]{0:T(256)(128)(2,1)}, u32[]{:S(2)}) copy-start(bf16[192]{0:T(256)(128)(2,1)} %param.25) | copy-start | bytes 1156
  334.4 171.1 %copy-start.20 = (bf16[192]{0:T(256)(128)(2,1)S(1)}, bf16[192]{0:T(256)(128)(2,1)}, u32[]{:S(2)}) copy-start(bf16[192]{0:T(256)(128)(2,1)} %param.28) | copy-start | bytes 1156
  334.5 171.6 %copy-start.14 = (f32[192]{0:T(256)S(1)}, f32[192]{0:T(256)}, u32[]{:S(2)}) copy-start(f32[192]{0:T(256)} %param.36) | copy-start | bytes 2308
  334.5 171.6 %copy-start.15 = (f32[192]{0:T(256)S(1)}, f32[192]{0:T(256)}, u32[]{:S(2)}) copy-start(f32[192]{0:T(256)} %param.34) | copy-start | bytes 2308
  334.5 172.4 %copy-start.16 = (f32[192]{0:T(256)S(1)}, f32[192]{0:T(256)}, u32[]{:S(2)}) copy-start(f32[192]{0:T(256)} %param.33) | copy-start | bytes 2308
  334.5 172.4 %copy-start.17 = (f32[192]{0:T(256)S(1)}, f32[192]{0:T(256)}, u32[]{:S(2)}) copy-start(f32[192]{0:T(256)} %param.32) | copy-start | bytes 2308
  507.5 18.2 %copy-start.5 = (f32[2304]{0:T(1024)S(1)}, f32[2304]{0:T(1024)}, u32[]{:S(2)}) copy-start(f32[2304]{0:T(1024)} %param.35) | copy-start | bytes 27652
  507.5 18.3 %copy-start.12 = (f32[768]{0:T(1024)S(1)}, f32[768]{0:T(1024)}, u32[]{:S(2)}) copy-start(f32[768]{0:T(1024)} %param.37) | copy-start | bytes 9220
  507.5 18.9 %copy-start.18 = (f32[16]{0:T(128)S(1)}, f32[16]{0:T(128)}, u32[]{:S(2)}) copy-start(f32[16]{0:T(128)} %param.39) | copy-start | bytes 196
  527.0 18.1 %copy-start.3 = (f32[32,192]{1,0:T(8,128)S(1)}, f32[32,192]{1,0:T(8,128)}, u32[]{:S(2)}) copy-start(f32[32,192]{1,0:T(8,128)} %get-tuple-element.101.mine) | copy-start | bytes 73732
  527.0 18.1 %copy-start.6 = (f32[2,192]{1,0:T(2,128)S(1)}, f32[2,192]{1,0:T(2,128)}, u32[]{:S(2)}) copy-start(f32[2,192]{1,0:T(2,128)} %get-tuple-element.105.v) | copy-start | bytes 4612
  527.0 25.9 %copy-start.4 = (f32[8,768]{1,0:T(8,128)S(1)}, f32[8,768]{1,0:T(8,128)}, u32[]{:S(2)}) copy-start(f32[8,768]{1,0:T(8,128)} %get-tuple-element.102.moments_mid) | copy-start | bytes 73732
  527.0 26.5 %copy-start.2 = (f32[192,2]{1,0:T(8,128)S(1)}, f32[192,2]{1,0:T(8,128)}, u32[]{:S(2)}) copy-start(f32[192,2]{1,0:T(8,128)} %get-tuple-element.103.rows3) | copy-start | bytes 4612
  557.9 2.7 copy-start.13

commit v5 on v3

--- a/solution.py
+++ b/solution.py
@@ -606,18 +606,18 @@
     w_copies = [
         pltpu.make_async_copy(wfull, w1v, wlsem.at[0]), pltpu.make_async_copy(xfar, xr.at[far_rows], wlsem.at[5])
     ] + [pltpu.make_async_copy(wfull2.at[f], w2v.at[pl.ds(f * D, D)], wlsem.at[1 + f]) for f in range(4)]
+    for step in (2, 1, 0):
+        for k in range(4):
+            p = me.plane(step) * 4 + k
+
+            @pl.when(p != me.number)
+            def _():
+                x_copy(p).start()
+
     for d in range(1, 16):
         g_copy((me.number + d) % 16).start()
     for cp in local_copies + w_copies:
         cp.start()
-    for step in (2, 1, 0):
-        for k in range(4):
-            p = me.plane(step) * 4 + k
-
-            @pl.when(p != me.number)
-            def _():
-                x_copy(p).start()
-
     ggs[...] = jnp.zeros_like(ggs)
     for cp in local_copies + w_copies:
         cp.wait()

time: 567 us -> 589 us (1.039)
  Pallas kernels: 527 us -> 549 us
    pallas_call x1, Pallas kernels: 164 us -> 186 us  [fast(): pl.pallas_call(functools.partial(kernel_e, cap), out_shape=(shape((slots,...]
where the time goes in v5:
time: 589 us; the launch traced here: 582 us
  Pallas kernels  549 us (93%)
  local copies, waits for them, and re-layouts  25.6 us (4%)
  other arithmetic  6.22 us (1%)
    pallas_call x1, Pallas kernels, fast(): pl.pallas_call(functools.partial(kernel_e, cap), out_shape=(shape((slots,...  186 us
    pallas_call x1, Pallas kernels, fast(): pl.pallas_call(functools.partial(kernel_b, cap), out_shape=(shape((rows,...  173 us
    pallas_call x1, Pallas kernels, fast(): pl.pallas_call(functools.partial(kernel_a, cap), out_shape=(shape((rows,...  160 us
    pallas_call x1, Pallas kernels, fast(): pl.pallas_call(kernel_u, out_shape=(shape((2, D, D), F32), shape((2, D, D...  15.2 us
    pallas_call x1, Pallas kernels, fast(): pl.pallas_call(kernel_s, out_shape=(shape((32, quarter), F32), shape((2,...  13.7 us

profile of v5, /device:TPU:0, one launch (start us, length us, event | category | flops | bytes accessed | tf_op | source)
XLA Modules:
  0.0 582.1 jit_solution(4583286515361324266)
XLA Ops:
  0.7 0.8 broadcast_in_dim.12
  1.4 0.7 broadcast_in_dim.13
  2.1 0.7 pad_maximum_fusion.1
  2.9 2.4 fusion.1.dsh
  5.7 1.2 pad.15
  6.8 0.6 copy-done.1
  7.8 1.2 pad.16
  9.0 0.7 reshape.101
  9.7 160.3 %forward.1 = (bf16[896,2304]{1,0:T(8,128)(2,1)}, bf16[896,768]{1,0:T(8,128)(2,1)}, f32[896,768]{1,0:T(8,128)}, f32[896,128]{1,0:T(8,128)}, f32[16,896]{1,0:T(8,1...) custom-call(bf16[896,768]{1,0:T(8,128)(2,1)} %bitcast.28, ...), custom_call_target="tpu_custom_call" | custom-call | tf_op jit(solution)/shard_map/forward/pallas_call | solution.py:1367
  170.0 186.4 %experts.1 = (bf16[2560,768]{1,0:T(8,128)(2,1)}, bf16[2560,768]{1,0:T(8,128)(2,1)}, bf16[2560,768]{1,0:T(8,128)(2,1)}, f32[16,8,256]{2,1,0:T(8,128)}, bf16[2,4,7...) custom-call(bf16[2560,768]{1,0:T(8,128)(2,1)} %get-tuple-element.81.xsend, f32[16,8,256]{2,1,0:T(8,128)} %get-tuple-element.82.gsend, ...), custom_call_target="tpu_custom_call" | custom-call | tf_op jit(solution)/shard_map/experts/pallas_call | solution.py:1388
  356.5 173.3 %backward.1 = (bf16[896,768]{1,0:T(8,128)(2,1)}, f32[896,768]{1,0:T(8,128)}, bf16[4,2,192,384]{3,2,1,0:T(8,128)(2,1)}, f32[32,768]{1,0:T(8,128)}, bf16[2560,768]...) custom-call(bf16[896,768]{1,0:T(8,128)(2,1)} %bitcast.29, bf16[896,768]{1,0:T(8,128)(2,1)} %bitcast.31, ...), custom_call_target="tpu_custom_call" | custom-call | tf_op jit(solution)/shard_map/backward/pallas_call | solution.py:1407
  529.9 0.6 pad_maximum_fusion.moments
  531.1 0.8 copy.65.rows3
  532.5 13.7 %update_sums.1 = (f32[32,192]{1,0:T(8,128)}, f32[2,192]{1,0:T(2,128)}, f32[192,2]{1,0:T(8,128)}, f32[1,192]{1,0:T(1,128)}, f32[8,768]{1,0:T(8,128)}, /*index=5*/f32[24,768]{1,0:T(8,128)}, f32[16,128]{1,0:T(8,128)}) custom-call(bf16[2,2,768,768]{3,2,1,0:T(8,128)(2,1)} %get-tuple-element.98.eg, bf16[4,2,192,384]{3,2,1,0:T(8,128)(2,1)} %get-tuple-element.99.ghat, ...), custom_call_target="tpu_custom_call" | custom-call | tf_op jit(solution)/shard_map/update_sums/pallas_call | solution.py:1436
  546.3 0.6 reshape.106.cols
  546.9 0.7 copy.66.col_router
  547.6 15.2 %update.1 = (f32[2,768,768]{2,1,0:T(8,128)}, f32[2,768,768]{2,1,0:T(8,128)}, f32[2,768,768]{2,1,0:T(8,128)}, f32[2,768,768]{2,1,0:T(8,128)}, f32[1,128]{1,0:T(1,...) custom-call(bf16[2,2,768,768]{3,2,1,0:T(8,128)(2,1)} %get-tuple-elem, ...), custom_call_target="tpu_custom_call" | custom-call | tf_op jit(solution)/shard_map/update/pallas_call | solution.py:1458
  562.8 1.6 copy.68
  564.4 1.3 reshape.107
  566.3 1.3 slice_reduce_fusion.2
  567.6 0.7 slice_reduce_fusion.3
  568.4 0.7 copy.67
  569.0 1.3 fusion.5
  570.3 1.3 reduce.4
  571.7 1.2 slice_bitcast_fusion.1
  572.8 0.6 slice_bitcast_fusion
  573.4 0.6 fusion.3
  574.0 0.8 slice_reduce_fusion
  574.8 1.9 slice.69
  576.7 1.7 reshape.105
  578.4 1.4 slice.68
  579.8 1.3 reshape.103
  (55 shorter events, 3.4 us)
Async XLA Ops:
  0.7 4.7 copy-start
  5.6 1.8 copy-start.1
  7.4 1.5 copy-start.7
  356.4 173.4 %copy-start.8 = (f32[2,768]{1,0:T(2,128)S(1)}, f32[2,768]{1,0:T(2,128)}, u32[]{:S(2)}) copy-start(f32[2,768]{1,0:T(2,128)} %param.43) | copy-start | bytes 18436
  356.4 173.4 %copy-start.9 = (f32[2,768]{1,0:T(2,128)S(1)}, f32[2,768]{1,0:T(2,128)}, u32[]{:S(2)}) copy-start(f32[2,768]{1,0:T(2,128)} %param.42) | copy-start | bytes 18436
  356.4 173.4 %copy-start.10 = (f32[2,768]{1,0:T(2,128)S(1)}, f32[2,768]{1,0:T(2,128)}, u32[]{:S(2)}) copy-start(f32[2,768]{1,0:T(2,128)} %param.41) | copy-start | bytes 18436
  356.4 173.4 %copy-start.11 = (f32[2,768]{1,0:T(2,128)S(1)}, f32[2,768]{1,0:T(2,128)}, u32[]{:S(2)}) copy-start(f32[2,768]{1,0:T(2,128)} %param.40) | copy-start | bytes 18436
  356.5 174.0 %copy-start.19 = (bf16[192]{0:T(256)(128)(2,1)S(1)}, bf16[192]{0:T(256)(128)(2,1)}, u32[]{:S(2)}) copy-start(bf16[192]{0:T(256)(128)(2,1)} %param.25) | copy-start | bytes 1156
  356.5 174.0 %copy-start.20 = (bf16[192]{0:T(256)(128)(2,1)S(1)}, bf16[192]{0:T(256)(128)(2,1)}, u32[]{:S(2)}) copy-start(bf16[192]{0:T(256)(128)(2,1)} %param.28) | copy-start | bytes 1156
  356.5 174.6 %copy-start.14 = (f32[192]{0:T(256)S(1)}, f32[192]{0:T(256)}, u32[]{:S(2)}) copy-start(f32[192]{0:T(256)} %param.36) | copy-start | bytes 2308
  356.5 174.6 %copy-start.15 = (f32[192]{0:T(256)S(1)}, f32[192]{0:T(256)}, u32[]{:S(2)}) copy-start(f32[192]{0:T(256)} %param.34) | copy-start | bytes 2308
  356.5 175.4 %copy-start.16 = (f32[192]{0:T(256)S(1)}, f32[192]{0:T(256)}, u32[]{:S(2)}) copy-start(f32[192]{0:T(256)} %param.33) | copy-start | bytes 2308
  356.5 175.4 %copy-start.17 = (f32[192]{0:T(256)S(1)}, f32[192]{0:T(256)}, u32[]{:S(2)}) copy-start(f32[192]{0:T(256)} %param.32) | copy-start | bytes 2308
  532.5 13.8 %copy-start.5 = (f32[2304]{0:T(1024)S(1)}, f32[2304]{0:T(1024)}, u32[]{:S(2)}) copy-start(f32[2304]{0:T(1024)} %param.35) | copy-start | bytes 27652
  532.5 13.8 %copy-start.12 = (f32[768]{0:T(1024)S(1)}, f32[768]{0:T(1024)}, u32[]{:S(2)}) copy-start(f32[768]{0:T(1024)} %param.37) | copy-start | bytes 9220
  532.5 14.4 %copy-start.18 = (f32[16]{0:T(128)S(1)}, f32[16]{0:T(128)}, u32[]{:S(2)}) copy-start(f32[16]{0:T(128)} %param.39) | copy-start | bytes 196
  547.6 18.1 %copy-start.3 = (f32[32,192]{1,0:T(8,128)S(1)}, f32[32,192]{1,0:T(8,128)}, u32[]{:S(2)}) copy-start(f32[32,192]{1,0:T(8,128)} %get-tuple-element.101.mine) | copy-start | bytes 73732
  547.6 18.1 %copy-start.6 = (f32[2,192]{1,0:T(2,128)S(1)}, f32[2,192]{1,0:T(2,128)}, u32[]{:S(2)}) copy-start(f32[2,192]{1,0:T(2,128)} %get-tuple-element.105.v) | copy-start | bytes 4612
  547.6 25.9 %copy-start.4 = (f32[8,768]{1,0:T(8,128)S(1)}, f32[8,768]{1,0:T(8,128)}, u32[]{:S(2)}) copy-start(f32[8,768]{1,0:T(8,128)} %get-tuple-element.102.moments_mid) | copy-start | bytes 73732
  547.6 26.5 %copy-start.2 = (f32[192,2]{1,0:T(8,128)S(1)}, f32[192,2]{1,0:T(8,128)}, u32[]{:S(2)}) copy-start(f32[192,2]{1,0:T(8,128)} %get-tuple-element.103.rows3) | copy-start | bytes 4612
  578.4 2.7 copy-start.13
